TPU v7x, 32 devices: a whole 2x2x4 slice. The times are simulated.
32 devices in a mesh: sample: 4 (over x, core), chan: 8 (over z, y).
Axes of the slice: x: 2, y: 2, z: 4, core: 2. Of those that a mesh axis runs over, the one named last changes fastest.
Arguments:
- act_64: bfloat16 [4, 64, 8, 8, 256], P('sample'), may hold values from -6 to 6
- cot_32: bfloat16 [4, 32, 4, 4, 512], P('sample', None, None, None, 'chan'), may hold values from -2.5 to 2.5
- filters_32: bfloat16 [3, 3, 3, 256, 512], P(None, None, None, None, 'chan'), may hold values from -0.078125 to 0.078125
- act_128: bfloat16 [4, 128, 16, 16, 128], P('sample', 'chan'), may hold values from -6 to 6
Outputs:
- grad_filters_32: float32 [3, 3, 3, 256, 512], P(None, None, None, None, 'chan')
- grad_filters_64: float32 [3, 3, 3, 128, 256], P(None, None, None, 'chan')
- cot_64: float32 [4, 64, 8, 8, 256], P('sample', 'chan')
All inputs are finite; a program needn't handle non-finite values.
Results may differ from a plain program's by a relative error of at most 0.0029.
Values may be sent and summed in bfloat16 or wider, within the bound.
No kernel may reach another device: no remote copies, remote signals or barrier semaphores. Data moves between devices by JAX's collectives and lax.ppermute only.
A program may use at most 64 MiB of HBM per device.

v0:
```python
import functools

import jax
import jax.numpy as jnp
from jax import lax
from jax.experimental import pallas as pl
from jax.experimental.pallas import tpu as pltpu
from jax.sharding import PartitionSpec as P

leak_slope = 0.3
low = jnp.bfloat16
wide = jnp.float32
params = pltpu.CompilerParams(vmem_limit_bytes=40 * 2**20)
whole = pl.BlockSpec(memory_space=pltpu.VMEM)
scalar = pl.BlockSpec(memory_space=pltpu.SMEM)


def slot_plan():
    groups = []
    for col in range(3):
        groups.append([(1, 1, col), (1, 2, col), (2, 1, col), (2, 2, col)])
    for col in range(3):
        groups.append([(2, 0, col), (1, 0, col), (0, 1, col), (0, 2, col)])
    groups.append([None, (0, 0, 2), (0, 0, 1), (0, 0, 0)])
    return groups


def tap_index(tap):
    return (tap[0] * 3 + tap[1]) * 3 + tap[2]


def lane_slot(shape):
    return lax.broadcasted_iota(jnp.int32, shape, len(shape) - 1) // 32


def pack_kernel(core_ref, filters_ref, cot_ref, sent_ref):
    half = filters_ref.shape[1] // 2
    groups = slot_plan()
    rows = len(groups) * half
    start = pl.multiple_of(core_ref[0] * half, half)
    slots = lane_slot((half, 128))
    shards = sent_ref.shape[0]
    for g, group in enumerate(groups):
        for tile in range(shards // 4):
            turned = []
            for tap in group:
                if tap is None:
                    turned.append([jnp.zeros((half, 128), wide)] * 4)
                    continue
                block = filters_ref[tap_index(tap), pl.ds(start, half), pl.ds(tile * 128, 128)].astype(wide)
                turned.append([block] + [pltpu.roll(block, 32 * r, 1) for r in range(1, 4)])
            for m in range(4):
                joined = turned[0][(0 - m) % 4]
                for k in range(1, 4):
                    joined = jnp.where(slots == k, turned[k][(k - m) % 4], joined)
                sent_ref[tile * 4 + m, pl.ds(g * half, half), :] = joined.astype(low)
    turned_cot = cot_ref[...].astype(wide).T.astype(low)
    outs, cells = turned_cot.shape
    for d in range(shards):
        for b in range(cells // 128):
            sent_ref[d, pl.ds(rows + b * outs, outs), :] = turned_cot[:, b * 128 : (b + 1) * 128]


def pack(core, filters, cot, shards):
    outs = filters.shape[1]
    rows = len(slot_plan()) * (outs // 2) + cot.shape[0] // 128 * outs
    return pl.pallas_call(
        pack_kernel,
        out_shape=jax.ShapeDtypeStruct((shards, rows, 128), low),
        in_specs=[scalar, whole, whole],
        out_specs=whole,
        compiler_params=params,
        cost_estimate=pl.CostEstimate(flops=10**6, bytes_accessed=3 * 10**6, transcendentals=0),
    )(core, filters, cot)


def sign_kernel(position_ref, volume_ref, own_ref):
    part = position_ref[0] % 4
    rows = own_ref.shape[0]
    slots = lane_slot((rows, 128))
    joined = None
    for depth_par in range(2):
        for row_par in range(2):
            slot = depth_par * 2 + row_par
            block = volume_ref[:, depth_par, :, row_par].astype(wide).reshape(rows, 128)
            block = pltpu.roll(block, (slot - part + 4) % 4 * 32, 1)
            joined = block if joined is None else jnp.where(slots == slot, block, joined)
    own_ref[...] = joined.astype(low)


def own_signs(position, volume):
    planes, rows, columns, channels = volume.shape
    split = volume.reshape(planes // 2, 2, rows // 2, 2, columns, channels)
    count = planes * rows * columns // 4
    return pl.pallas_call(
        sign_kernel,
        out_shape=jax.ShapeDtypeStruct((count, 128), low),
        grid_spec=pltpu.PrefetchScalarGridSpec(
            num_scalar_prefetch=1,
            grid=(1,),
            in_specs=[
                pl.BlockSpec(
                    (planes // 2, 2, rows // 2, 2, columns, 128),
                    lambda i, at: (0, 0, 0, 0, 0, at[0] // 4),
                )
            ],
            out_specs=pl.BlockSpec((count, 128), lambda i, at: (0, 0)),
        ),
        compiler_params=params,
        cost_estimate=pl.CostEstimate(flops=10**6, bytes_accessed=4 * 10**6, transcendentals=0),
    )(position, split)


def spread_kernel(grid, core_ref, got_ref, other_ref, own_ref, sent_ref, weight, turned, products, joined):
    depth, height, width = grid
    cells = depth * height * width
    shards = got_ref.shape[0]
    groups = len(slot_plan())
    half = other_ref.shape[1] // groups
    outs = 2 * half
    core = core_ref[0]
    for c in range(shards):
        first = pl.multiple_of(c * outs + core * half, half)
        second = pl.multiple_of(c * outs + (1 - core) * half, half)
        for g in range(groups):
            weight[pl.ds(first, half), pl.ds(g * 128, 128)] = got_ref[c, pl.ds(g * half, half), :]
            weight[pl.ds(second, half), pl.ds(g * 128, 128)] = other_ref[c, pl.ds(g * half, half), :]
        for b in range(cells // 128):
            turned[pl.ds(c * outs, outs), pl.ds(b * 128, 128)] = got_ref[
                c, pl.ds(groups * half + b * outs, outs), :
            ]
    products[pl.ds(0, cells), :] = lax.dot_general(
        turned[...], weight[...], (((0,), (0,)), ((), ())), preferred_element_type=wide
    )
    products[pl.ds(cells, products.shape[0] - cells), :] = jnp.zeros(
        (products.shape[0] - cells, products.shape[1]), wide
    )
    chunk = cells // shards
    place = lax.broadcasted_iota(jnp.int32, (chunk, 128), 0)
    slots = lane_slot((chunk, 128))
    last_col = place % width == width - 1
    last_row = place // width % height == height - 1
    row_step, plane_step = width, width * height
    for n in range(shards):
        sums = [None, None]
        for col in range(3):
            shift = 1 if col == 0 else 0
            base = n * chunk + shift

            def piece(group, offset):
                return products[pl.ds(base + offset, chunk), pl.ds(group * 128, 128)]

            part = piece(col, 0)
            part = part + jnp.where(slots >= 2, piece(3 + col, plane_step), 0.0)
            by_row = piece(3 + col, row_step)
            moved = pltpu.roll(by_row, 96, 1)
            corner = piece(6, plane_step + row_step)
            if col > 0:
                corner = pltpu.roll(corner, 32 * col, 1)
            rows = jnp.where(slots == 1, by_row, jnp.where(slots == 3, moved + corner, 0.0))
            part = part + jnp.where(last_row, 0.0, rows)
            if shift:
                part = jnp.where(last_col, 0.0, part)
            to = 0 if col == 1 else 1
            sums[to] = part if sums[to] is None else sums[to] + part
        joined[pl.ds(0, chunk, stride=2), :] = sums[0]
        joined[pl.ds(1, chunk, stride=2), :] = sums[1]
        span = pl.ds(n * 2 * chunk, 2 * chunk)
        slope = jnp.where(own_ref[span, :].astype(wide) > 0, 1.0, leak_slope)
        sent_ref[n] = (joined[...] * slope).astype(low)


def spread(core, got, other, own, grid):
    cells = grid[0] * grid[1] * grid[2]
    shards = got.shape[0]
    groups = len(slot_plan())
    outs = 2 * other.shape[1] // groups
    return pl.pallas_call(
        functools.partial(spread_kernel, grid),
        out_shape=jax.ShapeDtypeStruct((shards, 2 * cells // shards, 128), low),
        in_specs=[scalar, whole, whole, whole],
        out_specs=whole,
        scratch_shapes=[
            pltpu.VMEM((shards * outs, groups * 128), low),
            pltpu.VMEM((shards * outs, cells), low),
            pltpu.VMEM((cells + 32, groups * 128), wide),
            pltpu.VMEM((2 * cells // shards, 128), wide),
        ],
        compiler_params=params,
        cost_estimate=pl.CostEstimate(flops=5 * 10**8, bytes_accessed=3 * 10**6, transcendentals=0),
    )(core, got, other, own)


def unpack_kernel(got_ref, wide_ref, low_ref):
    shards, rows, _ = got_ref.shape
    planes, height, columns, _ = wide_ref.shape
    slots = lane_slot((rows, 128))
    for tile in range(shards // 4):
        turned = []
        for m in range(4):
            block = got_ref[tile * 4 + m].astype(wide)
            turned.append([block] + [pltpu.roll(block, 32 * r, 1) for r in range(1, 4)])
        for slot in range(4):
            joined = turned[0][(0 - slot) % 4]
            for m in range(1, 4):
                joined = jnp.where(slots == m, turned[m][(m - slot) % 4], joined)
            joined = joined.reshape(planes // 2, height // 2, columns, 128)
            lanes = pl.ds(tile * 128, 128)
            for z in range(planes // 2):
                for y in range(height // 2):
                    at = (2 * z + slot // 2, 2 * y + slot % 2)
                    wide_ref[at[0], at[1], :, lanes] = joined[z, y]
    low_ref[...] = wide_ref[...].astype(low)


def unpack(got, grid):
    shape = (*grid, got.shape[0] * 32)
    return pl.pallas_call(
        unpack_kernel,
        out_shape=(jax.ShapeDtypeStruct(shape, wide), jax.ShapeDtypeStruct(shape, low)),
        in_specs=[whole],
        out_specs=(whole, whole),
        compiler_params=params,
        cost_estimate=pl.CostEstimate(flops=10**6, bytes_accessed=2 * 10**6, transcendentals=0),
    )(got)


def partner(array, axis, by):
    size = lax.axis_size(axis)
    return lax.ppermute(array, axis, [(i, i ^ by) for i in range(size)])


def exchange(blocks, axis):
    return lax.all_to_all(blocks, axis, split_axis=0, concat_axis=0, tiled=True)


def filter_gradient(volume, cotangent, padding):
    return lax.conv_general_dilated(
        volume[None],
        cotangent[None],
        (1, 1, 1),
        padding,
        rhs_dilation=(2, 2, 2),
        dimension_numbers=("CDHWN", "IDHWO", "DHWNC"),
        preferred_element_type=jnp.float32,
    )


def input_gradient(cotangent, filters):
    return lax.conv_general_dilated(
        cotangent[None],
        filters[::-1, ::-1, ::-1],
        (1, 1, 1),
        ((1, 2), (1, 2), (1, 2)),
        lhs_dilation=(2, 2, 2),
        dimension_numbers=("NDHWC", "DHWOI", "NDHWC"),
        preferred_element_type=jnp.float32,
    )[0]


def plain_body(act_64, cot_32, filters_32, act_128):
    shards = lax.axis_size("chan")
    samples = lax.axis_size("sample")
    position = lax.axis_index("chan")
    core = lax.axis_index("sample") % 2
    volume_64 = act_64[0]
    cot_local = cot_32[0]
    depth, height, width, shard_out = cot_local.shape
    planes, rows, columns, middle = volume_64.shape
    below = act_128.shape[4]
    slab = planes // shards
    part = middle // shards

    rim = lax.ppermute(act_128[:, -1:], "chan", [(i, i + 1) for i in range(shards - 1)])

    taps = filters_32.reshape(27, shards, part, shard_out).transpose(1, 0, 3, 2)
    lanes = 128 if taps.size // shards % 256 == 0 else 64
    taps = taps.reshape(shards, 2, -1, lanes)
    own_half = lax.dynamic_index_in_dim(taps, core, 1, keepdims=False)
    cot_rows = jnp.broadcast_to(cot_local.reshape(1, -1, lanes), (shards, cot_local.size // lanes, lanes))
    sent = jnp.concatenate([own_half, cot_rows], axis=1)
    got = exchange(sent, "chan")
    cut = own_half.shape[1]
    got_half = got[:, :cut]
    other_half = partner(got_half, "sample", 1)
    first = jnp.where(core == 0, got_half, other_half)
    second = jnp.where(core == 0, other_half, got_half)
    part_filters = jnp.concatenate([first, second], axis=1)
    part_filters = part_filters.reshape(shards, 3, 3, 3, shard_out, part)
    part_filters = part_filters.transpose(1, 2, 3, 5, 0, 4).reshape(3, 3, 3, part, -1)
    cot_all = got[:, cut:].reshape(shards, depth, height, width, shard_out)
    cot_all = cot_all.transpose(1, 2, 3, 0, 4).reshape(depth, height, width, -1)

    grad_upper = filter_gradient(volume_64, cot_local, ((1, 0),) * 3)
    total_upper = lax.psum(grad_upper, "sample")

    grad_part = input_gradient(cot_all, part_filters)
    own_part = lax.dynamic_slice_in_dim(volume_64, position * part, part, 3)
    cot_part = (grad_part * jnp.where(own_part > 0, 1.0, leak_slope)).astype(low)
    cot_got = exchange(cot_part.reshape(shards, -1, 128), "chan")
    cot_low = cot_got.reshape(shards, slab, rows, columns, part)
    cot_low = cot_low.transpose(1, 2, 3, 0, 4).reshape(slab, rows, columns, middle)

    window = jnp.concatenate([rim, act_128], axis=1)[0]
    grad_lower = filter_gradient(window, cot_low, ((0, 0), (1, 0), (1, 0)))
    blocks = grad_lower.reshape(27, shards, 2, -1, middle).transpose(2, 1, 0, 3, 4)
    mine = lax.dynamic_index_in_dim(blocks, core, 0, keepdims=False)
    theirs = lax.dynamic_index_in_dim(blocks, 1 - core, 0, keepdims=False)
    mine = mine + partner(theirs.astype(low), "sample", 1).astype(jnp.float32)
    got_terms = exchange(mine.astype(low), "chan")
    share = jnp.sum(got_terms.astype(jnp.float32), axis=0)
    if samples > 2:
        pairs = [[2 * i + k for i in range(samples // 2)] for k in range(2)]
        share = lax.psum(share, "sample", axis_index_groups=pairs)
    share = lax.all_gather(
        share, "sample", axis=1, tiled=True, axis_index_groups=[[i, i + 1] for i in range(0, samples, 2)]
    )
    total_lower = share.reshape(3, 3, 3, below // shards, middle)
    return (
        total_upper / samples,
        total_lower / samples,
        cot_low.astype(jnp.float32)[None],
    )


def chip_sum(terms, samples):
    core = lax.axis_index("sample") % 2
    blocks = terms.reshape(27, 2, -1, terms.shape[2])
    mine = lax.dynamic_index_in_dim(blocks, core, 1, keepdims=False)
    theirs = lax.dynamic_index_in_dim(blocks, 1 - core, 1, keepdims=False)
    mine = (mine + partner(theirs.astype(low), "sample", 1).astype(wide)).astype(low)
    total = mine.astype(wide)
    for by in range(2, samples, 2):
        pairs = [(i, (i + by) % samples) for i in range(samples)]
        total = total + lax.ppermute(mine, "sample", pairs).astype(wide)
    total = total * (1.0 / samples)
    other = partner(total, "sample", 1)
    first = jnp.where(core == 0, total, other)
    second = jnp.where(core == 0, other, total)
    return jnp.concatenate([first, second], axis=1)


def body(act_64, cot_32, filters_32, act_128):
    shards = lax.axis_size("chan")
    samples = lax.axis_size("sample")
    middle = act_64.shape[4]
    grid = cot_32.shape[1:4]
    shard_out = cot_32.shape[4]
    below = act_128.shape[4]
    if middle != 32 * shards or shards % 4 or samples != 4 or shard_out != 64 or (2 * grid[2]) != 8:
        return plain_body(act_64, cot_32, filters_32, act_128)
    core = lax.axis_index("sample") % 2
    cores = core[None].astype(jnp.int32)
    position = lax.axis_index("chan")[None].astype(jnp.int32)
    volume_64 = act_64[0]
    cot_local = cot_32[0]
    slab = volume_64.shape[0] // shards

    rim = lax.ppermute(act_128[:, -1:], "chan", [(i, i + 1) for i in range(shards - 1)])
    turned = filters_32.transpose(0, 1, 2, 4, 3).reshape(27, shard_out, middle)
    sent = pack(cores, turned, cot_local.reshape(-1, shard_out), shards)
    got = exchange(sent, "chan")
    other = partner(got[:, : len(slot_plan()) * shard_out // 2], "sample", 1)
    own = own_signs(position, volume_64)

    grad_upper = filter_gradient(volume_64, cot_local, ((1, 0),) * 3)
    grad_upper = grad_upper.transpose(0, 1, 2, 4, 3).reshape(27, shard_out, middle)
    total_upper = chip_sum(grad_upper, samples).reshape(3, 3, 3, shard_out, middle)
    total_upper = total_upper.transpose(0, 1, 2, 4, 3)

    cot_got = exchange(spread(cores, got, other, own, grid), "chan")
    cot_full, cot_low = unpack(cot_got, (slab, *volume_64.shape[1:3]))

    window = jnp.concatenate([rim, act_128], axis=1)[0]
    grad_lower = filter_gradient(window, cot_low, ((0, 0), (1, 0), (1, 0)))
    blocks = grad_lower.reshape(27, shards, 2, -1, middle).transpose(2, 1, 0, 3, 4)
    mine = lax.dynamic_index_in_dim(blocks, core, 0, keepdims=False)
    theirs = lax.dynamic_index_in_dim(blocks, 1 - core, 0, keepdims=False)
    mine = mine + partner(theirs.astype(low), "sample", 1).astype(wide)
    got_terms = exchange(mine.astype(low), "chan")
    share = jnp.sum(got_terms.astype(wide), axis=0)
    shares = lax.all_gather(share, "sample", axis=0)
    shares = shares.reshape(samples // 2, 2, *share.shape).sum(axis=0) * (1.0 / samples)
    total_lower = shares.transpose(1, 0, 2, 3).reshape(3, 3, 3, below // shards, middle)
    return (total_upper, total_lower, cot_full[None])


def solution(mesh):
    placed = (
        P("sample", None, None, None, None),
        P("sample", None, None, None, "chan"),
        P(None, None, None, None, "chan"),
        P("sample", "chan", None, None, None),
    )
    return jax.shard_map(
        body,
        mesh=mesh,
        in_specs=placed,
        out_specs=(
            P(None, None, None, None, "chan"),
            P(None, None, None, "chan", None),
            P("sample", "chan", None, None, None),
        ),
        check_vma=False,
    )
```

profile of v0, /device:TPU:0, one launch (start us, length us, event | category | flops | bytes accessed | tf_op | source)
XLA Modules:
  0.0 117.5 jit_solution(7631629920849507329)
XLA Ops:
  0.6 0.0 copy-start.1
  0.7 1.2 copy-done.1
  1.8 0.0 copy-start.2
  1.8 0.9 copy-done.2
  2.7 0.0 copy-start.5
  2.7 0.5 shard_map.67
  3.2 31.5 %all_to_all.15.got_ref = bf16[8,480,128]{2,1,0:T(8,128)(2,1)S(1)} all-to-all(bf16[8,480,128]{2,1,0:T(8,128)(2,1)S(1)} %shard_map.67), channel_id=1, replica_groups=mesh['sample'=4,'chan'=8] {'chan'}, dimensions={0} | all-to-all | bytes 1966080 | tf_op jit(solution)/shard_map/all_to_all | solution.py:234
  34.7 0.0 copy-start
  34.7 0.8 slice.9
  35.5 0.0 collective-permute-start.4
  35.5 0.0 copy-done.5
  35.5 2.2 %copy.29 = bf16[1,16,16,16,128]{4,0,3,2,1:T(2,128)(2,1)S(1)} copy(bf16[1,16,16,16,128]{4,3,2,1,0:T(8,128)(2,1)S(1)} %copy-done.5) | data formatting | bytes 2097152 | tf_op args[3]
  37.7 0.0 copy-start.3
  37.7 1.3 %copy-done.3 = bf16[1,16,16,16,128]{4,0,3,2,1:T(2,128)(2,1)} copy-done((bf16[1,16,16,16,128]{4,0,3,2,1:T(2,128)(2,1)}, bf16[1,16,16,16,128]{4,0,3,2,1:T(2,128)(2,1)S(1)}, u32[]{:S(2)}) %copy-start.3) | copy-done | bytes 1048600
  39.0 0.8 slice.8
  39.8 3.9 %collective-permute-start.3 = (bf16[1,1,16,16,128]{4,0,3,2,1:T(2,128)(2,1)}, bf16[1,1,16,16,128]{4,0,3,2,1:T(2,128)(2,1)}, u32[]{:S(2)}, u32[]{:S(2)}) collective-permute-start(bf16[1,1,16,16,128]{4,0,3,2,1:T(2,128)(2,1)} %slice.8), channel_id=1, source_target_pairs={{0,1},{1,2},{2,3},{3,4},{4,5},{5,6},{6,7},{8,9},{9,10},{10,11},{11... | collective-permute-start | bytes 196616 | tf_op jit(solution)/shard_map/ppermute | solution.py:359
  43.7 0.0 copy-done
  43.7 0.4 shard_map.68.own_ref
  44.1 0.0 collective-permute-done.4.other_ref
  44.1 2.1 %shard_map.69 = bf16[8,128,128]{2,1,0:T(8,128)(2,1)} custom-call(s32[1]{0:T(128)} %bitcast.5.core_ref, bf16[8,480,128]{2,1,0:T(8,128)(2,1)S(1)} %all_to_all.15.got_ref, bf16[8,224,128]{2,1,0:T(8,128)(2,1)S(1)} %collective-permute-done.4.other_ref, bf16[1024,128]{1,0:T(8,128)(2,1)S(1)} %shard_map.68.own_ref), custom_call_target="tpu_custom_call" | custom-call | flops 500000000 | bytes 3000000 | tf_op jit(solution)/shard_map/pallas_call | solution.py:178
  46.3 3.6 %all-to-all-start.1 = ((bf16[8,128,128]{2,1,0:T(8,128)(2,1)}), bf16[8,128,128]{2,1,0:T(8,128)(2,1)S(1)}, u32[]{:S(2)}, u32[]{:S(2)}) async-start(bf16[8,128,128]{2,1,0:T(8,128)(2,1)} %shard_map.69), calls=%async_computation.1 | async-start | bytes 524288 | tf_op jit(solution)/shard_map/all_to_all | solution.py:234
  49.9 11.9 %fusion = f32[3,3,3,64,256]{4,3,2,1,0:T(8,128)} fusion(bf16[1,64,8,8,256]{4,3,2,1,0:T(8,128)(2,1)S(1)} %copy-done, bf16[1,32,4,4,64]{4,3,2,1,0:T(4,128)(2,1)} %param.5), kind=kOutput, calls=%fused_computation | convolution fusion | flops 376668160 | bytes 3932160 | tf_op jit(solution)/shard_map/transpose | solution.py:367
  61.8 0.0 all-to-all-done.1.got_ref
  61.8 1.1 shard_map.70
  62.9 0.0 collective-permute-done.3
  62.9 0.0 copy-start.6
  62.9 7.8 %fusion.2 = f32[3,3,3,128,256]{4,3,2,1,0:T(8,128)S(1)} fusion(bf16[1,16,16,16,128]{4,0,3,2,1:T(2,128)(2,1)} %copy-done.3, bf16[1,1,16,16,128]{4,0,3,2,1:T(2,128)(2,1)} %collective-permute-done.3, bf16[1,8,8,8,256]{4,3,2,1,0:T(8,128)(2,1)S(1)} %bitcast.39), kind=kOutput, calls=%fused_computation.3 | convolution fusion | flops 834273280 | bytes 4915200 | tf_op jit(solution)/shard_map/conv_general_dilated | solution.py:238
  70.7 0.0 copy-start.4
  70.7 1.7 %copy-done.4 = f32[3,3,3,128,256]{4,3,2,1,0:T(8,128)} copy-done((f32[3,3,3,128,256]{4,3,2,1,0:T(8,128)}, f32[3,3,3,128,256]{4,3,2,1,0:T(8,128)S(1)}, u32[]{:S(2)}) %copy-start.4) | copy-done | bytes 3538968
  72.4 0.1 fusion.5
  72.5 0.3 collective-permute-start.5
  72.8 0.0 copy-done.6
  72.8 0.1 fusion.8
  72.9 0.4 collective-permute-start
  73.2 2.4 %collective-permute-done = bf16[27,32,256]{2,1,0:T(8,128)(2,1)S(1)} collective-permute-done((bf16[27,32,256]{2,1,0:T(8,128)(2,1)S(1)}, bf16[27,32,256]{2,1,0:T(8,128)(2,1)S(1)}, u32[]{:S(2)}, u32[]{:S(2)}) %collective-permute-start) | collective-permute-done | bytes 442400 | tf_op jit(solution)/shard_map/ppermute | solution.py:230
  75.7 0.1 fusion.6
  75.8 1.6 %collective-permute-start.1 = (bf16[27,32,256]{2,1,0:T(8,128)(2,1)S(1)}, bf16[27,32,256]{2,1,0:T(8,128)(2,1)S(1)}, u32[]{:S(2)}, u32[]{:S(2)}) collective-permute-start(bf16[27,32,256]{2,1,0:T(8,128)(2,1)S(1)} %fusion.6), channel_id=1, source_target_pairs={{0,16},{8,24},{16,0},{24,8},{1,17},{9,25},{17,1},{25,9},{2,18},{10... | collective-permute-start | bytes 1327112 | tf_op jit(solution)/shard_map/ppermute | solution.py:335
  77.4 0.0 collective-permute-done.5
  77.4 2.9 %fusion.4 = bf16[8,27,8,256]{3,2,1,0:T(8,128)(2,1)} fusion(bf16[8,27,8,256]{3,2,1,0:T(8,128)(2,1)} %collective-permute-done.5, f32[27,8,2,8,256]{4,3,2,1,0:T(8,128)} %bitcast.42, s32[]{:T(128)S(6)} %select_n.33), kind=kLoop, calls=%fused_computation.8 | loop fusion | flops 1327104 | bytes 3538948 | tf_op jit(solution)/shard_map/convert_element_type | solution.py:380
  80.2 5.7 %all-to-all-start.2 = ((bf16[8,27,8,256]{3,2,1,0:T(8,128)(2,1)}), bf16[8,27,8,256]{3,2,1,0:T(8,128)(2,1)S(1)}, u32[]{:S(2)}, u32[]{:S(2)}) async-start(bf16[8,27,8,256]{3,2,1,0:T(8,128)(2,1)} %fusion.4), calls=%async_computation.2 | async-start | bytes 1769472 | tf_op jit(solution)/shard_map/all_to_all | solution.py:234
  86.0 2.2 %collective-permute-done.1 = bf16[27,32,256]{2,1,0:T(8,128)(2,1)S(1)} collective-permute-done((bf16[27,32,256]{2,1,0:T(8,128)(2,1)S(1)}, bf16[27,32,256]{2,1,0:T(8,128)(2,1)S(1)}, u32[]{:S(2)}, u32[]{:S(2)}) %collective-permute-start.1) | collective-permute-done | bytes 442400 | tf_op jit(solution)/shard_map/ppermute | solution.py:335
  88.2 0.1 add_multiply_fusion
  88.3 0.1 collective-permute-start.2
  88.4 2.4 %collective-permute-done.2 = f32[27,32,256]{2,1,0:T(8,128)S(1)} collective-permute-done((f32[27,32,256]{2,1,0:T(8,128)S(1)}, f32[27,32,256]{2,1,0:T(8,128)S(1)}, u32[]{:S(2)}, u32[]{:S(2)}) %collective-permute-start.2) | collective-permute-done | bytes 884768 | tf_op jit(solution)/shard_map/ppermute | solution.py:230
  90.8 0.3 broadcast_select_fusion.1
  91.1 1.3 %pad_maximum_fusion.2 = f32[27,64,256]{2,1,0:T(8,128)} fusion(f32[27,32,256]{2,1,0:T(8,128)S(1)} %get-tuple-element.8, f32[27,32,256]{2,1,0:T(8,128)S(1)} %get-tuple-element.7), kind=kLoop, calls=%fused_computation.4 | loop fusion | flops 442368 | bytes 3538944 | tf_op jit(solution)/shard_map/concatenate | solution.py:340
  92.4 15.9 %all-to-all-done.2 = bf16[8,27,8,256]{3,2,1,0:T(8,128)(2,1)S(1)} async-done(((bf16[8,27,8,256]{3,2,1,0:T(8,128)(2,1)}), bf16[8,27,8,256]{3,2,1,0:T(8,128)(2,1)S(1)}, u32[]{:S(2)}, u32[]{:S(2)}) %all-to-all-start.2) | async-done | bytes 884768 | tf_op jit(solution)/shard_map/all_to_all | solution.py:234
  108.3 0.1 convert_reduce_fusion
  108.4 8.2 %all-gather = f32[108,8,256]{2,1,0:T(8,128)S(1)} all-gather(f32[27,8,256]{2,1,0:T(8,128)S(1)} %convert_reduce_fusion), channel_id=2, replica_groups=mesh['sample'=4,'chan'=8] {'sample'}, dimensions={0}, use_global_device_ids=true | all-gather | bytes 1105920 | tf_op jit(solution)/shard_map/all_gather | solution.py:382
  116.6 0.1 reduce_sum.19
  116.7 0.8 copy.34
  (1 shorter events, 0.0 us)
Async XLA Ops:
  0.6 1.2 copy-start.1
  1.8 0.9 copy-start.2
  2.7 32.8 %copy-start.5 = (bf16[1,16,16,16,128]{4,3,2,1,0:T(8,128)(2,1)S(1)}, bf16[1,16,16,16,128]{4,3,2,1,0:T(8,128)(2,1)}, u32[]{:S(2)}) copy-start(bf16[1,16,16,16,128]{4,3,2,1,0:T(8,128)(2,1)} %param.7) | copy-start | bytes 3145732
  34.7 9.0 %copy-start = (bf16[1,64,8,8,256]{4,3,2,1,0:T(8,128)(2,1)S(1)}, bf16[1,64,8,8,256]{4,3,2,1,0:T(8,128)(2,1)}, u32[]{:S(2)}) copy-start(bf16[1,64,8,8,256]{4,3,2,1,0:T(8,128)(2,1)} %param.4) | copy-start | bytes 6291460
  35.5 8.6 %collective-permute-start.4 = (bf16[8,224,128]{2,1,0:T(8,128)(2,1)}, bf16[8,224,128]{2,1,0:T(8,128)(2,1)S(1)}, u32[]{:S(2)}, u32[]{:S(2)}) collective-permute-start(bf16[8,224,128]{2,1,0:T(8,128)(2,1)} %slice.9), channel_id=1, source_target_pairs={{0,8},{8,0},{16,24},{24,16},{1,9},{9,1},{17,25},{25,17},{2,10},{10... | collective-permute-start | bytes 1376264 | tf_op jit(solution)/shard_map/ppermute | solution.py:230
  37.7 1.3 %copy-start.3 = (bf16[1,16,16,16,128]{4,0,3,2,1:T(2,128)(2,1)}, bf16[1,16,16,16,128]{4,0,3,2,1:T(2,128)(2,1)S(1)}, u32[]{:S(2)}) copy-start(bf16[1,16,16,16,128]{4,0,3,2,1:T(2,128)(2,1)S(1)} %copy.29) | copy-start | bytes 3145732
  39.8 23.1 %collective-permute-start.3 = (bf16[1,1,16,16,128]{4,0,3,2,1:T(2,128)(2,1)}, bf16[1,1,16,16,128]{4,0,3,2,1:T(2,128)(2,1)}, u32[]{:S(2)}, u32[]{:S(2)}) collective-permute-start(bf16[1,1,16,16,128]{4,0,3,2,1:T(2,128)(2,1)} %slice.8), channel_id=1, source_target_pairs={{0,1},{1,2},{2,3},{3,4},{4,5},{5,6},{6,7},{8,9},{9,10},{10,11},{11... | collective-permute-start | bytes 196616 | tf_op jit(solution)/shard_map/ppermute | solution.py:359
  46.3 15.5 %all-to-all-start.1 = ((bf16[8,128,128]{2,1,0:T(8,128)(2,1)}), bf16[8,128,128]{2,1,0:T(8,128)(2,1)S(1)}, u32[]{:S(2)}, u32[]{:S(2)}) async-start(bf16[8,128,128]{2,1,0:T(8,128)(2,1)} %shard_map.69), calls=%async_computation.1 | async-start | bytes 524288 | tf_op jit(solution)/shard_map/all_to_all | solution.py:234
  62.9 9.9 %copy-start.6 = (f32[3,3,3,64,256]{4,3,2,1,0:T(8,128)S(1)}, f32[3,3,3,64,256]{4,3,2,1,0:T(8,128)}, u32[]{:S(2)}) copy-start(f32[3,3,3,64,256]{4,3,2,1,0:T(8,128)} %fusion) | copy-start | bytes 5308420
  70.7 1.8 %copy-start.4 = (f32[3,3,3,128,256]{4,3,2,1,0:T(8,128)}, f32[3,3,3,128,256]{4,3,2,1,0:T(8,128)S(1)}, u32[]{:S(2)}) copy-start(f32[3,3,3,128,256]{4,3,2,1,0:T(8,128)S(1)} %fusion.2) | copy-start | bytes 10616836
  72.5 4.8 %collective-permute-start.5 = (bf16[8,27,8,256]{3,2,1,0:T(8,128)(2,1)S(1)}, bf16[8,27,8,256]{3,2,1,0:T(8,128)(2,1)}, u32[]{:S(2)}, u32[]{:S(2)}) collective-permute-start(bf16[8,27,8,256]{3,2,1,0:T(8,128)(2,1)S(1)} %fusion.5), channel_id=1, source_target_pairs={{0,8},{8,0},{16,24},{24,16},{1,9},{9,1},{17,25},{25,17},{2,10},{10... | collective-permute-start | bytes 2654216 | tf_op jit(solution)/shard_map/ppermute | solution.py:230
  72.9 2.8 %collective-permute-start = (bf16[27,32,256]{2,1,0:T(8,128)(2,1)S(1)}, bf16[27,32,256]{2,1,0:T(8,128)(2,1)S(1)}, u32[]{:S(2)}, u32[]{:S(2)}) collective-permute-start(bf16[27,32,256]{2,1,0:T(8,128)(2,1)S(1)} %fusion.8), channel_id=1, source_target_pairs={{0,8},{8,0},{16,24},{24,16},{1,9},{9,1},{17,25},{25,17},{2,10},{10... | collective-permute-start | bytes 1327112 | tf_op jit(solution)/shard_map/ppermute | solution.py:230
  75.8 12.4 %collective-permute-start.1 = (bf16[27,32,256]{2,1,0:T(8,128)(2,1)S(1)}, bf16[27,32,256]{2,1,0:T(8,128)(2,1)S(1)}, u32[]{:S(2)}, u32[]{:S(2)}) collective-permute-start(bf16[27,32,256]{2,1,0:T(8,128)(2,1)S(1)} %fusion.6), channel_id=1, source_target_pairs={{0,16},{8,24},{16,0},{24,8},{1,17},{9,25},{17,1},{25,9},{2,18},{10... | collective-permute-start | bytes 1327112 | tf_op jit(solution)/shard_map/ppermute | solution.py:335
  80.2 28.1 %all-to-all-start.2 = ((bf16[8,27,8,256]{3,2,1,0:T(8,128)(2,1)}), bf16[8,27,8,256]{3,2,1,0:T(8,128)(2,1)S(1)}, u32[]{:S(2)}, u32[]{:S(2)}) async-start(bf16[8,27,8,256]{3,2,1,0:T(8,128)(2,1)} %fusion.4), calls=%async_computation.2 | async-start | bytes 1769472 | tf_op jit(solution)/shard_map/all_to_all | solution.py:234
  88.3 2.5 %collective-permute-start.2 = (f32[27,32,256]{2,1,0:T(8,128)S(1)}, f32[27,32,256]{2,1,0:T(8,128)S(1)}, u32[]{:S(2)}, u32[]{:S(2)}) collective-permute-start(f32[27,32,256]{2,1,0:T(8,128)S(1)} %add_multiply_fusion), channel_id=1, source_target_pairs={{0,8},{8,0},{16,24},{24,16},{1,9},{9,1},{17,25},{25,17},{2,10},{10... | collective-permute-start | bytes 2654216 | tf_op jit(solution)/shard_map/ppermute | solution.py:230
where the time goes:
time: 118 us
  blocking collectives  39.7 us (34%)
  waiting for transfers between devices  23 us (19%)
  matrix products  19.7 us (17%)
  starting transfers between devices  15.5 us (13%)
  local copies, waits for them, and re-layouts  9.87 us (8%)
  other arithmetic  4.94 us (4%)
  Pallas kernels  4.1 us (3%)
    all_to_all x1, blocking collectives, exchange(): return lax.all_to_all(blocks, axis, split_axis=0, concat_axis=0, tiled=True)  31.5 us
    all_to_all x2, waiting for transfers between devices, exchange(): return lax.all_to_all(blocks, axis, split_axis=0, concat_axis=0, tiled=True)  15.9 us
    transpose x1, matrix products, body(): grad_upper.transpose(0, 1, 2, 4, 3).reshape(27, shard_out, middle)  11.9 us
    all_to_all x2, starting transfers between devices, exchange(): return lax.all_to_all(blocks, axis, split_axis=0, concat_axis=0, tiled=True)  9.33 us
    all_gather x1, blocking collectives, body(): shares = lax.all_gather(share, 'sample', axis=0)  8.18 us
    conv_general_dilated x1, matrix products, filter_gradient(): lax.conv_general_dilated(volume[None], cotangent[None], (1, 1, 1), paddin...  7.76 us
    unnamed x15, local copies, waits for them, and re-layouts  7.3 us
    ppermute x4, waiting for transfers between devices, partner(): return lax.ppermute(array, axis, [(i, i ^ by) for i in range(size)])  4.83 us
  transfers between devices with their start and end apart: 8, of which 4 were waited for; matrix products, arithmetic and copies ran while one was open for 17% of the time, Pallas kernels for 3%

commit v1 on v0

--- a/solution.py
+++ b/solution.py
@@ -1,4 +1,5 @@
 import functools
+import math
 
 import jax
 import jax.numpy as jnp
@@ -13,6 +14,7 @@
 params = pltpu.CompilerParams(vmem_limit_bytes=40 * 2**20)
 whole = pl.BlockSpec(memory_space=pltpu.VMEM)
 scalar = pl.BlockSpec(memory_space=pltpu.SMEM)
+anywhere = pl.BlockSpec(memory_space=pltpu.HBM)
 
 
 def slot_plan():
@@ -33,13 +35,32 @@
     return lax.broadcasted_iota(jnp.int32, shape, len(shape) - 1) // 32
 
 
-def pack_kernel(core_ref, filters_ref, cot_ref, sent_ref):
-    half = filters_ref.shape[1] // 2
+def pack_kernel(core_ref, filters_ref, cot_ref, sent_ref, held, cot_held, staged, arrived, left):
+    taps, half, _ = held.shape
     groups = slot_plan()
+    start = pl.multiple_of(core_ref[0] * half, half)
+    fetch_filters = pltpu.make_async_copy(filters_ref.at[:, pl.ds(start, half), :], held, arrived.at[0])
+    fetch_cot = pltpu.make_async_copy(cot_ref, cot_held, arrived.at[1])
+    fetch_cot.start()
+    fetch_filters.start()
+    slots = lane_slot((half, 128))
+    shards = staged.shape[0]
     rows = len(groups) * half
-    start = pl.multiple_of(core_ref[0] * half, half)
-    slots = lane_slot((half, 128))
-    shards = sent_ref.shape[0]
+    outs = cot_held.shape[1]
+    cells = cot_held.shape[0]
+
+    def send(index, first, count):
+        part = pl.ds(first, count)
+        return pltpu.make_async_copy(staged.at[:, part, :], sent_ref.at[:, part, :], left.at[index])
+
+    fetch_cot.wait()
+    turned_cot = cot_held[...].astype(wide).T.astype(low)
+    for d in range(shards):
+        for b in range(cells // 128):
+            staged[d, pl.ds(rows + b * outs, outs), :] = turned_cot[:, b * 128 : (b + 1) * 128]
+    copies = [send(0, rows, cells // 128 * outs)]
+    copies[0].start()
+    fetch_filters.wait()
     for g, group in enumerate(groups):
         for tile in range(shards // 4):
             turned = []
@@ -47,31 +68,38 @@
                 if tap is None:
                     turned.append([jnp.zeros((half, 128), wide)] * 4)
                     continue
-                block = filters_ref[tap_index(tap), pl.ds(start, half), pl.ds(tile * 128, 128)].astype(wide)
+                block = held[tap_index(tap), :, pl.ds(tile * 128, 128)].astype(wide)
                 turned.append([block] + [pltpu.roll(block, 32 * r, 1) for r in range(1, 4)])
             for m in range(4):
                 joined = turned[0][(0 - m) % 4]
                 for k in range(1, 4):
                     joined = jnp.where(slots == k, turned[k][(k - m) % 4], joined)
-                sent_ref[tile * 4 + m, pl.ds(g * half, half), :] = joined.astype(low)
-    turned_cot = cot_ref[...].astype(wide).T.astype(low)
-    outs, cells = turned_cot.shape
-    for d in range(shards):
-        for b in range(cells // 128):
-            sent_ref[d, pl.ds(rows + b * outs, outs), :] = turned_cot[:, b * 128 : (b + 1) * 128]
+                staged[tile * 4 + m, pl.ds(g * half, half), :] = joined.astype(low)
+        copies.append(send(g + 1, g * half, half))
+        copies[-1].start()
+    for copy in copies:
+        copy.wait()
 
 
 def pack(core, filters, cot, shards):
-    outs = filters.shape[1]
-    rows = len(slot_plan()) * (outs // 2) + cot.shape[0] // 128 * outs
+    taps, outs, middle = filters.shape
+    groups = len(slot_plan())
+    shape = (shards, groups * (outs // 2) + cot.shape[0] // 128 * outs, 128)
     return pl.pallas_call(
         pack_kernel,
-        out_shape=jax.ShapeDtypeStruct((shards, rows, 128), low),
-        in_specs=[scalar, whole, whole],
-        out_specs=whole,
+        out_shape=pltpu.HBM(shape, low),
+        in_specs=[scalar, anywhere, anywhere],
+        out_specs=anywhere,
+        scratch_shapes=[
+            pltpu.VMEM((taps, outs // 2, middle), low),
+            pltpu.VMEM(cot.shape, low),
+            pltpu.VMEM(shape, low),
+            pltpu.SemaphoreType.DMA((2,)),
+            pltpu.SemaphoreType.DMA((groups + 1,)),
+        ],
         compiler_params=params,
         cost_estimate=pl.CostEstimate(flops=10**6, bytes_accessed=3 * 10**6, transcendentals=0),
-    )(core, filters, cot)
+    )(core, pltpu.with_memory_space_constraint(filters, pltpu.HBM), pltpu.with_memory_space_constraint(cot, pltpu.HBM))
 
 
 def sign_kernel(position_ref, volume_ref, own_ref):
@@ -111,26 +139,36 @@
     )(position, split)
 
 
-def spread_kernel(grid, core_ref, got_ref, other_ref, own_ref, sent_ref, weight, turned, products, joined):
+def first_kernel(core_ref, got_ref, products_ref, later_ref, weight, turned):
+    shards = got_ref.shape[0]
+    half = later_ref.shape[0] // shards
+    groups = len(slot_plan())
+    core = core_ref[0]
+    for c in range(shards):
+        span = pl.ds(c * half, half)
+        for g in range(groups):
+            weight[span, pl.ds(g * 128, 128)] = got_ref[c, pl.ds(g * half, half), :]
+        for b in range(later_ref.shape[1] // 128):
+            lanes = pl.ds(b * 128, 128)
+            first = groups * half + b * 2 * half
+            turned[span, lanes] = got_ref[c, pl.ds(pl.multiple_of(first + core * half, half), half), :]
+            later_ref[span, lanes] = got_ref[c, pl.ds(pl.multiple_of(first + (1 - core) * half, half), half), :]
+    products_ref[...] = lax.dot_general(
+        turned[...], weight[...], (((0,), (0,)), ((), ())), preferred_element_type=wide
+    )
+
+
+def spread_kernel(grid, first_ref, later_ref, other_ref, own_ref, sent_ref, weight, products, joined):
     depth, height, width = grid
     cells = depth * height * width
-    shards = got_ref.shape[0]
+    shards = other_ref.shape[0]
     groups = len(slot_plan())
-    half = other_ref.shape[1] // groups
-    outs = 2 * half
-    core = core_ref[0]
+    half = later_ref.shape[0] // shards
     for c in range(shards):
-        first = pl.multiple_of(c * outs + core * half, half)
-        second = pl.multiple_of(c * outs + (1 - core) * half, half)
         for g in range(groups):
-            weight[pl.ds(first, half), pl.ds(g * 128, 128)] = got_ref[c, pl.ds(g * half, half), :]
-            weight[pl.ds(second, half), pl.ds(g * 128, 128)] = other_ref[c, pl.ds(g * half, half), :]
-        for b in range(cells // 128):
-            turned[pl.ds(c * outs, outs), pl.ds(b * 128, 128)] = got_ref[
-                c, pl.ds(groups * half + b * outs, outs), :
-            ]
-    products[pl.ds(0, cells), :] = lax.dot_general(
-        turned[...], weight[...], (((0,), (0,)), ((), ())), preferred_element_type=wide
+            weight[pl.ds(c * half, half), pl.ds(g * 128, 128)] = other_ref[c, pl.ds(g * half, half), :]
+    products[pl.ds(0, cells), :] = first_ref[...] + lax.dot_general(
+        later_ref[...], weight[...], (((0,), (0,)), ((), ())), preferred_element_type=wide
     )
     products[pl.ds(cells, products.shape[0] - cells), :] = jnp.zeros(
         (products.shape[0] - cells, products.shape[1]), wide
@@ -170,28 +208,47 @@
         sent_ref[n] = (joined[...] * slope).astype(low)
 
 
-def spread(core, got, other, own, grid):
-    cells = grid[0] * grid[1] * grid[2]
+def first_terms(core, got, cells):
     shards = got.shape[0]
     groups = len(slot_plan())
-    outs = 2 * other.shape[1] // groups
+    half = got.shape[1] // (groups + 2 * (cells // 128))
+    lanes = groups * 128
+    return pl.pallas_call(
+        first_kernel,
+        out_shape=(
+            jax.ShapeDtypeStruct((cells, lanes), wide),
+            jax.ShapeDtypeStruct((shards * half, cells), low),
+        ),
+        in_specs=[scalar, whole],
+        out_specs=(whole, whole),
+        scratch_shapes=[pltpu.VMEM((shards * half, lanes), low), pltpu.VMEM((shards * half, cells), low)],
+        compiler_params=params,
+        cost_estimate=pl.CostEstimate(flops=10**8, bytes_accessed=3 * 10**6, transcendentals=0),
+    )(core, got)
+
+
+def spread(first, later, other, own, grid):
+    cells, lanes = first.shape
+    shards = other.shape[0]
+    half = later.shape[0] // shards
+    rows = lanes // 128 * half
     return pl.pallas_call(
         functools.partial(spread_kernel, grid),
         out_shape=jax.ShapeDtypeStruct((shards, 2 * cells // shards, 128), low),
-        in_specs=[scalar, whole, whole, whole],
+        grid=(1,),
+        in_specs=[whole, whole, pl.BlockSpec((shards, rows, 128), lambda i: (0, 0, 0)), whole],
         out_specs=whole,
         scratch_shapes=[
-            pltpu.VMEM((shards * outs, groups * 128), low),
-            pltpu.VMEM((shards * outs, cells), low),
-            pltpu.VMEM((cells + 32, groups * 128), wide),
+            pltpu.VMEM((shards * half, lanes), low),
+            pltpu.VMEM((cells + 32, lanes), wide),
             pltpu.VMEM((2 * cells // shards, 128), wide),
         ],
         compiler_params=params,
         cost_estimate=pl.CostEstimate(flops=5 * 10**8, bytes_accessed=3 * 10**6, transcendentals=0),
-    )(core, got, other, own)
-
-
-def unpack_kernel(got_ref, wide_ref, low_ref):
+    )(first, later, other, own)
+
+
+def unpack_kernel(got_ref, wide_ref):
     shards, rows, _ = got_ref.shape
     planes, height, columns, _ = wide_ref.shape
     slots = lane_slot((rows, 128))
@@ -210,19 +267,123 @@
                 for y in range(height // 2):
                     at = (2 * z + slot // 2, 2 * y + slot % 2)
                     wide_ref[at[0], at[1], :, lanes] = joined[z, y]
-    low_ref[...] = wide_ref[...].astype(low)
 
 
 def unpack(got, grid):
     shape = (*grid, got.shape[0] * 32)
     return pl.pallas_call(
         unpack_kernel,
-        out_shape=(jax.ShapeDtypeStruct(shape, wide), jax.ShapeDtypeStruct(shape, low)),
+        out_shape=jax.ShapeDtypeStruct(shape, wide),
         in_specs=[whole],
-        out_specs=(whole, whole),
+        out_specs=whole,
         compiler_params=params,
         cost_estimate=pl.CostEstimate(flops=10**6, bytes_accessed=2 * 10**6, transcendentals=0),
     )(got)
+
+
+def window_kernel(rim_ref, volume_ref, window_ref, grid):
+    planes, rows, columns, channels = grid.shape
+    grid[0] = rim_ref[0].astype(wide)
+    grid[pl.ds(1, planes - 1)] = volume_ref[...].astype(wide)
+    flat = grid.reshape(planes * rows * columns, channels)
+    half = columns // 2
+    count = planes * rows * half
+    first = lax.broadcasted_iota(jnp.int32, (count, channels), 0) % half == 0
+    even = flat[pl.ds(0, count, stride=2), :]
+    odd = flat[pl.ds(1, count, stride=2), :]
+    before = jnp.where(first, 0.0, pltpu.roll(odd, 1, 0))
+    for col, part in enumerate((before, even, odd)):
+        part = part.reshape(planes, rows // 2, 2, half, channels)
+        on_even, on_odd = part[:, :, 0], part[:, :, 1]
+        ahead = jnp.concatenate([jnp.zeros_like(on_odd[:, :1]), on_odd[:, :-1]], axis=1)
+        for row, taken in enumerate((ahead, on_even, on_odd)):
+            taken = taken.reshape(planes, rows // 2 * half, channels).astype(low)
+            for plane in range(planes):
+                window_ref[col * 3 + row, plane % 2, plane // 2] = taken[plane]
+
+
+def windows(rim, volume):
+    planes, rows, columns, channels = volume.shape
+    shape = (9, 2, planes // 2 + 1, rows * columns // 4, channels)
+    return pl.pallas_call(
+        window_kernel,
+        out_shape=jax.ShapeDtypeStruct(shape, low),
+        in_specs=[whole, whole],
+        out_specs=whole,
+        scratch_shapes=[pltpu.VMEM((planes + 1, rows, columns, channels), wide)],
+        compiler_params=params,
+        cost_estimate=pl.CostEstimate(flops=10**6, bytes_accessed=4 * 10**6, transcendentals=0),
+    )(rim, volume)
+
+
+def lanes_joined(blocks, slot, slots):
+    joined = blocks[0][(0 - slot) % 4]
+    for m in range(1, 4):
+        joined = jnp.where(slots == m, blocks[m][(m - slot) % 4], joined)
+    return joined
+
+
+def lower_kernel(core_ref, got_ref, other_ref, own_window, other_window, sent_ref, cells, staged, left):
+    shards, rows, _ = got_ref.shape
+    planes, height, columns, middle = cells.shape
+    count = staged.shape[1] // (own_window.shape[4] // shards)
+    slots = lane_slot((rows, 128))
+    sides = []
+    for source in (got_ref, other_ref):
+        for tile in range(shards // 4):
+            turned = []
+            for m in range(4):
+                block = source[tile * 4 + m].astype(wide)
+                turned.append([block] + [pltpu.roll(block, 32 * r, 1) for r in range(1, 4)])
+            for slot in range(4):
+                joined = lanes_joined(turned, slot, slots).reshape(planes // 2, height // 2, columns, 128)
+                for z in range(planes // 2):
+                    for y in range(height // 2):
+                        cells[2 * z + slot // 2, 2 * y + slot % 2, :, pl.ds(tile * 128, 128)] = joined[z, y]
+        sides.append(cells[...].reshape(planes * height * columns, middle).T.astype(low))
+    below = own_window.shape[4]
+    share = below // shards
+    copies = []
+    for pair in range(count // 2):
+        total = None
+        for side, window in zip(sides, (own_window, other_window), strict=True):
+            both = []
+            for n in range(2):
+                tap = jnp.minimum(core_ref[0] * count + 2 * pair + n, 26)
+                depth, row, col = tap // 9, tap // 3 % 3, tap % 3
+                taken = window[col * 3 + row, depth % 2, pl.ds(depth // 2, planes)]
+                both.append(taken.reshape(planes * height * columns, below))
+            term = jnp.dot(side, jnp.concatenate(both, axis=1), preferred_element_type=wide)
+            total = term if total is None else total + term
+        total = total.T.astype(low)
+        for n in range(2):
+            for d in range(shards):
+                start = n * below + d * share
+                staged[d, pl.ds((2 * pair + n) * share, share), :] = total[start : start + share]
+        part = pl.ds(2 * pair * share, 2 * share)
+        copies.append(pltpu.make_async_copy(staged.at[:, part, :], sent_ref.at[:, part, :], left.at[pair]))
+        copies[-1].start()
+    for copy in copies:
+        copy.wait()
+
+
+def lower_terms(core, got, other, own_window, other_window, grid):
+    shards = got.shape[0]
+    below = own_window.shape[4]
+    middle = 32 * shards
+    return pl.pallas_call(
+        lower_kernel,
+        out_shape=pltpu.HBM((shards, 14 * below // shards, middle), low),
+        in_specs=[scalar, whole, whole, whole, whole],
+        out_specs=anywhere,
+        scratch_shapes=[
+            pltpu.VMEM((*grid, middle), wide),
+            pltpu.VMEM((shards, 14 * below // shards, middle), low),
+            pltpu.SemaphoreType.DMA((7,)),
+        ],
+        compiler_params=params,
+        cost_estimate=pl.CostEstimate(flops=10**9, bytes_accessed=6 * 10**6, transcendentals=0),
+    )(core, got, other, own_window, other_window)
 
 
 def partner(array, axis, by):
@@ -323,12 +484,17 @@
     )
 
 
-def chip_sum(terms, samples):
+def core_halves(terms):
     core = lax.axis_index("sample") % 2
     blocks = terms.reshape(27, 2, -1, terms.shape[2])
     mine = lax.dynamic_index_in_dim(blocks, core, 1, keepdims=False)
     theirs = lax.dynamic_index_in_dim(blocks, 1 - core, 1, keepdims=False)
-    mine = (mine + partner(theirs.astype(low), "sample", 1).astype(wide)).astype(low)
+    return mine, theirs.astype(low)
+
+
+def sample_sum(mine, theirs, samples):
+    core = lax.axis_index("sample") % 2
+    mine = (mine + partner(theirs, "sample", 1).astype(wide)).astype(low)
     total = mine.astype(wide)
     for by in range(2, samples, 2):
         pairs = [(i, (i + by) % samples) for i in range(samples)]
@@ -360,28 +526,31 @@
     turned = filters_32.transpose(0, 1, 2, 4, 3).reshape(27, shard_out, middle)
     sent = pack(cores, turned, cot_local.reshape(-1, shard_out), shards)
     got = exchange(sent, "chan")
-    other = partner(got[:, : len(slot_plan()) * shard_out // 2], "sample", 1)
+
     own = own_signs(position, volume_64)
-
+    window = windows(rim[0], act_128[0])
     grad_upper = filter_gradient(volume_64, cot_local, ((1, 0),) * 3)
     grad_upper = grad_upper.transpose(0, 1, 2, 4, 3).reshape(27, shard_out, middle)
-    total_upper = chip_sum(grad_upper, samples).reshape(3, 3, 3, shard_out, middle)
+    halves = core_halves(grad_upper)
+    got, own, window, halves = lax.optimization_barrier((got, own, window, halves))
+    other = partner(got, "sample", 1)
+    first, later = first_terms(cores, got, math.prod(grid))
+    cot_sent = spread(first, later, other, own, grid)
+
+    cot_sent, window, halves = lax.optimization_barrier((cot_sent, window, halves))
+    cot_got = exchange(cot_sent, "chan")
+    other_window = partner(window, "sample", 1)
+    total_upper = sample_sum(*halves, samples).reshape(3, 3, 3, shard_out, middle)
     total_upper = total_upper.transpose(0, 1, 2, 4, 3)
 
-    cot_got = exchange(spread(cores, got, other, own, grid), "chan")
-    cot_full, cot_low = unpack(cot_got, (slab, *volume_64.shape[1:3]))
-
-    window = jnp.concatenate([rim, act_128], axis=1)[0]
-    grad_lower = filter_gradient(window, cot_low, ((0, 0), (1, 0), (1, 0)))
-    blocks = grad_lower.reshape(27, shards, 2, -1, middle).transpose(2, 1, 0, 3, 4)
-    mine = lax.dynamic_index_in_dim(blocks, core, 0, keepdims=False)
-    theirs = lax.dynamic_index_in_dim(blocks, 1 - core, 0, keepdims=False)
-    mine = mine + partner(theirs.astype(low), "sample", 1).astype(wide)
-    got_terms = exchange(mine.astype(low), "chan")
-    share = jnp.sum(got_terms.astype(wide), axis=0)
-    shares = lax.all_gather(share, "sample", axis=0)
-    shares = shares.reshape(samples // 2, 2, *share.shape).sum(axis=0) * (1.0 / samples)
-    total_lower = shares.transpose(1, 0, 2, 3).reshape(3, 3, 3, below // shards, middle)
+    other_cot = partner(cot_got, "sample", 1)
+    slab_grid = (slab, *volume_64.shape[1:3])
+    terms = lower_terms(cores, cot_got, other_cot, window, other_window, slab_grid)
+    share = jnp.sum(exchange(terms, "chan").astype(wide), axis=0)
+    cot_full = unpack(cot_got, slab_grid)
+    shares = lax.all_gather(share.astype(low), "sample", axis=0).astype(wide)
+    shares = shares.reshape(samples // 2, -1, middle).sum(axis=0) * (1.0 / samples)
+    total_lower = shares[: 27 * below // shards].reshape(3, 3, 3, below // shards, middle)
     return (total_upper, total_lower, cot_full[None])
 
 

time: 118 us -> 95.6 us (0.81)
  blocking collectives: 39.7 us -> 6.82 us
  waiting for transfers between devices: 23 us -> 33.1 us
  matrix products: 19.7 us -> 10.4 us
  Pallas kernels: 4.1 us -> 12.8 us
  local copies, waits for them, and re-layouts: 9.87 us -> 2.69 us
  starting transfers between devices: 15.5 us -> 22.1 us
  other arithmetic: 4.94 us -> 6.37 us
    all_to_all x1 -> x0, blocking collectives: 31.5 us -> none  [exchange(): return lax.all_to_all(blocks, axis, split_axis=0, concat_axis=0, tiled=True)]
    all_to_all x2 -> x3, waiting for transfers between devices: 15.9 us -> 28.9 us  [exchange(): return lax.all_to_all(blocks, axis, split_axis=0, concat_axis=0, tiled=True)]
    pallas_call x2 -> x5, Pallas kernels: 1.56 us -> 10.4 us  [the longest x1 4.38 us: lower_terms(): pl.pallas_call(lower_kernel, out_shape=pltpu.HBM((shards, 14 * below // s...]
    conv_general_dilated x1 -> x0, matrix products: 7.76 us -> none  [filter_gradient(): lax.conv_general_dilated(volume[None], cotangent[None], (1, 1, 1), paddin...]
    unnamed x15 -> x6, local copies, waits for them, and re-layouts: 7.3 us -> 0.02 us
    all_to_all x2 -> x3, starting transfers between devices: 9.33 us -> 15.9 us  [exchange(): return lax.all_to_all(blocks, axis, split_axis=0, concat_axis=0, tiled=True)]
    ppermute x1, waiting for transfers between devices: 2.21 us -> 0.01 us  [sample_sum(): total = total + lax.ppermute(mine, 'sample', pairs).astype(wide)]
    mul x2, other arithmetic: 0.18 us -> 1.95 us  [the longest x1 1.16 us: sample_sum(): total = total * (1.0 / samples)]
  transfers between devices with their start and end apart: 8 -> 10, of which waited for: 4 -> 7; matrix products, arithmetic and copies ran while one was open for 17% -> 19% of each run, Pallas kernels for 3% -> 9%
where the time goes in v1:
time: 95.6 us; the launch traced here: 95 us
  waiting for transfers between devices  33.1 us (35%)
  starting transfers between devices  22.1 us (23%)
  Pallas kernels  12.8 us (13%)
  matrix products  10.4 us (11%)
  blocking collectives  6.82 us (7%)
  other arithmetic  6.37 us (7%)
  local copies, waits for them, and re-layouts  2.69 us (3%)
    all_to_all x3, waiting for transfers between devices, exchange(): return lax.all_to_all(blocks, axis, split_axis=0, concat_axis=0, tiled=True)  28.9 us
    all_to_all x3, starting transfers between devices, exchange(): return lax.all_to_all(blocks, axis, split_axis=0, concat_axis=0, tiled=True)  15.9 us
    transpose x1, matrix products, body(): grad_upper.transpose(0, 1, 2, 4, 3).reshape(27, shard_out, middle)  10.4 us
    all_gather x1, blocking collectives, body(): shares = lax.all_gather(share.astype(low), 'sample', axis=0).astype(wide)  6.82 us
    pallas_call x1, Pallas kernels, lower_terms(): pl.pallas_call(lower_kernel, out_shape=pltpu.HBM((shards, 14 * below // s...  4.38 us
    ppermute x5, waiting for transfers between devices, partner(): return lax.ppermute(array, axis, [(i, i ^ by) for i in range(size)])  4.18 us
    ppermute x1, starting transfers between devices, body(): lax.ppermute(act_128[:, -1:], 'chan', [(i, i + 1) for i in range(shards -...  3.92 us
    pallas_call x1, Pallas kernels, pack(): pl.pallas_call(pack_kernel, out_shape=pltpu.HBM(shape, low), in_specs=[sc...  2.36 us
  transfers between devices with their start and end apart: 10, of which 7 were waited for; matrix products, arithmetic and copies ran while one was open for 19% of the time, Pallas kernels for 9%

profile of v1, /device:TPU:0, one launch (start us, length us, event | category | flops | bytes accessed | tf_op | source)
XLA Modules:
  0.0 95.0 jit_solution(5127386082533508488)
XLA Ops:
  0.6 0.0 copy-start
  0.7 2.4 %shard_map.67 = bf16[8,480,128]{2,1,0:T(8,128)(2,1)} custom-call(s32[1]{0:T(128)} %bitcast.core_ref, bf16[27,64,256]{2,1,0:T(8,128)(2,1)} %bitcast.28, bf16[512,64]{1,0:T(8,128)(2,1)} %bitcast.31), custom_call_target="tpu_custom_call" | custom-call | flops 1000000 | bytes 3000000 | tf_op jit(solution)/shard_map/pallas_call | solution.py:88
  3.0 0.0 copy-start.2
  3.0 7.4 %all-to-all-start = ((bf16[8,480,128]{2,1,0:T(8,128)(2,1)}), bf16[8,480,128]{2,1,0:T(8,128)(2,1)}, u32[]{:S(2)}, u32[]{:S(2)}) async-start(bf16[8,480,128]{2,1,0:T(8,128)(2,1)} %shard_map.67), calls=%async_computation | async-start | bytes 1966080 | tf_op jit(solution)/shard_map/all_to_all | solution.py:395
  10.5 0.8 slice.6
  11.3 3.9 %collective-permute-start = (bf16[1,1,16,16,128]{4,3,2,1,0:T(8,128)(2,1)S(1)}, bf16[1,1,16,16,128]{4,3,2,1,0:T(8,128)(2,1)S(1)}, u32[]{:S(2)}, u32[]{:S(2)}) collective-permute-start(bf16[1,1,16,16,128]{4,3,2,1,0:T(8,128)(2,1)S(1)} %slice.6), channel_id=1, source_target_pairs={{0,1},{1,2},{2,3},{3,4},{4,5},{5,6},{6,7},{8,9},{9,10},{10,11},{11... | collective-permute-start | bytes 196616 | tf_op jit(solution)/shard_map/ppermute | solution.py:525
  15.2 0.0 copy-done
  15.2 0.4 shard_map.68.own_ref
  15.7 0.0 copy-done.2
  15.7 10.4 %fusion = f32[3,3,3,64,256]{4,3,2,1,0:T(8,128)S(1)} fusion(bf16[1,64,8,8,256]{4,3,2,1,0:T(8,128)(2,1)S(1)} %copy-done, bf16[1,32,4,4,64]{4,3,2,1,0:T(4,128)(2,1)S(1)} %copy-done.2), kind=kOutput, calls=%fused_computation | convolution fusion | flops 376668160 | bytes 3932160 | tf_op jit(solution)/shard_map/transpose | solution.py:533
  26.1 0.0 copy-start.1
  26.1 1.0 %dynamic-slice_bitcast_fusion = f32[27,32,256]{2,1,0:T(8,128)} fusion(f32[27,2,32,256]{3,2,1,0:T(8,128)S(1)} %bitcast.26, s32[]{:T(128)S(6)} %select_n.32), kind=kLoop, calls=%fused_computation.7 | loop fusion | bytes 1769476 | tf_op jit(solution)/shard_map/jit(dynamic_index_in_dim)/squeeze | solution.py:490
  27.1 0.8 fusion.2
  27.9 0.0 collective-permute-done
  27.9 0.0 copy-done.1
  27.9 0.8 shard_map.69.own_window
  28.8 6.2 %all-to-all-done.got_ref = bf16[8,480,128]{2,1,0:T(8,128)(2,1)} async-done(((bf16[8,480,128]{2,1,0:T(8,128)(2,1)}), bf16[8,480,128]{2,1,0:T(8,128)(2,1)}, u32[]{:S(2)}, u32[]{:S(2)}) %all-to-all-start) | async-done | bytes 983072 | tf_op jit(solution)/shard_map/all_to_all | solution.py:395
  34.9 0.0 collective-permute-start.1
  35.0 1.8 %shard_map.70 = (f32[512,896]{1,0:T(8,128)S(1)}, bf16[256,512]{1,0:T(8,128)(2,1)S(1)}) custom-call(s32[1]{0:T(128)} %bitcast.core_ref, bf16[8,480,128]{2,1,0:T(8,128)(2,1)} %all-to-all-done.got_ref), custom_call_target="tpu_custom_call" | custom-call | flops 100000000 | bytes 3000000 | tf_op jit(solution)/shard_map/pallas_call | solution.py:216
  36.7 1.0 %collective-permute-done.1.other_ref = bf16[8,480,128]{2,1,0:T(8,128)(2,1)S(1)} collective-permute-done((bf16[8,480,128]{2,1,0:T(8,128)(2,1)}, bf16[8,480,128]{2,1,0:T(8,128)(2,1)S(1)}, u32[]{:S(2)}, u32[]{:S(2)}) %collective-permute-start.1) | collective-permute-done | bytes 983072 | tf_op jit(solution)/shard_map/ppermute | solution.py:391
  37.7 1.9 %shard_map.71 = bf16[8,128,128]{2,1,0:T(8,128)(2,1)} custom-call(f32[512,896]{1,0:T(8,128)S(1)} %get-tuple-element.15.first_ref, bf16[256,512]{1,0:T(8,128)(2,1)S(1)} %get-tuple-element.16.later_ref, bf16[8,480,128]{2,1,0:T(8,128)(2,1)S(1)} %collective-permute-done.1.other_ref, bf16[1024,128]{1,0:T(8,128)(2,1)S(1)} %shard_map.68.own_ref), custom_call_target="tpu_custom_call" | custom-call | flops 500000000 | bytes 3000000 | tf_op jit(solution)/shard_map/pallas_call | solution.py:235
  39.7 0.1 collective-permute-start.6
  39.8 0.4 collective-permute-start.2
  40.2 4.9 %all-to-all-start.1 = ((bf16[8,128,128]{2,1,0:T(8,128)(2,1)}), bf16[8,128,128]{2,1,0:T(8,128)(2,1)S(1)}, u32[]{:S(2)}, u32[]{:S(2)}) async-start(bf16[8,128,128]{2,1,0:T(8,128)(2,1)} %shard_map.71), calls=%async_computation.1 | async-start | bytes 524288 | tf_op jit(solution)/shard_map/all_to_all | solution.py:395
  45.0 0.3 collective-permute-done.2
  45.3 1.4 %add_convert_fusion = bf16[27,32,256]{2,1,0:T(8,128)(2,1)S(1)} fusion(f32[27,32,256]{2,1,0:T(8,128)} %dynamic-slice_bitcast_fusion, bf16[27,32,256]{2,1,0:T(8,128)(2,1)} %collective-permute-done.2), kind=kLoop, calls=%fused_computation.5 | loop fusion | flops 663552 | bytes 1769472 | tf_op jit(solution)/shard_map/convert_element_type | solution.py:497
  46.8 1.6 %collective-permute-start.3 = (bf16[27,32,256]{2,1,0:T(8,128)(2,1)S(1)}, bf16[27,32,256]{2,1,0:T(8,128)(2,1)}, u32[]{:S(2)}, u32[]{:S(2)}) collective-permute-start(bf16[27,32,256]{2,1,0:T(8,128)(2,1)S(1)} %add_convert_fusion), channel_id=1, source_target_pairs={{0,16},{8,24},{16,0},{24,8},{1,17},{9,25},{17,1},{25,9},{2,18},{10... | collective-permute-start | bytes 1327112 | tf_op jit(solution)/shard_map/ppermute | solution.py:501
  48.3 5.9 %all-to-all-done.1.got_ref = bf16[8,128,128]{2,1,0:T(8,128)(2,1)S(1)} async-done(((bf16[8,128,128]{2,1,0:T(8,128)(2,1)}), bf16[8,128,128]{2,1,0:T(8,128)(2,1)S(1)}, u32[]{:S(2)}, u32[]{:S(2)}) %all-to-all-start.1) | async-done | bytes 262176 | tf_op jit(solution)/shard_map/all_to_all | solution.py:395
  54.3 0.0 collective-permute-start.5
  54.3 1.5 %collective-permute-done.5.other_ref = bf16[8,128,128]{2,1,0:T(8,128)(2,1)S(1)} collective-permute-done((bf16[8,128,128]{2,1,0:T(8,128)(2,1)S(1)}, bf16[8,128,128]{2,1,0:T(8,128)(2,1)S(1)}, u32[]{:S(2)}, u32[]{:S(2)}) %collective-permute-start.5) | collective-permute-done | bytes 262176 | tf_op jit(solution)/shard_map/ppermute | solution.py:391
  55.8 0.0 collective-permute-done.6.other_window
  55.8 4.4 %shard_map.72 = bf16[8,224,256]{2,1,0:T(8,128)(2,1)} custom-call(s32[1]{0:T(128)} %bitcast.core_ref, bf16[8,128,128]{2,1,0:T(8,128)(2,1)S(1)} %all-to-all-done.1.got_ref, bf16[8,128,128]{2,1,0:T(8,128)(2,1)S(1)} %collective-permute-done.5.other_ref, bf16[9,2,9,64,128]{4,3,2,1,0:T(8,128)(2,1)S(1)} %shard_map.69.own_window, ...), custom_call_target="tpu_custom_call" | custom-call | flops 1000000000 | bytes 6000000 | tf_op jit(solution)/shard_map/pallas_call | solution.py:374
  60.2 3.6 %all-to-all-start.2 = ((bf16[8,224,256]{2,1,0:T(8,128)(2,1)}), bf16[8,224,256]{2,1,0:T(8,128)(2,1)S(1)}, u32[]{:S(2)}, u32[]{:S(2)}) async-start(bf16[8,224,256]{2,1,0:T(8,128)(2,1)} %shard_map.72), calls=%async_computation.2 | async-start | bytes 1835008 | tf_op jit(solution)/shard_map/all_to_all | solution.py:395
  63.8 0.0 collective-permute-done.3
  63.8 1.2 %add_multiply_fusion = f32[27,32,256]{2,1,0:T(8,128)S(1)} fusion(bf16[27,32,256]{2,1,0:T(8,128)(2,1)} %collective-permute-done.3, bf16[27,32,256]{2,1,0:T(8,128)(2,1)S(1)} %add_convert_fusion), kind=kLoop, calls=%fused_computation.4 | loop fusion | flops 884736 | bytes 1769472 | tf_op jit(solution)/shard_map/mul | solution.py:502
  65.0 0.2 collective-permute-start.4
  65.1 1.1 %shard_map.73 = f32[8,8,8,256]{3,2,1,0:T(8,128)} custom-call(bf16[8,128,128]{2,1,0:T(8,128)(2,1)S(1)} %all-to-all-done.1.got_ref), custom_call_target="tpu_custom_call" | custom-call | flops 1000000 | bytes 2000000 | tf_op jit(solution)/shard_map/pallas_call | solution.py:274
  66.2 1.3 %collective-permute-done.4 = f32[27,32,256]{2,1,0:T(8,128)} collective-permute-done((f32[27,32,256]{2,1,0:T(8,128)S(1)}, f32[27,32,256]{2,1,0:T(8,128)}, u32[]{:S(2)}, u32[]{:S(2)}) %collective-permute-start.4) | collective-permute-done | bytes 884768 | tf_op jit(solution)/shard_map/ppermute | solution.py:391
  67.6 1.5 %broadcast_select_fusion.1 = (f32[27,32,256]{2,1,0:T(8,128)S(1)}, f32[27,32,256]{2,1,0:T(8,128)S(1)}) fusion(f32[27,32,256]{2,1,0:T(8,128)} %collective-permute-done.4, pred[]{:T(512)S(6)} %eq.8, bf16[27,32,256]{2,1,0:T(8,128)(2,1)} %collective-permute-done.3, bf16[27,32,256]{2,1,0:T(8,128)(2,1)S(1)} %add_convert_fusion), kind=kLoop, calls=%fused_computation.11 | loop fusion | flops 1327104 | bytes 3538945 | tf_op jit(solution)/shard_map/jit(_where)/select_n | solution.py:504
  69.1 1.3 %pad_maximum_fusion = f32[27,64,256]{2,1,0:T(8,128)} fusion(f32[27,32,256]{2,1,0:T(8,128)S(1)} %get-tuple-element.26, f32[27,32,256]{2,1,0:T(8,128)S(1)} %get-tuple-element.25), kind=kLoop, calls=%fused_computation.2 | loop fusion | flops 442368 | bytes 3538944 | tf_op jit(solution)/shard_map/concatenate | solution.py:506
  70.4 16.8 %all-to-all-done.2 = bf16[8,224,256]{2,1,0:T(8,128)(2,1)S(1)} async-done(((bf16[8,224,256]{2,1,0:T(8,128)(2,1)}), bf16[8,224,256]{2,1,0:T(8,128)(2,1)S(1)}, u32[]{:S(2)}, u32[]{:S(2)}) %all-to-all-start.2) | async-done | bytes 917536 | tf_op jit(solution)/shard_map/all_to_all | solution.py:395
  87.2 0.1 reduce_sum.21
  87.4 6.8 %all-gather = bf16[896,256]{1,0:T(8,128)(2,1)S(1)} all-gather(bf16[224,256]{1,0:T(8,128)(2,1)S(1)} %reduce_sum.21), channel_id=2, replica_groups=mesh['sample'=4,'chan'=8] {'sample'}, dimensions={0}, use_global_device_ids=true | all-gather | bytes 573440 | tf_op jit(solution)/shard_map/all_gather | solution.py:551
  94.2 0.1 convert_reduce_fusion
  94.2 0.8 slice_multiply_fusion
Async XLA Ops:
  0.6 14.6 %copy-start = (bf16[1,64,8,8,256]{4,3,2,1,0:T(8,128)(2,1)S(1)}, bf16[1,64,8,8,256]{4,3,2,1,0:T(8,128)(2,1)}, u32[]{:S(2)}) copy-start(bf16[1,64,8,8,256]{4,3,2,1,0:T(8,128)(2,1)} %param.4) | copy-start | bytes 6291460
  3.0 12.7 %copy-start.2 = (bf16[1,32,4,4,64]{4,3,2,1,0:T(4,128)(2,1)S(1)}, bf16[1,32,4,4,64]{4,3,2,1,0:T(4,128)(2,1)}, u32[]{:S(2)}) copy-start(bf16[1,32,4,4,64]{4,3,2,1,0:T(4,128)(2,1)} %param.5) | copy-start | bytes 196612
  3.0 31.9 %all-to-all-start = ((bf16[8,480,128]{2,1,0:T(8,128)(2,1)}), bf16[8,480,128]{2,1,0:T(8,128)(2,1)}, u32[]{:S(2)}, u32[]{:S(2)}) async-start(bf16[8,480,128]{2,1,0:T(8,128)(2,1)} %shard_map.67), calls=%async_computation | async-start | bytes 1966080 | tf_op jit(solution)/shard_map/all_to_all | solution.py:395
  11.3 16.6 %collective-permute-start = (bf16[1,1,16,16,128]{4,3,2,1,0:T(8,128)(2,1)S(1)}, bf16[1,1,16,16,128]{4,3,2,1,0:T(8,128)(2,1)S(1)}, u32[]{:S(2)}, u32[]{:S(2)}) collective-permute-start(bf16[1,1,16,16,128]{4,3,2,1,0:T(8,128)(2,1)S(1)} %slice.6), channel_id=1, source_target_pairs={{0,1},{1,2},{2,3},{3,4},{4,5},{5,6},{6,7},{8,9},{9,10},{10,11},{11... | collective-permute-start | bytes 196616 | tf_op jit(solution)/shard_map/ppermute | solution.py:525
  26.1 1.9 %copy-start.1 = (bf16[1,16,16,16,128]{4,3,2,1,0:T(8,128)(2,1)S(1)}, bf16[1,16,16,16,128]{4,3,2,1,0:T(8,128)(2,1)}, u32[]{:S(2)}) copy-start(bf16[1,16,16,16,128]{4,3,2,1,0:T(8,128)(2,1)} %param.7) | copy-start | bytes 3145732
  34.9 2.8 %collective-permute-start.1 = (bf16[8,480,128]{2,1,0:T(8,128)(2,1)}, bf16[8,480,128]{2,1,0:T(8,128)(2,1)S(1)}, u32[]{:S(2)}, u32[]{:S(2)}) collective-permute-start(bf16[8,480,128]{2,1,0:T(8,128)(2,1)} %all-to-all-done.got_ref), channel_id=1, source_target_pairs={{0,8},{8,0},{16,24},{24,16},{1,9},{9,1},{17,25},{25,17},{2,10},{10... | collective-permute-start | bytes 2949128 | tf_op jit(solution)/shard_map/ppermute | solution.py:391
  39.7 16.2 %collective-permute-start.6 = (bf16[9,2,9,64,128]{4,3,2,1,0:T(8,128)(2,1)S(1)}, bf16[9,2,9,64,128]{4,3,2,1,0:T(8,128)(2,1)}, u32[]{:S(2)}, u32[]{:S(2)}) collective-permute-start(bf16[9,2,9,64,128]{4,3,2,1,0:T(8,128)(2,1)S(1)} %shard_map.69.own_window), channel_id=1, source_target_pairs={{0,8},{8,0},{16,24},{24,16},{1,9},{9,1},{17,25},{25,17},{2,10},{10... | collective-permute-start | bytes 7962632 | tf_op jit(solution)/shard_map/ppermute | solution.py:391
  39.8 5.6 %collective-permute-start.2 = (bf16[27,32,256]{2,1,0:T(8,128)(2,1)}, bf16[27,32,256]{2,1,0:T(8,128)(2,1)}, u32[]{:S(2)}, u32[]{:S(2)}) collective-permute-start(bf16[27,32,256]{2,1,0:T(8,128)(2,1)} %fusion.2), channel_id=1, source_target_pairs={{0,8},{8,0},{16,24},{24,16},{1,9},{9,1},{17,25},{25,17},{2,10},{10... | collective-permute-start | bytes 1327112 | tf_op jit(solution)/shard_map/ppermute | solution.py:391
  40.2 14.1 %all-to-all-start.1 = ((bf16[8,128,128]{2,1,0:T(8,128)(2,1)}), bf16[8,128,128]{2,1,0:T(8,128)(2,1)S(1)}, u32[]{:S(2)}, u32[]{:S(2)}) async-start(bf16[8,128,128]{2,1,0:T(8,128)(2,1)} %shard_map.71), calls=%async_computation.1 | async-start | bytes 524288 | tf_op jit(solution)/shard_map/all_to_all | solution.py:395
  46.8 17.0 %collective-permute-start.3 = (bf16[27,32,256]{2,1,0:T(8,128)(2,1)S(1)}, bf16[27,32,256]{2,1,0:T(8,128)(2,1)}, u32[]{:S(2)}, u32[]{:S(2)}) collective-permute-start(bf16[27,32,256]{2,1,0:T(8,128)(2,1)S(1)} %add_convert_fusion), channel_id=1, source_target_pairs={{0,16},{8,24},{16,0},{24,8},{1,17},{9,25},{17,1},{25,9},{2,18},{10... | collective-permute-start | bytes 1327112 | tf_op jit(solution)/shard_map/ppermute | solution.py:501
  54.3 1.5 %collective-permute-start.5 = (bf16[8,128,128]{2,1,0:T(8,128)(2,1)S(1)}, bf16[8,128,128]{2,1,0:T(8,128)(2,1)S(1)}, u32[]{:S(2)}, u32[]{:S(2)}) collective-permute-start(bf16[8,128,128]{2,1,0:T(8,128)(2,1)S(1)} %all-to-all-done.1.got_ref), channel_id=1, source_target_pairs={{0,8},{8,0},{16,24},{24,16},{1,9},{9,1},{17,25},{25,17},{2,10},{10... | collective-permute-start | bytes 786440 | tf_op jit(solution)/shard_map/ppermute | solution.py:391
  60.2 27.0 %all-to-all-start.2 = ((bf16[8,224,256]{2,1,0:T(8,128)(2,1)}), bf16[8,224,256]{2,1,0:T(8,128)(2,1)S(1)}, u32[]{:S(2)}, u32[]{:S(2)}) async-start(bf16[8,224,256]{2,1,0:T(8,128)(2,1)} %shard_map.72), calls=%async_computation.2 | async-start | bytes 1835008 | tf_op jit(solution)/shard_map/all_to_all | solution.py:395
  65.0 2.6 %collective-permute-start.4 = (f32[27,32,256]{2,1,0:T(8,128)S(1)}, f32[27,32,256]{2,1,0:T(8,128)}, u32[]{:S(2)}, u32[]{:S(2)}) collective-permute-start(f32[27,32,256]{2,1,0:T(8,128)S(1)} %add_multiply_fusion), channel_id=1, source_target_pairs={{0,8},{8,0},{16,24},{24,16},{1,9},{9,1},{17,25},{25,17},{2,10},{10... | collective-permute-start | bytes 2654216 | tf_op jit(solution)/shard_map/ppermute | solution.py:391

commit v2 on v1

--- a/solution.py
+++ b/solution.py
@@ -11,7 +11,7 @@
 leak_slope = 0.3
 low = jnp.bfloat16
 wide = jnp.float32
-params = pltpu.CompilerParams(vmem_limit_bytes=40 * 2**20)
+params = pltpu.CompilerParams(vmem_limit_bytes=20 * 2**20)
 whole = pl.BlockSpec(memory_space=pltpu.VMEM)
 scalar = pl.BlockSpec(memory_space=pltpu.SMEM)
 anywhere = pl.BlockSpec(memory_space=pltpu.HBM)
@@ -281,39 +281,45 @@
     )(got)
 
 
-def window_kernel(rim_ref, volume_ref, window_ref, grid):
-    planes, rows, columns, channels = grid.shape
-    grid[0] = rim_ref[0].astype(wide)
-    grid[pl.ds(1, planes - 1)] = volume_ref[...].astype(wide)
-    flat = grid.reshape(planes * rows * columns, channels)
+def tap_cells(flat, planes, rows, columns):
+    channels = flat.shape[1]
     half = columns // 2
     count = planes * rows * half
     first = lax.broadcasted_iota(jnp.int32, (count, channels), 0) % half == 0
     even = flat[pl.ds(0, count, stride=2), :]
     odd = flat[pl.ds(1, count, stride=2), :]
     before = jnp.where(first, 0.0, pltpu.roll(odd, 1, 0))
-    for col, part in enumerate((before, even, odd)):
+    cells = []
+    for part in (before, even, odd):
         part = part.reshape(planes, rows // 2, 2, half, channels)
         on_even, on_odd = part[:, :, 0], part[:, :, 1]
         ahead = jnp.concatenate([jnp.zeros_like(on_odd[:, :1]), on_odd[:, :-1]], axis=1)
-        for row, taken in enumerate((ahead, on_even, on_odd)):
-            taken = taken.reshape(planes, rows // 2 * half, channels).astype(low)
-            for plane in range(planes):
-                window_ref[col * 3 + row, plane % 2, plane // 2] = taken[plane]
-
-
-def windows(rim, volume):
+        for taken in (ahead, on_even, on_odd):
+            cells.append(taken.reshape(planes, rows // 2 * half, channels).astype(low))
+    return cells
+
+
+def window_kernel(volume_ref, window_ref, done_ref, flat):
+    done_ref[...] = jnp.zeros_like(done_ref)
+    planes, rows, columns, _ = volume_ref.shape
+    flat[...] = volume_ref[...].astype(wide).reshape(flat.shape)
+    for n, taken in enumerate(tap_cells(flat, planes, rows, columns)):
+        for plane in range(planes):
+            window_ref[n, plane % 2, plane // 2] = taken[plane]
+
+
+def windows(volume):
     planes, rows, columns, channels = volume.shape
-    shape = (9, 2, planes // 2 + 1, rows * columns // 4, channels)
+    shape = (9, 2, planes // 2, rows * columns // 4, channels)
     return pl.pallas_call(
         window_kernel,
-        out_shape=jax.ShapeDtypeStruct(shape, low),
-        in_specs=[whole, whole],
-        out_specs=whole,
-        scratch_shapes=[pltpu.VMEM((planes + 1, rows, columns, channels), wide)],
+        out_shape=(jax.ShapeDtypeStruct(shape, low), jax.ShapeDtypeStruct((8, 128), wide)),
+        in_specs=[whole],
+        out_specs=(whole, whole),
+        scratch_shapes=[pltpu.VMEM((planes * rows * columns, channels), wide)],
         compiler_params=params,
         cost_estimate=pl.CostEstimate(flops=10**6, bytes_accessed=4 * 10**6, transcendentals=0),
-    )(rim, volume)
+    )(volume)
 
 
 def lanes_joined(blocks, slot, slots):
@@ -323,38 +329,85 @@
     return joined
 
 
-def lower_kernel(core_ref, got_ref, other_ref, own_window, other_window, sent_ref, cells, staged, left):
-    shards, rows, _ = got_ref.shape
+def cotangent_side(source_ref, cells):
+    shards, rows, _ = source_ref.shape
     planes, height, columns, middle = cells.shape
-    count = staged.shape[1] // (own_window.shape[4] // shards)
     slots = lane_slot((rows, 128))
-    sides = []
-    for source in (got_ref, other_ref):
-        for tile in range(shards // 4):
-            turned = []
-            for m in range(4):
-                block = source[tile * 4 + m].astype(wide)
-                turned.append([block] + [pltpu.roll(block, 32 * r, 1) for r in range(1, 4)])
-            for slot in range(4):
-                joined = lanes_joined(turned, slot, slots).reshape(planes // 2, height // 2, columns, 128)
-                for z in range(planes // 2):
-                    for y in range(height // 2):
-                        cells[2 * z + slot // 2, 2 * y + slot % 2, :, pl.ds(tile * 128, 128)] = joined[z, y]
-        sides.append(cells[...].reshape(planes * height * columns, middle).T.astype(low))
-    below = own_window.shape[4]
+    for tile in range(shards // 4):
+        turned = []
+        for m in range(4):
+            block = source_ref[tile * 4 + m].astype(wide)
+            turned.append([block] + [pltpu.roll(block, 32 * r, 1) for r in range(1, 4)])
+        for slot in range(4):
+            joined = lanes_joined(turned, slot, slots).reshape(planes // 2, height // 2, columns, 128)
+            for z in range(planes // 2):
+                for y in range(height // 2):
+                    cells[2 * z + slot // 2, 2 * y + slot % 2, :, pl.ds(tile * 128, 128)] = joined[z, y]
+    return cells[...].reshape(planes * height * columns, middle).T.astype(low)
+
+
+def rim_cells(rim_ref, flat, first_cells):
+    _, rows, columns, _ = rim_ref.shape
+    flat[...] = rim_ref[...].astype(wide).reshape(flat.shape)
+    for n, taken in enumerate(tap_cells(flat, 1, rows, columns)):
+        first_cells[n] = taken[0]
+
+
+def tap_pair(window, first_cells, start):
+    planes = window.shape[2]
+    both = []
+    for n in range(2):
+        tap = jnp.minimum(start + n, 26)
+        depth, row, col = tap // 9, tap // 3 % 3, tap % 3
+        which, parity = col * 3 + row, (depth + 1) % 2
+        lowest = jnp.where(depth == 0, first_cells[which], window[which, parity, 0])
+        below = jnp.where(depth == 0, 0, 1)
+        rest = window[which, parity, pl.ds(below, planes - 1)]
+        both.append(jnp.concatenate([lowest, rest.reshape(-1, window.shape[4])], axis=0))
+    return jnp.concatenate(both, axis=1)
+
+
+def lower_first_kernel(core_ref, got_ref, window, rim_ref, done_ref, total_ref, cells, flat, first_cells):
+    del done_ref
+    rim_cells(rim_ref, flat, first_cells)
+    side = cotangent_side(got_ref, cells)
+    count = total_ref.shape[0]
+    for pair in range(count):
+        taps = tap_pair(window, first_cells, (core_ref[0] * count + pair) * 2)
+        total_ref[pair] = jnp.dot(side, taps, preferred_element_type=wide)
+
+
+def lower_scratch(grid, middle, window, rim):
+    return [
+        pltpu.VMEM((*grid, middle), wide),
+        pltpu.VMEM((math.prod(rim.shape[:3]), rim.shape[3]), wide),
+        pltpu.VMEM((9, *window.shape[3:]), low),
+    ]
+
+
+def lower_first(core, got, window, rim, done, grid):
+    middle = 32 * got.shape[0]
+    return pl.pallas_call(
+        lower_first_kernel,
+        out_shape=jax.ShapeDtypeStruct((7, middle, 2 * window.shape[4]), wide),
+        in_specs=[scalar, whole, whole, whole, whole],
+        out_specs=whole,
+        scratch_shapes=lower_scratch(grid, middle, window, rim),
+        compiler_params=params,
+        cost_estimate=pl.CostEstimate(flops=5 * 10**8, bytes_accessed=5 * 10**6, transcendentals=0),
+    )(core, got, window, rim, done)
+
+
+def lower_kernel(core_ref, total_ref, other_ref, window, rim_ref, sent_ref, cells, flat, first_cells, staged, left):
+    rim_cells(rim_ref, flat, first_cells)
+    side = cotangent_side(other_ref, cells)
+    shards = staged.shape[0]
+    below = window.shape[4]
     share = below // shards
     copies = []
-    for pair in range(count // 2):
-        total = None
-        for side, window in zip(sides, (own_window, other_window), strict=True):
-            both = []
-            for n in range(2):
-                tap = jnp.minimum(core_ref[0] * count + 2 * pair + n, 26)
-                depth, row, col = tap // 9, tap // 3 % 3, tap % 3
-                taken = window[col * 3 + row, depth % 2, pl.ds(depth // 2, planes)]
-                both.append(taken.reshape(planes * height * columns, below))
-            term = jnp.dot(side, jnp.concatenate(both, axis=1), preferred_element_type=wide)
-            total = term if total is None else total + term
+    for pair in range(total_ref.shape[0]):
+        taps = tap_pair(window, first_cells, (core_ref[0] * total_ref.shape[0] + pair) * 2)
+        total = total_ref[pair] + jnp.dot(side, taps, preferred_element_type=wide)
         total = total.T.astype(low)
         for n in range(2):
             for d in range(shards):
@@ -367,23 +420,78 @@
         copy.wait()
 
 
-def lower_terms(core, got, other, own_window, other_window, grid):
-    shards = got.shape[0]
-    below = own_window.shape[4]
-    middle = 32 * shards
+def lower_terms(core, total, other, window, rim, grid):
+    shards = other.shape[0]
+    pairs, middle, lanes = total.shape
+    shape = (shards, pairs * lanes // shards, middle)
     return pl.pallas_call(
         lower_kernel,
-        out_shape=pltpu.HBM((shards, 14 * below // shards, middle), low),
+        out_shape=pltpu.HBM(shape, low),
         in_specs=[scalar, whole, whole, whole, whole],
         out_specs=anywhere,
+        scratch_shapes=lower_scratch(grid, middle, window, rim)
+        + [pltpu.VMEM(shape, low), pltpu.SemaphoreType.DMA((pairs,))],
+        compiler_params=params,
+        cost_estimate=pl.CostEstimate(flops=5 * 10**8, bytes_accessed=5 * 10**6, transcendentals=0),
+    )(core, total, other, window, rim)
+
+
+def upper_kernel(core_ref, volume_ref, cot_ref, mine_ref, theirs_ref, flat, cot_flat, lined, left):
+    planes, rows, columns, channels = volume_ref.shape
+    depth, height, width, outs = cot_ref.shape
+    half = outs // 2
+    tiles = channels // 128
+    for tile in range(tiles):
+        lanes = pl.ds(tile * 128, 128)
+        flat[tile] = volume_ref[:, :, :, lanes].astype(wide).reshape(flat.shape[1:])
+    cot_wide = cot_ref[...].astype(wide).reshape(cot_flat.shape[0], outs)
+    cot_flat[...] = jnp.concatenate([cot_wide, jnp.zeros((cot_flat.shape[0], 128 - outs), wide)], axis=1)
+    pieces = [cot_flat[pl.ds(n, depth, stride=height * width), :] for n in range(height * width)]
+    left[...] = jnp.concatenate(pieces, axis=0).T[:outs].astype(low)
+    core = core_ref[0]
+    split = [left[pl.ds(pl.multiple_of(at * half, half), half), :] for at in (core, 1 - core)]
+    side = jnp.concatenate(split, axis=0)
+    first = lax.broadcasted_iota(jnp.int32, (depth, 128), 0) == 0
+    stride = 2 * rows * columns
+    for row in range(rows):
+        for col in range(columns):
+            for tile in range(tiles):
+                even = flat[tile, pl.ds(row * columns + col, depth, stride=stride), :]
+                odd = flat[tile, pl.ds(stride // 2 + row * columns + col, depth, stride=stride), :]
+                before = jnp.where(first, 0.0, pltpu.roll(odd, 1, 0))
+                for depth_tap, part in enumerate((before, even, odd)):
+                    lined[depth_tap, row, col, :, pl.ds(tile * 128, 128)] = part.astype(low)
+    nothing = jnp.zeros((depth, channels), low)
+    for tap in range(27):
+        depth_tap, row_tap, col_tap = tap // 9, tap // 3 % 3, tap % 3
+        taken = []
+        for y in range(height):
+            for x in range(width):
+                row, col = 2 * y + row_tap - 1, 2 * x + col_tap - 1
+                taken.append(nothing if row < 0 or col < 0 else lined[depth_tap, row, col])
+        term = jnp.dot(side, jnp.concatenate(taken, axis=0), preferred_element_type=wide)
+        mine_ref[tap] = term[:half]
+        theirs_ref[tap] = term[half:].astype(low)
+
+
+def upper_terms(core, volume, cot):
+    planes, rows, columns, channels = volume.shape
+    depth, height, width, outs = cot.shape
+    shape = (27, outs // 2, channels)
+    return pl.pallas_call(
+        upper_kernel,
+        out_shape=(jax.ShapeDtypeStruct(shape, wide), jax.ShapeDtypeStruct(shape, low)),
+        in_specs=[scalar, whole, whole],
+        out_specs=(whole, whole),
         scratch_shapes=[
-            pltpu.VMEM((*grid, middle), wide),
-            pltpu.VMEM((shards, 14 * below // shards, middle), low),
-            pltpu.SemaphoreType.DMA((7,)),
+            pltpu.VMEM((channels // 128, planes * rows * columns, 128), wide),
+            pltpu.VMEM((depth * height * width, 128), wide),
+            pltpu.VMEM((3, rows, columns, depth, channels), low),
+            pltpu.VMEM((outs, depth * height * width), low),
         ],
         compiler_params=params,
-        cost_estimate=pl.CostEstimate(flops=10**9, bytes_accessed=6 * 10**6, transcendentals=0),
-    )(core, got, other, own_window, other_window)
+        cost_estimate=pl.CostEstimate(flops=5 * 10**8, bytes_accessed=6 * 10**6, transcendentals=0),
+    )(core, volume, cot)
 
 
 def partner(array, axis, by):
@@ -484,17 +592,12 @@
     )
 
 
-def core_halves(terms):
+def core_sum(mine, theirs):
+    return (mine + partner(theirs, "sample", 1).astype(wide)).astype(low)
+
+
+def sample_sum(mine, samples):
     core = lax.axis_index("sample") % 2
-    blocks = terms.reshape(27, 2, -1, terms.shape[2])
-    mine = lax.dynamic_index_in_dim(blocks, core, 1, keepdims=False)
-    theirs = lax.dynamic_index_in_dim(blocks, 1 - core, 1, keepdims=False)
-    return mine, theirs.astype(low)
-
-
-def sample_sum(mine, theirs, samples):
-    core = lax.axis_index("sample") % 2
-    mine = (mine + partner(theirs, "sample", 1).astype(wide)).astype(low)
     total = mine.astype(wide)
     for by in range(2, samples, 2):
         pairs = [(i, (i + by) % samples) for i in range(samples)]
@@ -528,24 +631,28 @@
     got = exchange(sent, "chan")
 
     own = own_signs(position, volume_64)
-    window = windows(rim[0], act_128[0])
-    grad_upper = filter_gradient(volume_64, cot_local, ((1, 0),) * 3)
-    grad_upper = grad_upper.transpose(0, 1, 2, 4, 3).reshape(27, shard_out, middle)
-    halves = core_halves(grad_upper)
-    got, own, window, halves = lax.optimization_barrier((got, own, window, halves))
+    other_act = partner(act_128, "sample", 1)
+    halves = upper_terms(cores, volume_64, cot_local)
+    window, done = windows(act_128[0])
+    other_window, other_done = windows(other_act[0])
+    done = done + other_done
+    got, own, rim, done, halves = lax.optimization_barrier((got, own, rim, done, halves))
     other = partner(got, "sample", 1)
     first, later = first_terms(cores, got, math.prod(grid))
     cot_sent = spread(first, later, other, own, grid)
 
-    cot_sent, window, halves = lax.optimization_barrier((cot_sent, window, halves))
+    cot_sent, rim, halves = lax.optimization_barrier((cot_sent, rim, halves))
     cot_got = exchange(cot_sent, "chan")
-    other_window = partner(window, "sample", 1)
-    total_upper = sample_sum(*halves, samples).reshape(3, 3, 3, shard_out, middle)
+    chip_upper = core_sum(*halves)
+    chip_upper, rim = lax.optimization_barrier((chip_upper, rim))
+    other_rim = partner(rim, "sample", 1)
+    total_upper = sample_sum(chip_upper, samples).reshape(3, 3, 3, shard_out, middle)
     total_upper = total_upper.transpose(0, 1, 2, 4, 3)
 
     other_cot = partner(cot_got, "sample", 1)
     slab_grid = (slab, *volume_64.shape[1:3])
-    terms = lower_terms(cores, cot_got, other_cot, window, other_window, slab_grid)
+    own_terms = lower_first(cores, cot_got, window, rim[0], done, slab_grid)
+    terms = lower_terms(cores, own_terms, other_cot, other_window, other_rim[0], slab_grid)
     share = jnp.sum(exchange(terms, "chan").astype(wide), axis=0)
     cot_full = unpack(cot_got, slab_grid)
     shares = lax.all_gather(share.astype(low), "sample", axis=0).astype(wide)

time: 95.6 us -> 92.1 us (0.963)
  matrix products: 10.4 us -> 0 us
  local copies, waits for them, and re-layouts: 2.69 us -> 7.82 us
  Pallas kernels: 12.8 us -> 16.4 us
  waiting for transfers between devices: 33.1 us -> 31.9 us
    transpose x1 -> x0, matrix products: 10.4 us -> none  [body(): grad_upper.transpose(0, 1, 2, 4, 3).reshape(27, shard_out, middle)]
    unnamed x6 -> x20, local copies, waits for them, and re-layouts: 0.02 us -> 6.35 us
    pallas_call x2 -> x5, Pallas kernels: 5.21 us -> 10.3 us  [the longest x1 4.83 us: upper_terms(): pl.pallas_call(upper_kernel, out_shape=(jax.ShapeDtypeStruct(shape, wide)...]
    pallas_call x1, Pallas kernels: 1.77 us -> 0.57 us  [first_terms(): pl.pallas_call(first_kernel, out_shape=(jax.ShapeDtypeStruct((cells, lane...]
    squeeze x1 -> x0, local copies, waits for them, and re-layouts: 1.01 us -> none  [core_halves(): mine = lax.dynamic_index_in_dim(blocks, core, 1, keepdims=False)]
    ppermute x5 -> x6, waiting for transfers between devices: 4.18 us -> 3.6 us  [partner(): return lax.ppermute(array, axis, [(i, i ^ by) for i in range(size)])]
  transfers between devices with their start and end apart: 10 -> 11, of which waited for: 7 -> 6; matrix products, arithmetic and copies ran while one was open for 19% -> 8% of each run, Pallas kernels for 9% -> 14%
where the time goes in v2:
time: 92.1 us; the launch traced here: 91.4 us
  waiting for transfers between devices  31.9 us (35%)
  starting transfers between devices  21.3 us (23%)
  Pallas kernels  16.4 us (18%)
  local copies, waits for them, and re-layouts  7.82 us (8%)
  blocking collectives  6.82 us (7%)
  other arithmetic  6.37 us (7%)
    all_to_all x3, waiting for transfers between devices, exchange(): return lax.all_to_all(blocks, axis, split_axis=0, concat_axis=0, tiled=True)  28.3 us
    all_to_all x3, starting transfers between devices, exchange(): return lax.all_to_all(blocks, axis, split_axis=0, concat_axis=0, tiled=True)  15.1 us
    all_gather x1, blocking collectives, body(): shares = lax.all_gather(share.astype(low), 'sample', axis=0).astype(wide)  6.82 us
    unnamed x20, local copies, waits for them, and re-layouts  6.35 us
    pallas_call x1, Pallas kernels, upper_terms(): pl.pallas_call(upper_kernel, out_shape=(jax.ShapeDtypeStruct(shape, wide)...  4.83 us
    ppermute x1, starting transfers between devices, body(): lax.ppermute(act_128[:, -1:], 'chan', [(i, i + 1) for i in range(shards -...  3.9 us
    ppermute x6, waiting for transfers between devices, partner(): return lax.ppermute(array, axis, [(i, i ^ by) for i in range(size)])  3.6 us
    pallas_call x2, Pallas kernels, windows(): pl.pallas_call(window_kernel, out_shape=(jax.ShapeDtypeStruct(shape, low)...  2.77 us
  transfers between devices with their start and end apart: 11, of which 6 were waited for; matrix products, arithmetic and copies ran while one was open for 8% of the time, Pallas kernels for 14%

profile of v2, /device:TPU:0, one launch (start us, length us, event | category | flops | bytes accessed | tf_op | source)
XLA Modules:
  0.0 91.4 jit_solution(11895116022592763706)
XLA Ops:
  0.6 0.0 copy-start.7
  0.7 2.2 %shard_map.67 = bf16[8,480,128]{2,1,0:T(8,128)(2,1)} custom-call(s32[1]{0:T(128)} %bitcast.core_ref, bf16[27,64,256]{2,1,0:T(8,128)(2,1)} %bitcast.29, bf16[512,64]{1,0:T(8,128)(2,1)} %bitcast.23), custom_call_target="tpu_custom_call" | custom-call | flops 1000000 | bytes 3000000 | tf_op jit(solution)/shard_map/pallas_call | solution.py:88
  2.9 0.0 copy-start
  2.9 7.4 %all-to-all-start = ((bf16[8,480,128]{2,1,0:T(8,128)(2,1)}), bf16[8,480,128]{2,1,0:T(8,128)(2,1)S(1)}, u32[]{:S(2)}, u32[]{:S(2)}) async-start(bf16[8,480,128]{2,1,0:T(8,128)(2,1)} %shard_map.67), calls=%async_computation | async-start | bytes 1966080 | tf_op jit(solution)/shard_map/all_to_all | solution.py:503
  10.3 0.0 collective-permute-start.1
  10.4 1.5 %slice.6 = bf16[1,1,16,16,128]{4,3,2,1,0:T(8,128)(2,1)} slice(bf16[1,16,16,16,128]{4,3,2,1,0:T(8,128)(2,1)} %param.7), slice={[0:1], [15:16], [0:16], [0:16], [0:128]} | slice | bytes 131072 | tf_op jit(solution)/shard_map/slice | solution.py:628
  11.8 3.9 %collective-permute-start = (bf16[1,1,16,16,128]{4,3,2,1,0:T(8,128)(2,1)}, bf16[1,1,16,16,128]{4,3,2,1,0:T(8,128)(2,1)S(1)}, u32[]{:S(2)}, u32[]{:S(2)}) collective-permute-start(bf16[1,1,16,16,128]{4,3,2,1,0:T(8,128)(2,1)} %slice.6), channel_id=1, source_target_pairs={{0,1},{1,2},{2,3},{3,4},{4,5},{5,6},{6,7},{8,9},{9,10},{10,11},{11... | collective-permute-start | bytes 196616 | tf_op jit(solution)/shard_map/ppermute | solution.py:628
  15.7 0.0 copy-start.5
  15.8 1.2 %copy-done.5 = bf16[1,16,16,16,128]{4,3,2,1,0:T(8,128)(2,1)S(1)} copy-done((bf16[1,16,16,16,128]{4,3,2,1,0:T(8,128)(2,1)S(1)}, bf16[1,16,16,16,128]{4,3,2,1,0:T(8,128)(2,1)}, u32[]{:S(2)}) %copy-start.5) | copy-done | bytes 1048600
  17.0 0.8 shard_map.69
  17.7 0.0 copy-start.1
  17.8 1.4 %copy-done.1 = bf16[9,2,8,64,128]{4,3,2,1,0:T(8,128)(2,1)} copy-done((bf16[9,2,8,64,128]{4,3,2,1,0:T(8,128)(2,1)}, bf16[9,2,8,64,128]{4,3,2,1,0:T(8,128)(2,1)S(1)}, u32[]{:S(2)}) %copy-start.1) | copy-done | bytes 2359320
  19.2 0.0 copy-done
  19.2 0.4 shard_map.68.own_ref
  19.6 0.0 copy-done.7
  19.6 4.8 %shard_map.71 = (f32[27,32,256]{2,1,0:T(8,128)S(1)}, bf16[27,32,256]{2,1,0:T(8,128)(2,1)S(1)}) custom-call(s32[1]{0:T(128)} %bitcast.core_ref, bf16[64,8,8,256]{3,2,1,0:T(8,128)(2,1)S(1)} %bitcast.21, bf16[32,4,4,64]{3,2,1,0:T(4,128)(2,1)S(1)} %bitcast.24), custom_call_target="tpu_custom_call" | custom-call | flops 500000000 | bytes 6000000 | tf_op jit(solution)/shard_map/pallas_call | solution.py:481
  24.4 0.0 copy-start.8
  24.4 0.8 copy-done.8
  25.2 0.0 copy-start.6
  25.2 0.0 collective-permute-done.1
  25.2 0.9 %copy-done.6 = f32[27,32,256]{2,1,0:T(8,128)} copy-done((f32[27,32,256]{2,1,0:T(8,128)}, f32[27,32,256]{2,1,0:T(8,128)S(1)}, u32[]{:S(2)}) %copy-start.6) | copy-done | bytes 884760
  26.1 2.0 %shard_map.70 = (bf16[9,2,8,64,128]{4,3,2,1,0:T(8,128)(2,1)S(1)}, f32[8,128]{1,0:T(8,128)S(1)}) custom-call(bf16[16,16,16,128]{3,2,1,0:T(8,128)(2,1)} %bitcast.7.volume_ref), custom_call_target="tpu_custom_call" | custom-call | flops 1000000 | bytes 4000000 | tf_op jit(solution)/shard_map/pallas_call | solution.py:314
  28.1 0.0 copy-start.3
  28.2 1.4 %copy-done.3 = bf16[9,2,8,64,128]{4,3,2,1,0:T(8,128)(2,1)} copy-done((bf16[9,2,8,64,128]{4,3,2,1,0:T(8,128)(2,1)}, bf16[9,2,8,64,128]{4,3,2,1,0:T(8,128)(2,1)S(1)}, u32[]{:S(2)}) %copy-start.3) | copy-done | bytes 2359320
  29.6 0.0 collective-permute-done
  29.6 5.1 %all-to-all-done.got_ref = bf16[8,480,128]{2,1,0:T(8,128)(2,1)S(1)} async-done(((bf16[8,480,128]{2,1,0:T(8,128)(2,1)}), bf16[8,480,128]{2,1,0:T(8,128)(2,1)S(1)}, u32[]{:S(2)}, u32[]{:S(2)}) %all-to-all-start) | async-done | bytes 983072 | tf_op jit(solution)/shard_map/all_to_all | solution.py:503
  34.7 0.0 collective-permute-start.2
  34.7 0.6 shard_map.72
  35.3 0.0 copy-start.9
  35.3 2.0 %collective-permute-done.2.other_ref = bf16[8,480,128]{2,1,0:T(8,128)(2,1)S(1)} collective-permute-done((bf16[8,480,128]{2,1,0:T(8,128)(2,1)S(1)}, bf16[8,480,128]{2,1,0:T(8,128)(2,1)S(1)}, u32[]{:S(2)}, u32[]{:S(2)}) %collective-permute-start.2) | collective-permute-done | bytes 983072 | tf_op jit(solution)/shard_map/ppermute | solution.py:499
  37.3 0.0 copy-start.2
  37.3 1.8 %shard_map.73 = bf16[8,128,128]{2,1,0:T(8,128)(2,1)} custom-call(f32[512,896]{1,0:T(8,128)S(1)} %get-tuple-element.28.first_ref, bf16[256,512]{1,0:T(8,128)(2,1)S(1)} %get-tuple-element.29.later_ref, bf16[8,480,128]{2,1,0:T(8,128)(2,1)S(1)} %collective-permute-done.2.other_ref, bf16[1024,128]{1,0:T(8,128)(2,1)S(1)} %shard_map.68.own_ref), custom_call_target="tpu_custom_call" | custom-call | flops 500000000 | bytes 3000000 | tf_op jit(solution)/shard_map/pallas_call | solution.py:235
  39.1 0.0 copy-done.9
  39.1 0.1 collective-permute-start.3
  39.2 4.1 %all-to-all-start.1 = ((bf16[8,128,128]{2,1,0:T(8,128)(2,1)}), bf16[8,128,128]{2,1,0:T(8,128)(2,1)S(1)}, u32[]{:S(2)}, u32[]{:S(2)}) async-start(bf16[8,128,128]{2,1,0:T(8,128)(2,1)} %shard_map.73), calls=%async_computation.1 | async-start | bytes 524288 | tf_op jit(solution)/shard_map/all_to_all | solution.py:503
  43.3 0.0 collective-permute-done.3
  43.3 1.4 %add_convert_fusion = bf16[27,32,256]{2,1,0:T(8,128)(2,1)S(1)} fusion(f32[27,32,256]{2,1,0:T(8,128)} %copy-done.6, bf16[27,32,256]{2,1,0:T(8,128)(2,1)} %collective-permute-done.3), kind=kLoop, calls=%fused_computation.3 | loop fusion | flops 663552 | bytes 1769472 | tf_op jit(solution)/shard_map/convert_element_type | solution.py:596
  44.7 1.6 %collective-permute-start.4 = (bf16[27,32,256]{2,1,0:T(8,128)(2,1)S(1)}, bf16[27,32,256]{2,1,0:T(8,128)(2,1)}, u32[]{:S(2)}, u32[]{:S(2)}) collective-permute-start(bf16[27,32,256]{2,1,0:T(8,128)(2,1)S(1)} %add_convert_fusion), channel_id=1, source_target_pairs={{0,16},{8,24},{16,0},{24,8},{1,17},{9,25},{17,1},{25,9},{2,18},{10... | collective-permute-start | bytes 1327112 | tf_op jit(solution)/shard_map/ppermute | solution.py:604
  46.3 6.5 %all-to-all-done.1.got_ref = bf16[8,128,128]{2,1,0:T(8,128)(2,1)S(1)} async-done(((bf16[8,128,128]{2,1,0:T(8,128)(2,1)}), bf16[8,128,128]{2,1,0:T(8,128)(2,1)S(1)}, u32[]{:S(2)}, u32[]{:S(2)}) %all-to-all-start.1) | async-done | bytes 262176 | tf_op jit(solution)/shard_map/all_to_all | solution.py:503
  52.7 0.0 collective-permute-start.6
  52.7 0.5 collective-permute-start.7
  53.2 0.0 copy-done.2
  53.2 0.0 copy-start.4
  53.2 0.9 %shard_map.74.total_ref = f32[7,256,256]{2,1,0:T(8,128)S(1)} custom-call(s32[1]{0:T(128)} %bitcast.core_ref, bf16[8,128,128]{2,1,0:T(8,128)(2,1)S(1)} %all-to-all-done.1.got_ref, bf16[9,2,8,64,128]{4,3,2,1,0:T(8,128)(2,1)S(1)} %copy-done.2, bf16[1,16,16,128]{3,2,1,0:T(8,128)(2,1)S(1)} %bitcast.25, f32[8,128]{1,0:T(8,128)S(1)} %add.15.done_ref), custom_call_target="tpu_custom_call" | custom-call | flops 500000000 | bytes 5000000 | tf_op jit(solution)/shard_map/pallas_call | solution.py:390
  54.2 0.2 collective-permute-done.7
  54.4 0.0 collective-permute-done.6.other_ref
  54.4 0.5 copy-done.4
  54.9 1.8 %shard_map.75 = bf16[8,224,256]{2,1,0:T(8,128)(2,1)} custom-call(s32[1]{0:T(128)} %bitcast.core_ref, f32[7,256,256]{2,1,0:T(8,128)S(1)} %shard_map.74.total_ref, bf16[8,128,128]{2,1,0:T(8,128)(2,1)S(1)} %collective-permute-done.6.other_ref, bf16[9,2,8,64,128]{4,3,2,1,0:T(8,128)(2,1)S(1)} %copy-done.4, bf16[1,16,16,128]{3,2,1,0:T(8,128)(2,1)S(1)} %bitcast.26), custom_call_target="tpu_custom_call" | custom-call | flops 500000000 | bytes 5000000 | tf_op jit(solution)/shard_map/pallas_call | solution.py:427
  56.7 3.6 %all-to-all-start.2 = ((bf16[8,224,256]{2,1,0:T(8,128)(2,1)}), bf16[8,224,256]{2,1,0:T(8,128)(2,1)S(1)}, u32[]{:S(2)}, u32[]{:S(2)}) async-start(bf16[8,224,256]{2,1,0:T(8,128)(2,1)} %shard_map.75), calls=%async_computation.2 | async-start | bytes 1835008 | tf_op jit(solution)/shard_map/all_to_all | solution.py:503
  60.3 0.0 collective-permute-done.4
  60.3 1.2 %add_multiply_fusion = f32[27,32,256]{2,1,0:T(8,128)S(1)} fusion(bf16[27,32,256]{2,1,0:T(8,128)(2,1)} %collective-permute-done.4, bf16[27,32,256]{2,1,0:T(8,128)(2,1)S(1)} %add_convert_fusion), kind=kLoop, calls=%fused_computation.2 | loop fusion | flops 884736 | bytes 1769472 | tf_op jit(solution)/shard_map/mul | solution.py:605
  61.5 0.1 collective-permute-start.5
  61.6 1.1 %shard_map.76 = f32[8,8,8,256]{3,2,1,0:T(8,128)} custom-call(bf16[8,128,128]{2,1,0:T(8,128)(2,1)S(1)} %all-to-all-done.1.got_ref), custom_call_target="tpu_custom_call" | custom-call | flops 1000000 | bytes 2000000 | tf_op jit(solution)/shard_map/pallas_call | solution.py:274
  62.7 1.4 %collective-permute-done.5 = f32[27,32,256]{2,1,0:T(8,128)} collective-permute-done((f32[27,32,256]{2,1,0:T(8,128)S(1)}, f32[27,32,256]{2,1,0:T(8,128)}, u32[]{:S(2)}, u32[]{:S(2)}) %collective-permute-start.5) | collective-permute-done | bytes 884768 | tf_op jit(solution)/shard_map/ppermute | solution.py:499
  64.1 1.5 %broadcast_select_fusion.1 = (f32[27,32,256]{2,1,0:T(8,128)S(1)}, f32[27,32,256]{2,1,0:T(8,128)S(1)}) fusion(f32[27,32,256]{2,1,0:T(8,128)} %collective-permute-done.5, pred[]{:T(512)S(6)} %eq.7, bf16[27,32,256]{2,1,0:T(8,128)(2,1)} %collective-permute-done.4, bf16[27,32,256]{2,1,0:T(8,128)(2,1)S(1)} %add_convert_fusion), kind=kLoop, calls=%fused_computation.6 | loop fusion | flops 1327104 | bytes 3538945 | tf_op jit(solution)/shard_map/jit(_where)/select_n | solution.py:607
  65.6 1.3 %pad_maximum_fusion = f32[27,64,256]{2,1,0:T(8,128)} fusion(f32[27,32,256]{2,1,0:T(8,128)S(1)} %get-tuple-element.44, f32[27,32,256]{2,1,0:T(8,128)S(1)} %get-tuple-element.43), kind=kLoop, calls=%fused_computation | loop fusion | flops 442368 | bytes 3538944 | tf_op jit(solution)/shard_map/concatenate | solution.py:609
  66.9 16.7 %all-to-all-done.2 = bf16[8,224,256]{2,1,0:T(8,128)(2,1)S(1)} async-done(((bf16[8,224,256]{2,1,0:T(8,128)(2,1)}), bf16[8,224,256]{2,1,0:T(8,128)(2,1)S(1)}, u32[]{:S(2)}, u32[]{:S(2)}) %all-to-all-start.2) | async-done | bytes 917536 | tf_op jit(solution)/shard_map/all_to_all | solution.py:503
  83.6 0.1 reduce_sum.21
  83.7 6.8 %all-gather = bf16[896,256]{1,0:T(8,128)(2,1)S(1)} all-gather(bf16[224,256]{1,0:T(8,128)(2,1)S(1)} %reduce_sum.21), channel_id=2, replica_groups=mesh['sample'=4,'chan'=8] {'sample'}, dimensions={0}, use_global_device_ids=true | all-gather | bytes 573440 | tf_op jit(solution)/shard_map/all_gather | solution.py:658
  90.6 0.1 convert_reduce_fusion
  90.6 0.8 slice_multiply_fusion
  (1 shorter events, 0.0 us)
Async XLA Ops:
  0.6 19.0 %copy-start.7 = (bf16[1,32,4,4,64]{4,3,2,1,0:T(4,128)(2,1)S(1)}, bf16[1,32,4,4,64]{4,3,2,1,0:T(4,128)(2,1)}, u32[]{:S(2)}) copy-start(bf16[1,32,4,4,64]{4,3,2,1,0:T(4,128)(2,1)} %param.5) | copy-start | bytes 196612
  2.9 16.3 %copy-start = (bf16[1,64,8,8,256]{4,3,2,1,0:T(8,128)(2,1)S(1)}, bf16[1,64,8,8,256]{4,3,2,1,0:T(8,128)(2,1)}, u32[]{:S(2)}) copy-start(bf16[1,64,8,8,256]{4,3,2,1,0:T(8,128)(2,1)} %param.4) | copy-start | bytes 6291460
  2.9 31.8 %all-to-all-start = ((bf16[8,480,128]{2,1,0:T(8,128)(2,1)}), bf16[8,480,128]{2,1,0:T(8,128)(2,1)S(1)}, u32[]{:S(2)}, u32[]{:S(2)}) async-start(bf16[8,480,128]{2,1,0:T(8,128)(2,1)} %shard_map.67), calls=%async_computation | async-start | bytes 1966080 | tf_op jit(solution)/shard_map/all_to_all | solution.py:503
  10.3 14.9 %collective-permute-start.1 = (bf16[1,16,16,16,128]{4,3,2,1,0:T(8,128)(2,1)}, bf16[1,16,16,16,128]{4,3,2,1,0:T(8,128)(2,1)}, u32[]{:S(2)}, u32[]{:S(2)}) collective-permute-start(bf16[1,16,16,16,128]{4,3,2,1,0:T(8,128)(2,1)} %param.7), channel_id=1, source_target_pairs={{0,8},{8,0},{16,24},{24,16},{1,9},{9,1},{17,25},{25,17},{2,10},{10... | collective-permute-start | bytes 3145736 | tf_op jit(solution)/shard_map/ppermute | solution.py:499
  11.8 17.8 %collective-permute-start = (bf16[1,1,16,16,128]{4,3,2,1,0:T(8,128)(2,1)}, bf16[1,1,16,16,128]{4,3,2,1,0:T(8,128)(2,1)S(1)}, u32[]{:S(2)}, u32[]{:S(2)}) collective-permute-start(bf16[1,1,16,16,128]{4,3,2,1,0:T(8,128)(2,1)} %slice.6), channel_id=1, source_target_pairs={{0,1},{1,2},{2,3},{3,4},{4,5},{5,6},{6,7},{8,9},{9,10},{10,11},{11... | collective-permute-start | bytes 196616 | tf_op jit(solution)/shard_map/ppermute | solution.py:628
  15.7 1.2 %copy-start.5 = (bf16[1,16,16,16,128]{4,3,2,1,0:T(8,128)(2,1)S(1)}, bf16[1,16,16,16,128]{4,3,2,1,0:T(8,128)(2,1)}, u32[]{:S(2)}) copy-start(bf16[1,16,16,16,128]{4,3,2,1,0:T(8,128)(2,1)} %param.7) | copy-start | bytes 3145732
  17.7 1.4 %copy-start.1 = (bf16[9,2,8,64,128]{4,3,2,1,0:T(8,128)(2,1)}, bf16[9,2,8,64,128]{4,3,2,1,0:T(8,128)(2,1)S(1)}, u32[]{:S(2)}) copy-start(bf16[9,2,8,64,128]{4,3,2,1,0:T(8,128)(2,1)S(1)} %get-tuple-element.39.window) | copy-start | bytes 7077892
  24.4 0.8 copy-start.8
  25.2 0.9 %copy-start.6 = (f32[27,32,256]{2,1,0:T(8,128)}, f32[27,32,256]{2,1,0:T(8,128)S(1)}, u32[]{:S(2)}) copy-start(f32[27,32,256]{2,1,0:T(8,128)S(1)} %get-tuple-element.34) | copy-start | bytes 2654212
  28.1 1.4 %copy-start.3 = (bf16[9,2,8,64,128]{4,3,2,1,0:T(8,128)(2,1)}, bf16[9,2,8,64,128]{4,3,2,1,0:T(8,128)(2,1)S(1)}, u32[]{:S(2)}) copy-start(bf16[9,2,8,64,128]{4,3,2,1,0:T(8,128)(2,1)S(1)} %get-tuple-element.42.window) | copy-start | bytes 7077892
  34.7 2.6 %collective-permute-start.2 = (bf16[8,480,128]{2,1,0:T(8,128)(2,1)S(1)}, bf16[8,480,128]{2,1,0:T(8,128)(2,1)S(1)}, u32[]{:S(2)}, u32[]{:S(2)}) collective-permute-start(bf16[8,480,128]{2,1,0:T(8,128)(2,1)S(1)} %all-to-all-done.got_ref), channel_id=1, source_target_pairs={{0,8},{8,0},{16,24},{24,16},{1,9},{9,1},{17,25},{25,17},{2,10},{10... | collective-permute-start | bytes 2949128 | tf_op jit(solution)/shard_map/ppermute | solution.py:499
  35.3 3.7 %copy-start.9 = (bf16[27,32,256]{2,1,0:T(8,128)(2,1)S(1)}, bf16[27,32,256]{2,1,0:T(8,128)(2,1)}, u32[]{:S(2)}) copy-start(bf16[27,32,256]{2,1,0:T(8,128)(2,1)} %copy-done.8) | copy-start | bytes 1327108
  37.3 15.9 %copy-start.2 = (bf16[9,2,8,64,128]{4,3,2,1,0:T(8,128)(2,1)S(1)}, bf16[9,2,8,64,128]{4,3,2,1,0:T(8,128)(2,1)}, u32[]{:S(2)}) copy-start(bf16[9,2,8,64,128]{4,3,2,1,0:T(8,128)(2,1)} %copy-done.1) | copy-start | bytes 7077892
  39.1 4.2 %collective-permute-start.3 = (bf16[27,32,256]{2,1,0:T(8,128)(2,1)S(1)}, bf16[27,32,256]{2,1,0:T(8,128)(2,1)}, u32[]{:S(2)}, u32[]{:S(2)}) collective-permute-start(bf16[27,32,256]{2,1,0:T(8,128)(2,1)S(1)} %copy-done.9), channel_id=1, source_target_pairs={{0,8},{8,0},{16,24},{24,16},{1,9},{9,1},{17,25},{25,17},{2,10},{10... | collective-permute-start | bytes 1327112 | tf_op jit(solution)/shard_map/ppermute | solution.py:499
  39.2 13.5 %all-to-all-start.1 = ((bf16[8,128,128]{2,1,0:T(8,128)(2,1)}), bf16[8,128,128]{2,1,0:T(8,128)(2,1)S(1)}, u32[]{:S(2)}, u32[]{:S(2)}) async-start(bf16[8,128,128]{2,1,0:T(8,128)(2,1)} %shard_map.73), calls=%async_computation.1 | async-start | bytes 524288 | tf_op jit(solution)/shard_map/all_to_all | solution.py:503
  44.7 15.6 %collective-permute-start.4 = (bf16[27,32,256]{2,1,0:T(8,128)(2,1)S(1)}, bf16[27,32,256]{2,1,0:T(8,128)(2,1)}, u32[]{:S(2)}, u32[]{:S(2)}) collective-permute-start(bf16[27,32,256]{2,1,0:T(8,128)(2,1)S(1)} %add_convert_fusion), channel_id=1, source_target_pairs={{0,16},{8,24},{16,0},{24,8},{1,17},{9,25},{17,1},{25,9},{2,18},{10... | collective-permute-start | bytes 1327112 | tf_op jit(solution)/shard_map/ppermute | solution.py:604
  52.7 1.6 %collective-permute-start.6 = (bf16[8,128,128]{2,1,0:T(8,128)(2,1)S(1)}, bf16[8,128,128]{2,1,0:T(8,128)(2,1)S(1)}, u32[]{:S(2)}, u32[]{:S(2)}) collective-permute-start(bf16[8,128,128]{2,1,0:T(8,128)(2,1)S(1)} %all-to-all-done.1.got_ref), channel_id=1, source_target_pairs={{0,8},{8,0},{16,24},{24,16},{1,9},{9,1},{17,25},{25,17},{2,10},{10... | collective-permute-start | bytes 786440 | tf_op jit(solution)/shard_map/ppermute | solution.py:499
  52.7 1.6 %collective-permute-start.7 = (bf16[1,1,16,16,128]{4,3,2,1,0:T(8,128)(2,1)S(1)}, bf16[1,1,16,16,128]{4,3,2,1,0:T(8,128)(2,1)S(1)}, u32[]{:S(2)}, u32[]{:S(2)}) collective-permute-start(bf16[1,1,16,16,128]{4,3,2,1,0:T(8,128)(2,1)S(1)} %collective-permute-done), channel_id=1, source_target_pairs={{0,8},{8,0},{16,24},{24,16},{1,9},{9,1},{17,25},{25,17},{2,10},{10... | collective-permute-start | bytes 196616 | tf_op jit(solution)/shard_map/ppermute | solution.py:499
  53.2 1.7 %copy-start.4 = (bf16[9,2,8,64,128]{4,3,2,1,0:T(8,128)(2,1)S(1)}, bf16[9,2,8,64,128]{4,3,2,1,0:T(8,128)(2,1)}, u32[]{:S(2)}) copy-start(bf16[9,2,8,64,128]{4,3,2,1,0:T(8,128)(2,1)} %copy-done.3) | copy-start | bytes 7077892
  56.7 26.9 %all-to-all-start.2 = ((bf16[8,224,256]{2,1,0:T(8,128)(2,1)}), bf16[8,224,256]{2,1,0:T(8,128)(2,1)S(1)}, u32[]{:S(2)}, u32[]{:S(2)}) async-start(bf16[8,224,256]{2,1,0:T(8,128)(2,1)} %shard_map.75), calls=%async_computation.2 | async-start | bytes 1835008 | tf_op jit(solution)/shard_map/all_to_all | solution.py:503
  61.5 2.6 %collective-permute-start.5 = (f32[27,32,256]{2,1,0:T(8,128)S(1)}, f32[27,32,256]{2,1,0:T(8,128)}, u32[]{:S(2)}, u32[]{:S(2)}) collective-permute-start(f32[27,32,256]{2,1,0:T(8,128)S(1)} %add_multiply_fusion), channel_id=1, source_target_pairs={{0,8},{8,0},{16,24},{24,16},{1,9},{9,1},{17,25},{25,17},{2,10},{10... | collective-permute-start | bytes 2654216 | tf_op jit(solution)/shard_map/ppermute | solution.py:499

commit v3 on v2

--- a/solution.py
+++ b/solution.py
@@ -139,36 +139,52 @@
     )(position, split)
 
 
-def first_kernel(core_ref, got_ref, products_ref, later_ref, weight, turned):
+def weight_kernel(got_ref, weight_ref):
+    shards = got_ref.shape[0]
+    groups = len(slot_plan())
+    half = weight_ref.shape[0] // shards
+    for c in range(shards):
+        for g in range(groups):
+            weight_ref[pl.ds(c * half, half), pl.ds(g * 128, 128)] = got_ref[c, pl.ds(g * half, half), :]
+
+
+def weights(got, half):
+    shards = got.shape[0]
+    groups = len(slot_plan())
+    return pl.pallas_call(
+        weight_kernel,
+        out_shape=jax.ShapeDtypeStruct((shards * half, groups * 128), low),
+        grid=(1,),
+        in_specs=[pl.BlockSpec((shards, groups * half, 128), lambda i: (0, 0, 0))],
+        out_specs=whole,
+        compiler_params=params,
+        cost_estimate=pl.CostEstimate(flops=10**5, bytes_accessed=10**6, transcendentals=0),
+    )(got)
+
+
+def first_kernel(core_ref, got_ref, weight_ref, products_ref, later_ref, turned):
     shards = got_ref.shape[0]
     half = later_ref.shape[0] // shards
     groups = len(slot_plan())
     core = core_ref[0]
     for c in range(shards):
         span = pl.ds(c * half, half)
-        for g in range(groups):
-            weight[span, pl.ds(g * 128, 128)] = got_ref[c, pl.ds(g * half, half), :]
         for b in range(later_ref.shape[1] // 128):
             lanes = pl.ds(b * 128, 128)
             first = groups * half + b * 2 * half
             turned[span, lanes] = got_ref[c, pl.ds(pl.multiple_of(first + core * half, half), half), :]
             later_ref[span, lanes] = got_ref[c, pl.ds(pl.multiple_of(first + (1 - core) * half, half), half), :]
     products_ref[...] = lax.dot_general(
-        turned[...], weight[...], (((0,), (0,)), ((), ())), preferred_element_type=wide
-    )
-
-
-def spread_kernel(grid, first_ref, later_ref, other_ref, own_ref, sent_ref, weight, products, joined):
+        turned[...], weight_ref[...], (((0,), (0,)), ((), ())), preferred_element_type=wide
+    )
+
+
+def spread_kernel(grid, first_ref, later_ref, other_ref, own_ref, sent_ref, products, joined):
     depth, height, width = grid
     cells = depth * height * width
-    shards = other_ref.shape[0]
-    groups = len(slot_plan())
-    half = later_ref.shape[0] // shards
-    for c in range(shards):
-        for g in range(groups):
-            weight[pl.ds(c * half, half), pl.ds(g * 128, 128)] = other_ref[c, pl.ds(g * half, half), :]
+    shards = sent_ref.shape[0]
     products[pl.ds(0, cells), :] = first_ref[...] + lax.dot_general(
-        later_ref[...], weight[...], (((0,), (0,)), ((), ())), preferred_element_type=wide
+        later_ref[...], other_ref[...], (((0,), (0,)), ((), ())), preferred_element_type=wide
     )
     products[pl.ds(cells, products.shape[0] - cells), :] = jnp.zeros(
         (products.shape[0] - cells, products.shape[1]), wide
@@ -208,38 +224,27 @@
         sent_ref[n] = (joined[...] * slope).astype(low)
 
 
-def first_terms(core, got, cells):
-    shards = got.shape[0]
-    groups = len(slot_plan())
-    half = got.shape[1] // (groups + 2 * (cells // 128))
-    lanes = groups * 128
+def first_terms(core, got, weight, cells):
+    rows, lanes = weight.shape
     return pl.pallas_call(
         first_kernel,
-        out_shape=(
-            jax.ShapeDtypeStruct((cells, lanes), wide),
-            jax.ShapeDtypeStruct((shards * half, cells), low),
-        ),
-        in_specs=[scalar, whole],
+        out_shape=(jax.ShapeDtypeStruct((cells, lanes), wide), jax.ShapeDtypeStruct((rows, cells), low)),
+        in_specs=[scalar, whole, whole],
         out_specs=(whole, whole),
-        scratch_shapes=[pltpu.VMEM((shards * half, lanes), low), pltpu.VMEM((shards * half, cells), low)],
+        scratch_shapes=[pltpu.VMEM((rows, cells), low)],
         compiler_params=params,
         cost_estimate=pl.CostEstimate(flops=10**8, bytes_accessed=3 * 10**6, transcendentals=0),
-    )(core, got)
-
-
-def spread(first, later, other, own, grid):
+    )(core, got, weight)
+
+
+def spread(first, later, other, own, grid, shards):
     cells, lanes = first.shape
-    shards = other.shape[0]
-    half = later.shape[0] // shards
-    rows = lanes // 128 * half
     return pl.pallas_call(
         functools.partial(spread_kernel, grid),
         out_shape=jax.ShapeDtypeStruct((shards, 2 * cells // shards, 128), low),
-        grid=(1,),
-        in_specs=[whole, whole, pl.BlockSpec((shards, rows, 128), lambda i: (0, 0, 0)), whole],
+        in_specs=[whole, whole, whole, whole],
         out_specs=whole,
         scratch_shapes=[
-            pltpu.VMEM((shards * half, lanes), low),
             pltpu.VMEM((cells + 32, lanes), wide),
             pltpu.VMEM((2 * cells // shards, 128), wide),
         ],
@@ -636,16 +641,18 @@
     window, done = windows(act_128[0])
     other_window, other_done = windows(other_act[0])
     done = done + other_done
-    got, own, rim, done, halves = lax.optimization_barrier((got, own, rim, done, halves))
-    other = partner(got, "sample", 1)
-    first, later = first_terms(cores, got, math.prod(grid))
-    cot_sent = spread(first, later, other, own, grid)
-
-    cot_sent, rim, halves = lax.optimization_barrier((cot_sent, rim, halves))
+    chip_upper = core_sum(*halves)
+    beside = (got, own, rim, done, chip_upper)
+    got, own, rim, done, chip_upper = lax.optimization_barrier(beside)
+    weight = weights(got, shard_out // 2)
+    other_weight = partner(weight, "sample", 1)
+    first, later = first_terms(cores, got, weight, math.prod(grid))
+    cot_sent = spread(first, later, other_weight, own, grid, shards)
+
+    cot_sent, rim, chip_upper = lax.optimization_barrier((cot_sent, rim, chip_upper))
     cot_got = exchange(cot_sent, "chan")
-    chip_upper = core_sum(*halves)
-    chip_upper, rim = lax.optimization_barrier((chip_upper, rim))
     other_rim = partner(rim, "sample", 1)
+    cot_got, other_rim = lax.optimization_barrier((cot_got, other_rim))
     total_upper = sample_sum(chip_upper, samples).reshape(3, 3, 3, shard_out, middle)
     total_upper = total_upper.transpose(0, 1, 2, 4, 3)
 

time: 92.1 us -> 91.2 us (level)
  local copies, waits for them, and re-layouts: 7.82 us -> 5.99 us
    unnamed x20, local copies, waits for them, and re-layouts: 6.35 us -> 5.14 us
    mul x1, other arithmetic: 1.16 us -> 0.15 us  [sample_sum(): total = total * (1.0 / samples)]
  transfers between devices with their start and end apart: 11 -> 11, of which waited for: 6 -> 7; matrix products, arithmetic and copies ran while one was open for 8% -> 6% of each run, Pallas kernels for 14% -> 15%
where the time goes in v3:
time: 91.2 us; the launch traced here: 90.5 us
  waiting for transfers between devices  32.2 us (35%)
  starting transfers between devices  21.6 us (24%)
  Pallas kernels  17.3 us (19%)
  blocking collectives  6.78 us (7%)
  local copies, waits for them, and re-layouts  5.99 us (7%)
  other arithmetic  5.81 us (6%)
    all_to_all x3, waiting for transfers between devices, exchange(): return lax.all_to_all(blocks, axis, split_axis=0, concat_axis=0, tiled=True)  28 us
    all_to_all x3, starting transfers between devices, exchange(): return lax.all_to_all(blocks, axis, split_axis=0, concat_axis=0, tiled=True)  15.1 us
    all_gather x1, blocking collectives, body(): shares = lax.all_gather(share.astype(low), 'sample', axis=0).astype(wide)  6.78 us
    pallas_call x1, Pallas kernels, upper_terms(): pl.pallas_call(upper_kernel, out_shape=(jax.ShapeDtypeStruct(shape, wide)...  5.58 us
    unnamed x20, local copies, waits for them, and re-layouts  5.14 us
    ppermute x6, waiting for transfers between devices, partner(): return lax.ppermute(array, axis, [(i, i ^ by) for i in range(size)])  4.18 us
    ppermute x1, starting transfers between devices, body(): lax.ppermute(act_128[:, -1:], 'chan', [(i, i + 1) for i in range(shards -...  3.91 us
    pallas_call x2, Pallas kernels, windows(): pl.pallas_call(window_kernel, out_shape=(jax.ShapeDtypeStruct(shape, low)...  2.77 us
  transfers between devices with their start and end apart: 11, of which 7 were waited for; matrix products, arithmetic and copies ran while one was open for 6% of the time, Pallas kernels for 15%

profile of v3, /device:TPU:0, one launch (start us, length us, event | category | flops | bytes accessed | tf_op | source)
XLA Modules:
  0.0 90.5 jit_solution(11324157668189981223)
XLA Ops:
  0.6 0.0 copy-start
  0.7 0.0 copy-start.8
  0.7 2.4 %shard_map.67 = bf16[8,480,128]{2,1,0:T(8,128)(2,1)} custom-call(s32[1]{0:T(128)} %bitcast.core_ref, bf16[27,64,256]{2,1,0:T(8,128)(2,1)} %bitcast.29, bf16[512,64]{1,0:T(8,128)(2,1)} %bitcast.23), custom_call_target="tpu_custom_call" | custom-call | flops 1000000 | bytes 3000000 | tf_op jit(solution)/shard_map/pallas_call | solution.py:88
  3.0 7.3 %all-to-all-start = ((bf16[8,480,128]{2,1,0:T(8,128)(2,1)}), bf16[8,480,128]{2,1,0:T(8,128)(2,1)S(1)}, u32[]{:S(2)}, u32[]{:S(2)}) async-start(bf16[8,480,128]{2,1,0:T(8,128)(2,1)} %shard_map.67), calls=%async_computation | async-start | bytes 1966080 | tf_op jit(solution)/shard_map/all_to_all | solution.py:508
  10.3 0.0 collective-permute-start.1
  10.3 0.0 copy-done
  10.3 0.0 copy-done.8
  10.4 5.6 %shard_map.71 = (f32[27,32,256]{2,1,0:T(8,128)S(1)}, bf16[27,32,256]{2,1,0:T(8,128)(2,1)}) custom-call(s32[1]{0:T(128)} %bitcast.core_ref, bf16[64,8,8,256]{3,2,1,0:T(8,128)(2,1)S(1)} %bitcast.20, bf16[32,4,4,64]{3,2,1,0:T(4,128)(2,1)S(1)} %bitcast.24), custom_call_target="tpu_custom_call" | custom-call | flops 500000000 | bytes 6000000 | tf_op jit(solution)/shard_map/pallas_call | solution.py:486
  15.9 0.0 copy-start.6
  15.9 0.9 copy-done.6
  16.8 0.5 collective-permute-start.2
  17.3 0.8 slice.6
  18.2 3.9 %collective-permute-start = (bf16[1,1,16,16,128]{4,3,2,1,0:T(8,128)(2,1)S(1)}, bf16[1,1,16,16,128]{4,3,2,1,0:T(8,128)(2,1)S(1)}, u32[]{:S(2)}, u32[]{:S(2)}) collective-permute-start(bf16[1,1,16,16,128]{4,3,2,1,0:T(8,128)(2,1)S(1)} %slice.6), channel_id=1, source_target_pairs={{0,1},{1,2},{2,3},{3,4},{4,5},{5,6},{6,7},{8,9},{9,10},{10,11},{11... | collective-permute-start | bytes 196616 | tf_op jit(solution)/shard_map/ppermute | solution.py:633
  22.1 0.0 copy-start.5
  22.1 1.2 %copy-done.5 = bf16[1,16,16,16,128]{4,3,2,1,0:T(8,128)(2,1)S(1)} copy-done((bf16[1,16,16,16,128]{4,3,2,1,0:T(8,128)(2,1)S(1)}, bf16[1,16,16,16,128]{4,3,2,1,0:T(8,128)(2,1)}, u32[]{:S(2)}) %copy-start.5) | copy-done | bytes 1048600
  23.3 0.0 copy-start.7
  23.3 0.8 shard_map.69
  24.1 0.0 copy-start.1
  24.1 1.4 %copy-done.1 = bf16[9,2,8,64,128]{4,3,2,1,0:T(8,128)(2,1)} copy-done((bf16[9,2,8,64,128]{4,3,2,1,0:T(8,128)(2,1)}, bf16[9,2,8,64,128]{4,3,2,1,0:T(8,128)(2,1)S(1)}, u32[]{:S(2)}) %copy-start.1) | copy-done | bytes 2359320
  25.5 0.4 shard_map.68.own_ref
  25.9 0.0 collective-permute-done.2
  25.9 0.0 copy-done.7
  26.0 1.9 %add_convert_fusion = bf16[27,32,256]{2,1,0:T(8,128)(2,1)} fusion(f32[27,32,256]{2,1,0:T(8,128)S(1)} %copy-done.7, bf16[27,32,256]{2,1,0:T(8,128)(2,1)} %collective-permute-done.2), kind=kLoop, calls=%fused_computation.3 | loop fusion | flops 663552 | bytes 1769472 | tf_op jit(solution)/shard_map/convert_element_type | solution.py:601
  27.9 0.0 collective-permute-done.1
  27.9 2.0 %shard_map.70 = (bf16[9,2,8,64,128]{4,3,2,1,0:T(8,128)(2,1)S(1)}, f32[8,128]{1,0:T(8,128)S(1)}) custom-call(bf16[16,16,16,128]{3,2,1,0:T(8,128)(2,1)} %bitcast.7.volume_ref), custom_call_target="tpu_custom_call" | custom-call | flops 1000000 | bytes 4000000 | tf_op jit(solution)/shard_map/pallas_call | solution.py:319
  29.9 0.0 copy-start.3
  29.9 1.4 %copy-done.3 = bf16[9,2,8,64,128]{4,3,2,1,0:T(8,128)(2,1)} copy-done((bf16[9,2,8,64,128]{4,3,2,1,0:T(8,128)(2,1)}, bf16[9,2,8,64,128]{4,3,2,1,0:T(8,128)(2,1)S(1)}, u32[]{:S(2)}) %copy-start.3) | copy-done | bytes 2359320
  31.3 0.0 collective-permute-done
  31.3 3.4 %all-to-all-done.got_ref = bf16[8,480,128]{2,1,0:T(8,128)(2,1)S(1)} async-done(((bf16[8,480,128]{2,1,0:T(8,128)(2,1)}), bf16[8,480,128]{2,1,0:T(8,128)(2,1)S(1)}, u32[]{:S(2)}, u32[]{:S(2)}) %all-to-all-start) | async-done | bytes 983072 | tf_op jit(solution)/shard_map/all_to_all | solution.py:508
  34.7 0.1 shard_map.72.weight_ref
  34.8 0.1 collective-permute-start.3
  34.9 0.5 shard_map.73
  35.4 0.0 copy-start.2
  35.4 1.3 %collective-permute-done.3.other_ref = bf16[256,896]{1,0:T(8,128)(2,1)S(1)} collective-permute-done((bf16[256,896]{1,0:T(8,128)(2,1)S(1)}, bf16[256,896]{1,0:T(8,128)(2,1)S(1)}, u32[]{:S(2)}, u32[]{:S(2)}) %collective-permute-start.3) | collective-permute-done | bytes 458784 | tf_op jit(solution)/shard_map/ppermute | solution.py:504
  36.7 1.7 %shard_map.74 = bf16[8,128,128]{2,1,0:T(8,128)(2,1)} custom-call(f32[512,896]{1,0:T(8,128)S(1)} %get-tuple-element.26.first_ref, bf16[256,512]{1,0:T(8,128)(2,1)S(1)} %get-tuple-element.27.later_ref, bf16[256,896]{1,0:T(8,128)(2,1)S(1)} %collective-permute-done.3.other_ref, bf16[1024,128]{1,0:T(8,128)(2,1)S(1)} %shard_map.68.own_ref), custom_call_target="tpu_custom_call" | custom-call | flops 500000000 | bytes 3000000 | tf_op jit(solution)/shard_map/pallas_call | solution.py:242
  38.4 4.1 %all-to-all-start.1 = ((bf16[8,128,128]{2,1,0:T(8,128)(2,1)}), bf16[8,128,128]{2,1,0:T(8,128)(2,1)S(1)}, u32[]{:S(2)}, u32[]{:S(2)}) async-start(bf16[8,128,128]{2,1,0:T(8,128)(2,1)} %shard_map.74), calls=%async_computation.1 | async-start | bytes 524288 | tf_op jit(solution)/shard_map/all_to_all | solution.py:508
  42.5 1.5 %collective-permute-start.4 = (bf16[27,32,256]{2,1,0:T(8,128)(2,1)}, bf16[27,32,256]{2,1,0:T(8,128)(2,1)S(1)}, u32[]{:S(2)}, u32[]{:S(2)}) collective-permute-start(bf16[27,32,256]{2,1,0:T(8,128)(2,1)} %add_convert_fusion), channel_id=1, source_target_pairs={{0,16},{8,24},{16,0},{24,8},{1,17},{9,25},{17,1},{25,9},{2,18},{10... | collective-permute-start | bytes 1327112 | tf_op jit(solution)/shard_map/ppermute | solution.py:609
  44.0 0.0 collective-permute-start.6
  44.0 1.3 %collective-permute-done.6 = bf16[1,1,16,16,128]{4,3,2,1,0:T(8,128)(2,1)S(1)} collective-permute-done((bf16[1,1,16,16,128]{4,3,2,1,0:T(8,128)(2,1)S(1)}, bf16[1,1,16,16,128]{4,3,2,1,0:T(8,128)(2,1)S(1)}, u32[]{:S(2)}, u32[]{:S(2)}) %collective-permute-start.6) | collective-permute-done | bytes 65568 | tf_op jit(solution)/shard_map/ppermute | solution.py:504
  45.2 6.5 %all-to-all-done.1.got_ref = bf16[8,128,128]{2,1,0:T(8,128)(2,1)S(1)} async-done(((bf16[8,128,128]{2,1,0:T(8,128)(2,1)}), bf16[8,128,128]{2,1,0:T(8,128)(2,1)S(1)}, u32[]{:S(2)}, u32[]{:S(2)}) %all-to-all-start.1) | async-done | bytes 262176 | tf_op jit(solution)/shard_map/all_to_all | solution.py:508
  51.7 0.0 collective-permute-start.7
  51.7 0.0 copy-done.2
  51.7 0.0 copy-start.4
  51.7 0.9 %shard_map.75.total_ref = f32[7,256,256]{2,1,0:T(8,128)S(1)} custom-call(s32[1]{0:T(128)} %bitcast.core_ref, bf16[8,128,128]{2,1,0:T(8,128)(2,1)S(1)} %all-to-all-done.1.got_ref, bf16[9,2,8,64,128]{4,3,2,1,0:T(8,128)(2,1)S(1)} %copy-done.2, bf16[1,16,16,128]{3,2,1,0:T(8,128)(2,1)S(1)} %bitcast.25, f32[8,128]{1,0:T(8,128)S(1)} %add.15.done_ref), custom_call_target="tpu_custom_call" | custom-call | flops 500000000 | bytes 5000000 | tf_op jit(solution)/shard_map/pallas_call | solution.py:395
  52.7 0.6 collective-permute-done.7.other_ref
  53.2 0.1 copy-done.4
  53.4 1.8 %shard_map.76 = bf16[8,224,256]{2,1,0:T(8,128)(2,1)} custom-call(s32[1]{0:T(128)} %bitcast.core_ref, f32[7,256,256]{2,1,0:T(8,128)S(1)} %shard_map.75.total_ref, bf16[8,128,128]{2,1,0:T(8,128)(2,1)S(1)} %collective-permute-done.7.other_ref, bf16[9,2,8,64,128]{4,3,2,1,0:T(8,128)(2,1)S(1)} %copy-done.4, bf16[1,16,16,128]{3,2,1,0:T(8,128)(2,1)S(1)} %bitcast.26), custom_call_target="tpu_custom_call" | custom-call | flops 500000000 | bytes 5000000 | tf_op jit(solution)/shard_map/pallas_call | solution.py:432
  55.2 0.0 copy-start.9
  55.2 3.7 %all-to-all-start.2 = ((bf16[8,224,256]{2,1,0:T(8,128)(2,1)}), bf16[8,224,256]{2,1,0:T(8,128)(2,1)S(1)}, u32[]{:S(2)}, u32[]{:S(2)}) async-start(bf16[8,224,256]{2,1,0:T(8,128)(2,1)} %shard_map.76), calls=%async_computation.2 | async-start | bytes 1835008 | tf_op jit(solution)/shard_map/all_to_all | solution.py:508
  58.9 0.0 collective-permute-done.4
  58.9 0.0 copy-done.9
  58.9 0.1 add_multiply_fusion
  59.1 0.6 collective-permute-start.5
  59.6 1.1 %shard_map.77 = f32[8,8,8,256]{3,2,1,0:T(8,128)} custom-call(bf16[8,128,128]{2,1,0:T(8,128)(2,1)S(1)} %all-to-all-done.1.got_ref), custom_call_target="tpu_custom_call" | custom-call | flops 1000000 | bytes 2000000 | tf_op jit(solution)/shard_map/pallas_call | solution.py:279
  60.7 1.1 %collective-permute-done.5 = f32[27,32,256]{2,1,0:T(8,128)} collective-permute-done((f32[27,32,256]{2,1,0:T(8,128)S(1)}, f32[27,32,256]{2,1,0:T(8,128)}, u32[]{:S(2)}, u32[]{:S(2)}) %collective-permute-start.5) | collective-permute-done | bytes 884768 | tf_op jit(solution)/shard_map/ppermute | solution.py:504
  61.8 1.4 %broadcast_select_fusion.1 = (f32[27,32,256]{2,1,0:T(8,128)S(1)}, f32[27,32,256]{2,1,0:T(8,128)S(1)}) fusion(f32[27,32,256]{2,1,0:T(8,128)} %collective-permute-done.5, pred[]{:T(512)S(6)} %eq.7, bf16[27,32,256]{2,1,0:T(8,128)(2,1)S(1)} %collective-permute-done.4, bf16[27,32,256]{2,1,0:T(8,128)(2,1)S(1)} %copy-done.9), kind=kLoop, calls=%fused_computation.6 | loop fusion | flops 1327104 | bytes 3538945 | tf_op jit(solution)/shard_map/jit(_where)/select_n | solution.py:612
  63.3 1.3 %pad_maximum_fusion = f32[27,64,256]{2,1,0:T(8,128)} fusion(f32[27,32,256]{2,1,0:T(8,128)S(1)} %get-tuple-element.40, f32[27,32,256]{2,1,0:T(8,128)S(1)} %get-tuple-element.39), kind=kLoop, calls=%fused_computation | loop fusion | flops 442368 | bytes 3538944 | tf_op jit(solution)/shard_map/concatenate | solution.py:614
  64.6 18.2 %all-to-all-done.2 = bf16[8,224,256]{2,1,0:T(8,128)(2,1)S(1)} async-done(((bf16[8,224,256]{2,1,0:T(8,128)(2,1)}), bf16[8,224,256]{2,1,0:T(8,128)(2,1)S(1)}, u32[]{:S(2)}, u32[]{:S(2)}) %all-to-all-start.2) | async-done | bytes 917536 | tf_op jit(solution)/shard_map/all_to_all | solution.py:508
  82.8 0.1 reduce_sum.21
  82.9 6.8 %all-gather = bf16[896,256]{1,0:T(8,128)(2,1)S(1)} all-gather(bf16[224,256]{1,0:T(8,128)(2,1)S(1)} %reduce_sum.21), channel_id=2, replica_groups=mesh['sample'=4,'chan'=8] {'sample'}, dimensions={0}, use_global_device_ids=true | all-gather | bytes 573440 | tf_op jit(solution)/shard_map/all_gather | solution.py:665
  89.7 0.1 convert_reduce_fusion
  89.7 0.8 slice_multiply_fusion
  (1 shorter events, 0.0 us)
Async XLA Ops:
  0.6 9.7 %copy-start = (bf16[1,64,8,8,256]{4,3,2,1,0:T(8,128)(2,1)S(1)}, bf16[1,64,8,8,256]{4,3,2,1,0:T(8,128)(2,1)}, u32[]{:S(2)}) copy-start(bf16[1,64,8,8,256]{4,3,2,1,0:T(8,128)(2,1)} %param.4) | copy-start | bytes 6291460
  0.7 9.7 %copy-start.8 = (bf16[1,32,4,4,64]{4,3,2,1,0:T(4,128)(2,1)S(1)}, bf16[1,32,4,4,64]{4,3,2,1,0:T(4,128)(2,1)}, u32[]{:S(2)}) copy-start(bf16[1,32,4,4,64]{4,3,2,1,0:T(4,128)(2,1)} %param.5) | copy-start | bytes 196612
  3.0 31.7 %all-to-all-start = ((bf16[8,480,128]{2,1,0:T(8,128)(2,1)}), bf16[8,480,128]{2,1,0:T(8,128)(2,1)S(1)}, u32[]{:S(2)}, u32[]{:S(2)}) async-start(bf16[8,480,128]{2,1,0:T(8,128)(2,1)} %shard_map.67), calls=%async_computation | async-start | bytes 1966080 | tf_op jit(solution)/shard_map/all_to_all | solution.py:508
  10.3 17.6 %collective-permute-start.1 = (bf16[1,16,16,16,128]{4,3,2,1,0:T(8,128)(2,1)}, bf16[1,16,16,16,128]{4,3,2,1,0:T(8,128)(2,1)}, u32[]{:S(2)}, u32[]{:S(2)}) collective-permute-start(bf16[1,16,16,16,128]{4,3,2,1,0:T(8,128)(2,1)} %param.7), channel_id=1, source_target_pairs={{0,8},{8,0},{16,24},{24,16},{1,9},{9,1},{17,25},{25,17},{2,10},{10... | collective-permute-start | bytes 3145736 | tf_op jit(solution)/shard_map/ppermute | solution.py:504
  15.9 0.9 copy-start.6
  16.8 9.1 %collective-permute-start.2 = (bf16[27,32,256]{2,1,0:T(8,128)(2,1)}, bf16[27,32,256]{2,1,0:T(8,128)(2,1)}, u32[]{:S(2)}, u32[]{:S(2)}) collective-permute-start(bf16[27,32,256]{2,1,0:T(8,128)(2,1)} %get-tuple-element.24), channel_id=1, source_target_pairs={{0,8},{8,0},{16,24},{24,16},{1,9},{9,1},{17,25},{25,17},{2,10},{10... | collective-permute-start | bytes 1327112 | tf_op jit(solution)/shard_map/ppermute | solution.py:504
  18.2 13.2 %collective-permute-start = (bf16[1,1,16,16,128]{4,3,2,1,0:T(8,128)(2,1)S(1)}, bf16[1,1,16,16,128]{4,3,2,1,0:T(8,128)(2,1)S(1)}, u32[]{:S(2)}, u32[]{:S(2)}) collective-permute-start(bf16[1,1,16,16,128]{4,3,2,1,0:T(8,128)(2,1)S(1)} %slice.6), channel_id=1, source_target_pairs={{0,1},{1,2},{2,3},{3,4},{4,5},{5,6},{6,7},{8,9},{9,10},{10,11},{11... | collective-permute-start | bytes 196616 | tf_op jit(solution)/shard_map/ppermute | solution.py:633
  22.1 1.2 %copy-start.5 = (bf16[1,16,16,16,128]{4,3,2,1,0:T(8,128)(2,1)S(1)}, bf16[1,16,16,16,128]{4,3,2,1,0:T(8,128)(2,1)}, u32[]{:S(2)}) copy-start(bf16[1,16,16,16,128]{4,3,2,1,0:T(8,128)(2,1)} %param.7) | copy-start | bytes 3145732
  23.3 2.6 %copy-start.7 = (f32[27,32,256]{2,1,0:T(8,128)S(1)}, f32[27,32,256]{2,1,0:T(8,128)}, u32[]{:S(2)}) copy-start(f32[27,32,256]{2,1,0:T(8,128)} %copy-done.6) | copy-start | bytes 2654212
  24.1 1.4 %copy-start.1 = (bf16[9,2,8,64,128]{4,3,2,1,0:T(8,128)(2,1)}, bf16[9,2,8,64,128]{4,3,2,1,0:T(8,128)(2,1)S(1)}, u32[]{:S(2)}) copy-start(bf16[9,2,8,64,128]{4,3,2,1,0:T(8,128)(2,1)S(1)} %get-tuple-element.35.window) | copy-start | bytes 7077892
  29.9 1.4 %copy-start.3 = (bf16[9,2,8,64,128]{4,3,2,1,0:T(8,128)(2,1)}, bf16[9,2,8,64,128]{4,3,2,1,0:T(8,128)(2,1)S(1)}, u32[]{:S(2)}) copy-start(bf16[9,2,8,64,128]{4,3,2,1,0:T(8,128)(2,1)S(1)} %get-tuple-element.37.window) | copy-start | bytes 7077892
  34.8 1.9 %collective-permute-start.3 = (bf16[256,896]{1,0:T(8,128)(2,1)S(1)}, bf16[256,896]{1,0:T(8,128)(2,1)S(1)}, u32[]{:S(2)}, u32[]{:S(2)}) collective-permute-start(bf16[256,896]{1,0:T(8,128)(2,1)S(1)} %shard_map.72.weight_ref), channel_id=1, source_target_pairs={{0,8},{8,0},{16,24},{24,16},{1,9},{9,1},{17,25},{25,17},{2,10},{10... | collective-permute-start | bytes 1376264 | tf_op jit(solution)/shard_map/ppermute | solution.py:504
  35.4 16.3 %copy-start.2 = (bf16[9,2,8,64,128]{4,3,2,1,0:T(8,128)(2,1)S(1)}, bf16[9,2,8,64,128]{4,3,2,1,0:T(8,128)(2,1)}, u32[]{:S(2)}) copy-start(bf16[9,2,8,64,128]{4,3,2,1,0:T(8,128)(2,1)} %copy-done.1) | copy-start | bytes 7077892
  38.4 13.3 %all-to-all-start.1 = ((bf16[8,128,128]{2,1,0:T(8,128)(2,1)}), bf16[8,128,128]{2,1,0:T(8,128)(2,1)S(1)}, u32[]{:S(2)}, u32[]{:S(2)}) async-start(bf16[8,128,128]{2,1,0:T(8,128)(2,1)} %shard_map.74), calls=%async_computation.1 | async-start | bytes 524288 | tf_op jit(solution)/shard_map/all_to_all | solution.py:508
  42.5 16.5 %collective-permute-start.4 = (bf16[27,32,256]{2,1,0:T(8,128)(2,1)}, bf16[27,32,256]{2,1,0:T(8,128)(2,1)S(1)}, u32[]{:S(2)}, u32[]{:S(2)}) collective-permute-start(bf16[27,32,256]{2,1,0:T(8,128)(2,1)} %add_convert_fusion), channel_id=1, source_target_pairs={{0,16},{8,24},{16,0},{24,8},{1,17},{9,25},{17,1},{25,9},{2,18},{10... | collective-permute-start | bytes 1327112 | tf_op jit(solution)/shard_map/ppermute | solution.py:609
  44.0 1.3 %collective-permute-start.6 = (bf16[1,1,16,16,128]{4,3,2,1,0:T(8,128)(2,1)S(1)}, bf16[1,1,16,16,128]{4,3,2,1,0:T(8,128)(2,1)S(1)}, u32[]{:S(2)}, u32[]{:S(2)}) collective-permute-start(bf16[1,1,16,16,128]{4,3,2,1,0:T(8,128)(2,1)S(1)} %collective-permute-done), channel_id=1, source_target_pairs={{0,8},{8,0},{16,24},{24,16},{1,9},{9,1},{17,25},{25,17},{2,10},{10... | collective-permute-start | bytes 196616 | tf_op jit(solution)/shard_map/ppermute | solution.py:504
  51.7 1.5 %collective-permute-start.7 = (bf16[8,128,128]{2,1,0:T(8,128)(2,1)S(1)}, bf16[8,128,128]{2,1,0:T(8,128)(2,1)S(1)}, u32[]{:S(2)}, u32[]{:S(2)}) collective-permute-start(bf16[8,128,128]{2,1,0:T(8,128)(2,1)S(1)} %all-to-all-done.1.got_ref), channel_id=1, source_target_pairs={{0,8},{8,0},{16,24},{24,16},{1,9},{9,1},{17,25},{25,17},{2,10},{10... | collective-permute-start | bytes 786440 | tf_op jit(solution)/shard_map/ppermute | solution.py:504
  51.7 1.7 %copy-start.4 = (bf16[9,2,8,64,128]{4,3,2,1,0:T(8,128)(2,1)S(1)}, bf16[9,2,8,64,128]{4,3,2,1,0:T(8,128)(2,1)}, u32[]{:S(2)}) copy-start(bf16[9,2,8,64,128]{4,3,2,1,0:T(8,128)(2,1)} %copy-done.3) | copy-start | bytes 7077892
  55.2 3.8 %copy-start.9 = (bf16[27,32,256]{2,1,0:T(8,128)(2,1)S(1)}, bf16[27,32,256]{2,1,0:T(8,128)(2,1)}, u32[]{:S(2)}) copy-start(bf16[27,32,256]{2,1,0:T(8,128)(2,1)} %add_convert_fusion) | copy-start | bytes 1327108
  55.2 27.6 %all-to-all-start.2 = ((bf16[8,224,256]{2,1,0:T(8,128)(2,1)}), bf16[8,224,256]{2,1,0:T(8,128)(2,1)S(1)}, u32[]{:S(2)}, u32[]{:S(2)}) async-start(bf16[8,224,256]{2,1,0:T(8,128)(2,1)} %shard_map.76), calls=%async_computation.2 | async-start | bytes 1835008 | tf_op jit(solution)/shard_map/all_to_all | solution.py:508
  59.1 2.7 %collective-permute-start.5 = (f32[27,32,256]{2,1,0:T(8,128)S(1)}, f32[27,32,256]{2,1,0:T(8,128)}, u32[]{:S(2)}, u32[]{:S(2)}) collective-permute-start(f32[27,32,256]{2,1,0:T(8,128)S(1)} %add_multiply_fusion), channel_id=1, source_target_pairs={{0,8},{8,0},{16,24},{24,16},{1,9},{9,1},{17,25},{25,17},{2,10},{10... | collective-permute-start | bytes 2654216 | tf_op jit(solution)/shard_map/ppermute | solution.py:504

commit v4 on v3

--- a/solution.py
+++ b/solution.py
@@ -358,11 +358,11 @@
         first_cells[n] = taken[0]
 
 
-def tap_pair(window, first_cells, start):
+def tap_pair(window, first_cells, core, pair):
     planes = window.shape[2]
     both = []
-    for n in range(2):
-        tap = jnp.minimum(start + n, 26)
+    for n in (2 * pair, 2 * pair + 1):
+        tap = core * 14 + n if n < 13 else 13
         depth, row, col = tap // 9, tap // 3 % 3, tap % 3
         which, parity = col * 3 + row, (depth + 1) % 2
         lowest = jnp.where(depth == 0, first_cells[which], window[which, parity, 0])
@@ -378,7 +378,7 @@
     side = cotangent_side(got_ref, cells)
     count = total_ref.shape[0]
     for pair in range(count):
-        taps = tap_pair(window, first_cells, (core_ref[0] * count + pair) * 2)
+        taps = tap_pair(window, first_cells, core_ref[0], pair)
         total_ref[pair] = jnp.dot(side, taps, preferred_element_type=wide)
 
 
@@ -411,14 +411,21 @@
     share = below // shards
     copies = []
     for pair in range(total_ref.shape[0]):
-        taps = tap_pair(window, first_cells, (core_ref[0] * total_ref.shape[0] + pair) * 2)
+        taps = tap_pair(window, first_cells, core_ref[0], pair)
         total = total_ref[pair] + jnp.dot(side, taps, preferred_element_type=wide)
         total = total.T.astype(low)
-        for n in range(2):
-            for d in range(shards):
-                start = n * below + d * share
-                staged[d, pl.ds((2 * pair + n) * share, share), :] = total[start : start + share]
-        part = pl.ds(2 * pair * share, 2 * share)
+        count = 0
+        for n in (2 * pair, 2 * pair + 1):
+            rows = total[n % 2 * below : (n % 2 + 1) * below]
+            halves = [rows[:, :128], rows[:, 128:]]
+            if n == 13:
+                halves = [jnp.where(core_ref[0] == 0, *halves)]
+            for half in halves:
+                start = 2 * pair * 2 * share + count * share
+                for d in range(shards):
+                    staged[d, pl.ds(start, share), :] = half[d * share : (d + 1) * share]
+                count += 1
+        part = pl.ds(4 * pair * share, count * share)
         copies.append(pltpu.make_async_copy(staged.at[:, part, :], sent_ref.at[:, part, :], left.at[pair]))
         copies[-1].start()
     for copy in copies:
@@ -427,8 +434,8 @@
 
 def lower_terms(core, total, other, window, rim, grid):
     shards = other.shape[0]
-    pairs, middle, lanes = total.shape
-    shape = (shards, pairs * lanes // shards, middle)
+    pairs, middle, _ = total.shape
+    shape = (shards, 27 * window.shape[4] // shards, 128)
     return pl.pallas_call(
         lower_kernel,
         out_shape=pltpu.HBM(shape, low),
@@ -439,6 +446,31 @@
         compiler_params=params,
         cost_estimate=pl.CostEstimate(flops=5 * 10**8, bytes_accessed=5 * 10**6, transcendentals=0),
     )(core, total, other, window, rim)
+
+
+def total_kernel(shares_ref, total_ref, *, scale):
+    share = total_ref.shape[1]
+    for core in range(2):
+        total = shares_ref[core].astype(wide)
+        for by in range(2, shares_ref.shape[0], 2):
+            total = total + shares_ref[core + by].astype(wide)
+        total = total * scale
+        for n in range(13):
+            for half in range(2):
+                start = (2 * n + half) * share
+                total_ref[core * 14 + n, :, pl.ds(half * 128, 128)] = total[start : start + share]
+        total_ref[13, :, pl.ds(core * 128, 128)] = total[26 * share : 27 * share]
+
+
+def total_terms(shares, scale):
+    return pl.pallas_call(
+        functools.partial(total_kernel, scale=scale),
+        out_shape=jax.ShapeDtypeStruct((27, shares.shape[1] // 27, 2 * shares.shape[2]), wide),
+        in_specs=[whole],
+        out_specs=whole,
+        compiler_params=params,
+        cost_estimate=pl.CostEstimate(flops=10**6, bytes_accessed=10**6, transcendentals=0),
+    )(shares)
 
 
 def upper_kernel(core_ref, volume_ref, cot_ref, mine_ref, theirs_ref, flat, cot_flat, lined, left):
@@ -662,9 +694,8 @@
     terms = lower_terms(cores, own_terms, other_cot, other_window, other_rim[0], slab_grid)
     share = jnp.sum(exchange(terms, "chan").astype(wide), axis=0)
     cot_full = unpack(cot_got, slab_grid)
-    shares = lax.all_gather(share.astype(low), "sample", axis=0).astype(wide)
-    shares = shares.reshape(samples // 2, -1, middle).sum(axis=0) * (1.0 / samples)
-    total_lower = shares[: 27 * below // shards].reshape(3, 3, 3, below // shards, middle)
+    shares = lax.all_gather(share.astype(low), "sample", axis=0)
+    total_lower = total_terms(shares, 1.0 / samples).reshape(3, 3, 3, below // shards, middle)
     return (total_upper, total_lower, cot_full[None])
 
 

time: 91.2 us -> 90.3 us (level)
  no operation moved by 1% of the time
where the time goes in v4:
time: 90.3 us; the launch traced here: 89.7 us
  waiting for transfers between devices  31.4 us (35%)
  starting transfers between devices  21.6 us (24%)
  Pallas kernels  18.1 us (20%)
  blocking collectives  6.73 us (7%)
  local copies, waits for them, and re-layouts  6.02 us (7%)
  other arithmetic  4.95 us (5%)
    all_to_all x3, waiting for transfers between devices, exchange(): return lax.all_to_all(blocks, axis, split_axis=0, concat_axis=0, tiled=True)  27.3 us
    all_to_all x3, starting transfers between devices, exchange(): return lax.all_to_all(blocks, axis, split_axis=0, concat_axis=0, tiled=True)  15.1 us
    all_gather x1, blocking collectives, body(): shares = lax.all_gather(share.astype(low), 'sample', axis=0)  6.73 us
    pallas_call x1, Pallas kernels, upper_terms(): pl.pallas_call(upper_kernel, out_shape=(jax.ShapeDtypeStruct(shape, wide)...  5.58 us
    unnamed x20, local copies, waits for them, and re-layouts  5.17 us
    ppermute x6, waiting for transfers between devices, partner(): return lax.ppermute(array, axis, [(i, i ^ by) for i in range(size)])  4.18 us
    ppermute x1, starting transfers between devices, body(): lax.ppermute(act_128[:, -1:], 'chan', [(i, i + 1) for i in range(shards -...  3.91 us
    pallas_call x2, Pallas kernels, windows(): pl.pallas_call(window_kernel, out_shape=(jax.ShapeDtypeStruct(shape, low)...  2.77 us
  transfers between devices with their start and end apart: 11, of which 7 were waited for; matrix products, arithmetic and copies ran while one was open for 6% of the time, Pallas kernels for 15%

profile of v4, /device:TPU:0, one launch (start us, length us, event | category | flops | bytes accessed | tf_op | source)
XLA Modules:
  0.0 89.7 jit_solution(17928010740363807595)
XLA Ops:
  0.6 0.0 copy-start
  0.7 0.0 copy-start.8
  0.7 2.4 %shard_map.67 = bf16[8,480,128]{2,1,0:T(8,128)(2,1)} custom-call(s32[1]{0:T(128)} %bitcast.core_ref, bf16[27,64,256]{2,1,0:T(8,128)(2,1)} %bitcast.28, bf16[512,64]{1,0:T(8,128)(2,1)} %bitcast.23), custom_call_target="tpu_custom_call" | custom-call | flops 1000000 | bytes 3000000 | tf_op jit(solution)/shard_map/pallas_call | solution.py:88
  3.0 7.3 %all-to-all-start = ((bf16[8,480,128]{2,1,0:T(8,128)(2,1)}), bf16[8,480,128]{2,1,0:T(8,128)(2,1)S(1)}, u32[]{:S(2)}, u32[]{:S(2)}) async-start(bf16[8,480,128]{2,1,0:T(8,128)(2,1)} %shard_map.67), calls=%async_computation | async-start | bytes 1966080 | tf_op jit(solution)/shard_map/all_to_all | solution.py:540
  10.3 0.0 collective-permute-start.1
  10.3 0.0 copy-done
  10.3 0.0 copy-done.8
  10.4 5.6 %shard_map.71 = (f32[27,32,256]{2,1,0:T(8,128)S(1)}, bf16[27,32,256]{2,1,0:T(8,128)(2,1)}) custom-call(s32[1]{0:T(128)} %bitcast.core_ref, bf16[64,8,8,256]{3,2,1,0:T(8,128)(2,1)S(1)} %bitcast.19, bf16[32,4,4,64]{3,2,1,0:T(4,128)(2,1)S(1)} %bitcast.24), custom_call_target="tpu_custom_call" | custom-call | flops 500000000 | bytes 6000000 | tf_op jit(solution)/shard_map/pallas_call | solution.py:518
  15.9 0.0 copy-start.6
  15.9 0.9 %copy-done.6 = f32[27,32,256]{2,1,0:T(8,128)} copy-done((f32[27,32,256]{2,1,0:T(8,128)}, f32[27,32,256]{2,1,0:T(8,128)S(1)}, u32[]{:S(2)}) %copy-start.6) | copy-done | bytes 884760
  16.9 0.5 collective-permute-start.2
  17.3 0.8 slice.3
  18.2 3.9 %collective-permute-start = (bf16[1,1,16,16,128]{4,3,2,1,0:T(8,128)(2,1)S(1)}, bf16[1,1,16,16,128]{4,3,2,1,0:T(8,128)(2,1)S(1)}, u32[]{:S(2)}, u32[]{:S(2)}) collective-permute-start(bf16[1,1,16,16,128]{4,3,2,1,0:T(8,128)(2,1)S(1)} %slice.3), channel_id=1, source_target_pairs={{0,1},{1,2},{2,3},{3,4},{4,5},{5,6},{6,7},{8,9},{9,10},{10,11},{11... | collective-permute-start | bytes 196616 | tf_op jit(solution)/shard_map/ppermute | solution.py:665
  22.1 0.0 copy-start.5
  22.1 1.2 %copy-done.5 = bf16[1,16,16,16,128]{4,3,2,1,0:T(8,128)(2,1)S(1)} copy-done((bf16[1,16,16,16,128]{4,3,2,1,0:T(8,128)(2,1)S(1)}, bf16[1,16,16,16,128]{4,3,2,1,0:T(8,128)(2,1)}, u32[]{:S(2)}) %copy-start.5) | copy-done | bytes 1048600
  23.3 0.0 copy-start.7
  23.3 0.8 shard_map.69
  24.1 0.0 copy-start.1
  24.1 1.4 %copy-done.1 = bf16[9,2,8,64,128]{4,3,2,1,0:T(8,128)(2,1)} copy-done((bf16[9,2,8,64,128]{4,3,2,1,0:T(8,128)(2,1)}, bf16[9,2,8,64,128]{4,3,2,1,0:T(8,128)(2,1)S(1)}, u32[]{:S(2)}) %copy-start.1) | copy-done | bytes 2359320
  25.6 0.4 shard_map.68.own_ref
  26.0 0.0 collective-permute-done.2
  26.0 0.0 copy-done.7
  26.0 1.9 %add_convert_fusion = bf16[27,32,256]{2,1,0:T(8,128)(2,1)} fusion(f32[27,32,256]{2,1,0:T(8,128)S(1)} %copy-done.7, bf16[27,32,256]{2,1,0:T(8,128)(2,1)} %collective-permute-done.2), kind=kLoop, calls=%fused_computation.2 | loop fusion | flops 663552 | bytes 1769472 | tf_op jit(solution)/shard_map/convert_element_type | solution.py:633
  27.9 0.0 collective-permute-done.1
  27.9 2.0 %shard_map.70 = (bf16[9,2,8,64,128]{4,3,2,1,0:T(8,128)(2,1)S(1)}, f32[8,128]{1,0:T(8,128)S(1)}) custom-call(bf16[16,16,16,128]{3,2,1,0:T(8,128)(2,1)} %bitcast.7.volume_ref), custom_call_target="tpu_custom_call" | custom-call | flops 1000000 | bytes 4000000 | tf_op jit(solution)/shard_map/pallas_call | solution.py:319
  29.9 0.0 copy-start.3
  29.9 1.4 %copy-done.3 = bf16[9,2,8,64,128]{4,3,2,1,0:T(8,128)(2,1)} copy-done((bf16[9,2,8,64,128]{4,3,2,1,0:T(8,128)(2,1)}, bf16[9,2,8,64,128]{4,3,2,1,0:T(8,128)(2,1)S(1)}, u32[]{:S(2)}) %copy-start.3) | copy-done | bytes 2359320
  31.4 0.0 collective-permute-done
  31.4 3.3 %all-to-all-done.got_ref = bf16[8,480,128]{2,1,0:T(8,128)(2,1)S(1)} async-done(((bf16[8,480,128]{2,1,0:T(8,128)(2,1)}), bf16[8,480,128]{2,1,0:T(8,128)(2,1)S(1)}, u32[]{:S(2)}, u32[]{:S(2)}) %all-to-all-start) | async-done | bytes 983072 | tf_op jit(solution)/shard_map/all_to_all | solution.py:540
  34.7 0.1 shard_map.72.weight_ref
  34.8 0.1 collective-permute-start.3
  34.9 0.5 shard_map.73
  35.4 0.0 copy-start.2
  35.4 1.3 %collective-permute-done.3.other_ref = bf16[256,896]{1,0:T(8,128)(2,1)S(1)} collective-permute-done((bf16[256,896]{1,0:T(8,128)(2,1)S(1)}, bf16[256,896]{1,0:T(8,128)(2,1)S(1)}, u32[]{:S(2)}, u32[]{:S(2)}) %collective-permute-start.3) | collective-permute-done | bytes 458784 | tf_op jit(solution)/shard_map/ppermute | solution.py:536
  36.7 1.7 %shard_map.74 = bf16[8,128,128]{2,1,0:T(8,128)(2,1)} custom-call(f32[512,896]{1,0:T(8,128)S(1)} %get-tuple-element.26.first_ref, bf16[256,512]{1,0:T(8,128)(2,1)S(1)} %get-tuple-element.27.later_ref, bf16[256,896]{1,0:T(8,128)(2,1)S(1)} %collective-permute-done.3.other_ref, bf16[1024,128]{1,0:T(8,128)(2,1)S(1)} %shard_map.68.own_ref), custom_call_target="tpu_custom_call" | custom-call | flops 500000000 | bytes 3000000 | tf_op jit(solution)/shard_map/pallas_call | solution.py:242
  38.4 4.1 %all-to-all-start.1 = ((bf16[8,128,128]{2,1,0:T(8,128)(2,1)}), bf16[8,128,128]{2,1,0:T(8,128)(2,1)S(1)}, u32[]{:S(2)}, u32[]{:S(2)}) async-start(bf16[8,128,128]{2,1,0:T(8,128)(2,1)} %shard_map.74), calls=%async_computation.1 | async-start | bytes 524288 | tf_op jit(solution)/shard_map/all_to_all | solution.py:540
  42.5 1.5 %collective-permute-start.4 = (bf16[27,32,256]{2,1,0:T(8,128)(2,1)}, bf16[27,32,256]{2,1,0:T(8,128)(2,1)S(1)}, u32[]{:S(2)}, u32[]{:S(2)}) collective-permute-start(bf16[27,32,256]{2,1,0:T(8,128)(2,1)} %add_convert_fusion), channel_id=1, source_target_pairs={{0,16},{8,24},{16,0},{24,8},{1,17},{9,25},{17,1},{25,9},{2,18},{10... | collective-permute-start | bytes 1327112 | tf_op jit(solution)/shard_map/ppermute | solution.py:641
  44.0 0.0 collective-permute-start.6
  44.0 1.3 %collective-permute-done.6 = bf16[1,1,16,16,128]{4,3,2,1,0:T(8,128)(2,1)S(1)} collective-permute-done((bf16[1,1,16,16,128]{4,3,2,1,0:T(8,128)(2,1)S(1)}, bf16[1,1,16,16,128]{4,3,2,1,0:T(8,128)(2,1)S(1)}, u32[]{:S(2)}, u32[]{:S(2)}) %collective-permute-start.6) | collective-permute-done | bytes 65568 | tf_op jit(solution)/shard_map/ppermute | solution.py:536
  45.2 6.5 %all-to-all-done.1.got_ref = bf16[8,128,128]{2,1,0:T(8,128)(2,1)S(1)} async-done(((bf16[8,128,128]{2,1,0:T(8,128)(2,1)}), bf16[8,128,128]{2,1,0:T(8,128)(2,1)S(1)}, u32[]{:S(2)}, u32[]{:S(2)}) %all-to-all-start.1) | async-done | bytes 262176 | tf_op jit(solution)/shard_map/all_to_all | solution.py:540
  51.7 0.0 collective-permute-start.7
  51.7 0.0 copy-done.2
  51.7 0.0 copy-start.4
  51.7 0.9 %shard_map.75.total_ref = f32[7,256,256]{2,1,0:T(8,128)S(1)} custom-call(s32[1]{0:T(128)} %bitcast.core_ref, bf16[8,128,128]{2,1,0:T(8,128)(2,1)S(1)} %all-to-all-done.1.got_ref, bf16[9,2,8,64,128]{4,3,2,1,0:T(8,128)(2,1)S(1)} %copy-done.2, bf16[1,16,16,128]{3,2,1,0:T(8,128)(2,1)S(1)} %bitcast.25, f32[8,128]{1,0:T(8,128)S(1)} %add.15.done_ref), custom_call_target="tpu_custom_call" | custom-call | flops 500000000 | bytes 5000000 | tf_op jit(solution)/shard_map/pallas_call | solution.py:395
  52.7 0.6 collective-permute-done.7.other_ref
  53.2 0.1 copy-done.4
  53.4 1.8 %shard_map.76 = bf16[8,432,128]{2,1,0:T(8,128)(2,1)} custom-call(s32[1]{0:T(128)} %bitcast.core_ref, f32[7,256,256]{2,1,0:T(8,128)S(1)} %shard_map.75.total_ref, bf16[8,128,128]{2,1,0:T(8,128)(2,1)S(1)} %collective-permute-done.7.other_ref, bf16[9,2,8,64,128]{4,3,2,1,0:T(8,128)(2,1)S(1)} %copy-done.4, bf16[1,16,16,128]{3,2,1,0:T(8,128)(2,1)S(1)} %bitcast.26), custom_call_target="tpu_custom_call" | custom-call | flops 500000000 | bytes 5000000 | tf_op jit(solution)/shard_map/pallas_call | solution.py:439
  55.2 0.0 copy-start.9
  55.2 3.7 %all-to-all-start.2 = ((bf16[8,432,128]{2,1,0:T(8,128)(2,1)}), bf16[8,432,128]{2,1,0:T(8,128)(2,1)S(1)}, u32[]{:S(2)}, u32[]{:S(2)}) async-start(bf16[8,432,128]{2,1,0:T(8,128)(2,1)} %shard_map.76), calls=%async_computation.2 | async-start | bytes 1769472 | tf_op jit(solution)/shard_map/all_to_all | solution.py:540
  58.9 0.0 collective-permute-done.4
  58.9 0.0 copy-done.9
  58.9 0.1 add_multiply_fusion
  59.1 0.5 collective-permute-start.5
  59.6 1.1 %shard_map.78 = f32[8,8,8,256]{3,2,1,0:T(8,128)} custom-call(bf16[8,128,128]{2,1,0:T(8,128)(2,1)S(1)} %all-to-all-done.1.got_ref), custom_call_target="tpu_custom_call" | custom-call | flops 1000000 | bytes 2000000 | tf_op jit(solution)/shard_map/pallas_call | solution.py:279
  60.7 1.1 %collective-permute-done.5 = f32[27,32,256]{2,1,0:T(8,128)} collective-permute-done((f32[27,32,256]{2,1,0:T(8,128)S(1)}, f32[27,32,256]{2,1,0:T(8,128)}, u32[]{:S(2)}, u32[]{:S(2)}) %collective-permute-start.5) | collective-permute-done | bytes 884768 | tf_op jit(solution)/shard_map/ppermute | solution.py:536
  61.8 1.4 %broadcast_select_fusion.1 = (f32[27,32,256]{2,1,0:T(8,128)S(1)}, f32[27,32,256]{2,1,0:T(8,128)S(1)}) fusion(f32[27,32,256]{2,1,0:T(8,128)} %collective-permute-done.5, pred[]{:T(512)S(6)} %eq.7, bf16[27,32,256]{2,1,0:T(8,128)(2,1)S(1)} %collective-permute-done.4, bf16[27,32,256]{2,1,0:T(8,128)(2,1)S(1)} %copy-done.9), kind=kLoop, calls=%fused_computation.4 | loop fusion | flops 1327104 | bytes 3538945 | tf_op jit(solution)/shard_map/jit(_where)/select_n | solution.py:644
  63.2 1.3 %pad_maximum_fusion = f32[27,64,256]{2,1,0:T(8,128)} fusion(f32[27,32,256]{2,1,0:T(8,128)S(1)} %get-tuple-element.40, f32[27,32,256]{2,1,0:T(8,128)S(1)} %get-tuple-element.39), kind=kLoop, calls=%fused_computation | loop fusion | flops 442368 | bytes 3538944 | tf_op jit(solution)/shard_map/concatenate | solution.py:646
  64.6 17.4 %all-to-all-done.2 = bf16[8,432,128]{2,1,0:T(8,128)(2,1)S(1)} async-done(((bf16[8,432,128]{2,1,0:T(8,128)(2,1)}), bf16[8,432,128]{2,1,0:T(8,128)(2,1)S(1)}, u32[]{:S(2)}, u32[]{:S(2)}) %all-to-all-start.2) | async-done | bytes 884768 | tf_op jit(solution)/shard_map/all_to_all | solution.py:540
  82.0 0.1 reduce_sum.12
  82.1 6.7 %all-gather = bf16[1728,128]{1,0:T(8,128)(2,1)S(1)} all-gather(bf16[432,128]{1,0:T(8,128)(2,1)S(1)} %reduce_sum.12), channel_id=2, replica_groups=mesh['sample'=4,'chan'=8] {'sample'}, dimensions={0}, use_global_device_ids=true | all-gather | bytes 552960 | tf_op jit(solution)/shard_map/all_gather | solution.py:697
  88.9 0.8 shard_map.77
  (1 shorter events, 0.0 us)
Async XLA Ops:
  0.6 9.7 %copy-start = (bf16[1,64,8,8,256]{4,3,2,1,0:T(8,128)(2,1)S(1)}, bf16[1,64,8,8,256]{4,3,2,1,0:T(8,128)(2,1)}, u32[]{:S(2)}) copy-start(bf16[1,64,8,8,256]{4,3,2,1,0:T(8,128)(2,1)} %param.4) | copy-start | bytes 6291460
  0.7 9.7 %copy-start.8 = (bf16[1,32,4,4,64]{4,3,2,1,0:T(4,128)(2,1)S(1)}, bf16[1,32,4,4,64]{4,3,2,1,0:T(4,128)(2,1)}, u32[]{:S(2)}) copy-start(bf16[1,32,4,4,64]{4,3,2,1,0:T(4,128)(2,1)} %param.5) | copy-start | bytes 196612
  3.0 31.7 %all-to-all-start = ((bf16[8,480,128]{2,1,0:T(8,128)(2,1)}), bf16[8,480,128]{2,1,0:T(8,128)(2,1)S(1)}, u32[]{:S(2)}, u32[]{:S(2)}) async-start(bf16[8,480,128]{2,1,0:T(8,128)(2,1)} %shard_map.67), calls=%async_computation | async-start | bytes 1966080 | tf_op jit(solution)/shard_map/all_to_all | solution.py:540
  10.3 17.6 %collective-permute-start.1 = (bf16[1,16,16,16,128]{4,3,2,1,0:T(8,128)(2,1)}, bf16[1,16,16,16,128]{4,3,2,1,0:T(8,128)(2,1)}, u32[]{:S(2)}, u32[]{:S(2)}) collective-permute-start(bf16[1,16,16,16,128]{4,3,2,1,0:T(8,128)(2,1)} %param.7), channel_id=1, source_target_pairs={{0,8},{8,0},{16,24},{24,16},{1,9},{9,1},{17,25},{25,17},{2,10},{10... | collective-permute-start | bytes 3145736 | tf_op jit(solution)/shard_map/ppermute | solution.py:536
  15.9 0.9 %copy-start.6 = (f32[27,32,256]{2,1,0:T(8,128)}, f32[27,32,256]{2,1,0:T(8,128)S(1)}, u32[]{:S(2)}) copy-start(f32[27,32,256]{2,1,0:T(8,128)S(1)} %get-tuple-element.23) | copy-start | bytes 2654212
  16.9 9.1 %collective-permute-start.2 = (bf16[27,32,256]{2,1,0:T(8,128)(2,1)}, bf16[27,32,256]{2,1,0:T(8,128)(2,1)}, u32[]{:S(2)}, u32[]{:S(2)}) collective-permute-start(bf16[27,32,256]{2,1,0:T(8,128)(2,1)} %get-tuple-element.24), channel_id=1, source_target_pairs={{0,8},{8,0},{16,24},{24,16},{1,9},{9,1},{17,25},{25,17},{2,10},{10... | collective-permute-start | bytes 1327112 | tf_op jit(solution)/shard_map/ppermute | solution.py:536
  18.2 13.2 %collective-permute-start = (bf16[1,1,16,16,128]{4,3,2,1,0:T(8,128)(2,1)S(1)}, bf16[1,1,16,16,128]{4,3,2,1,0:T(8,128)(2,1)S(1)}, u32[]{:S(2)}, u32[]{:S(2)}) collective-permute-start(bf16[1,1,16,16,128]{4,3,2,1,0:T(8,128)(2,1)S(1)} %slice.3), channel_id=1, source_target_pairs={{0,1},{1,2},{2,3},{3,4},{4,5},{5,6},{6,7},{8,9},{9,10},{10,11},{11... | collective-permute-start | bytes 196616 | tf_op jit(solution)/shard_map/ppermute | solution.py:665
  22.1 1.2 %copy-start.5 = (bf16[1,16,16,16,128]{4,3,2,1,0:T(8,128)(2,1)S(1)}, bf16[1,16,16,16,128]{4,3,2,1,0:T(8,128)(2,1)}, u32[]{:S(2)}) copy-start(bf16[1,16,16,16,128]{4,3,2,1,0:T(8,128)(2,1)} %param.7) | copy-start | bytes 3145732
  23.3 2.6 %copy-start.7 = (f32[27,32,256]{2,1,0:T(8,128)S(1)}, f32[27,32,256]{2,1,0:T(8,128)}, u32[]{:S(2)}) copy-start(f32[27,32,256]{2,1,0:T(8,128)} %copy-done.6) | copy-start | bytes 2654212
  24.1 1.4 %copy-start.1 = (bf16[9,2,8,64,128]{4,3,2,1,0:T(8,128)(2,1)}, bf16[9,2,8,64,128]{4,3,2,1,0:T(8,128)(2,1)S(1)}, u32[]{:S(2)}) copy-start(bf16[9,2,8,64,128]{4,3,2,1,0:T(8,128)(2,1)S(1)} %get-tuple-element.35.window) | copy-start | bytes 7077892
  29.9 1.4 %copy-start.3 = (bf16[9,2,8,64,128]{4,3,2,1,0:T(8,128)(2,1)}, bf16[9,2,8,64,128]{4,3,2,1,0:T(8,128)(2,1)S(1)}, u32[]{:S(2)}) copy-start(bf16[9,2,8,64,128]{4,3,2,1,0:T(8,128)(2,1)S(1)} %get-tuple-element.37.window) | copy-start | bytes 7077892
  34.8 1.9 %collective-permute-start.3 = (bf16[256,896]{1,0:T(8,128)(2,1)S(1)}, bf16[256,896]{1,0:T(8,128)(2,1)S(1)}, u32[]{:S(2)}, u32[]{:S(2)}) collective-permute-start(bf16[256,896]{1,0:T(8,128)(2,1)S(1)} %shard_map.72.weight_ref), channel_id=1, source_target_pairs={{0,8},{8,0},{16,24},{24,16},{1,9},{9,1},{17,25},{25,17},{2,10},{10... | collective-permute-start | bytes 1376264 | tf_op jit(solution)/shard_map/ppermute | solution.py:536
  35.4 16.3 %copy-start.2 = (bf16[9,2,8,64,128]{4,3,2,1,0:T(8,128)(2,1)S(1)}, bf16[9,2,8,64,128]{4,3,2,1,0:T(8,128)(2,1)}, u32[]{:S(2)}) copy-start(bf16[9,2,8,64,128]{4,3,2,1,0:T(8,128)(2,1)} %copy-done.1) | copy-start | bytes 7077892
  38.4 13.3 %all-to-all-start.1 = ((bf16[8,128,128]{2,1,0:T(8,128)(2,1)}), bf16[8,128,128]{2,1,0:T(8,128)(2,1)S(1)}, u32[]{:S(2)}, u32[]{:S(2)}) async-start(bf16[8,128,128]{2,1,0:T(8,128)(2,1)} %shard_map.74), calls=%async_computation.1 | async-start | bytes 524288 | tf_op jit(solution)/shard_map/all_to_all | solution.py:540
  42.5 16.4 %collective-permute-start.4 = (bf16[27,32,256]{2,1,0:T(8,128)(2,1)}, bf16[27,32,256]{2,1,0:T(8,128)(2,1)S(1)}, u32[]{:S(2)}, u32[]{:S(2)}) collective-permute-start(bf16[27,32,256]{2,1,0:T(8,128)(2,1)} %add_convert_fusion), channel_id=1, source_target_pairs={{0,16},{8,24},{16,0},{24,8},{1,17},{9,25},{17,1},{25,9},{2,18},{10... | collective-permute-start | bytes 1327112 | tf_op jit(solution)/shard_map/ppermute | solution.py:641
  44.0 1.3 %collective-permute-start.6 = (bf16[1,1,16,16,128]{4,3,2,1,0:T(8,128)(2,1)S(1)}, bf16[1,1,16,16,128]{4,3,2,1,0:T(8,128)(2,1)S(1)}, u32[]{:S(2)}, u32[]{:S(2)}) collective-permute-start(bf16[1,1,16,16,128]{4,3,2,1,0:T(8,128)(2,1)S(1)} %collective-permute-done), channel_id=1, source_target_pairs={{0,8},{8,0},{16,24},{24,16},{1,9},{9,1},{17,25},{25,17},{2,10},{10... | collective-permute-start | bytes 196616 | tf_op jit(solution)/shard_map/ppermute | solution.py:536
  51.7 1.5 %collective-permute-start.7 = (bf16[8,128,128]{2,1,0:T(8,128)(2,1)S(1)}, bf16[8,128,128]{2,1,0:T(8,128)(2,1)S(1)}, u32[]{:S(2)}, u32[]{:S(2)}) collective-permute-start(bf16[8,128,128]{2,1,0:T(8,128)(2,1)S(1)} %all-to-all-done.1.got_ref), channel_id=1, source_target_pairs={{0,8},{8,0},{16,24},{24,16},{1,9},{9,1},{17,25},{25,17},{2,10},{10... | collective-permute-start | bytes 786440 | tf_op jit(solution)/shard_map/ppermute | solution.py:536
  51.7 1.7 %copy-start.4 = (bf16[9,2,8,64,128]{4,3,2,1,0:T(8,128)(2,1)S(1)}, bf16[9,2,8,64,128]{4,3,2,1,0:T(8,128)(2,1)}, u32[]{:S(2)}) copy-start(bf16[9,2,8,64,128]{4,3,2,1,0:T(8,128)(2,1)} %copy-done.3) | copy-start | bytes 7077892
  55.2 3.8 %copy-start.9 = (bf16[27,32,256]{2,1,0:T(8,128)(2,1)S(1)}, bf16[27,32,256]{2,1,0:T(8,128)(2,1)}, u32[]{:S(2)}) copy-start(bf16[27,32,256]{2,1,0:T(8,128)(2,1)} %add_convert_fusion) | copy-start | bytes 1327108
  55.2 26.8 %all-to-all-start.2 = ((bf16[8,432,128]{2,1,0:T(8,128)(2,1)}), bf16[8,432,128]{2,1,0:T(8,128)(2,1)S(1)}, u32[]{:S(2)}, u32[]{:S(2)}) async-start(bf16[8,432,128]{2,1,0:T(8,128)(2,1)} %shard_map.76), calls=%async_computation.2 | async-start | bytes 1769472 | tf_op jit(solution)/shard_map/all_to_all | solution.py:540
  59.1 2.7 %collective-permute-start.5 = (f32[27,32,256]{2,1,0:T(8,128)S(1)}, f32[27,32,256]{2,1,0:T(8,128)}, u32[]{:S(2)}, u32[]{:S(2)}) collective-permute-start(f32[27,32,256]{2,1,0:T(8,128)S(1)} %add_multiply_fusion), channel_id=1, source_target_pairs={{0,8},{8,0},{16,24},{24,16},{1,9},{9,1},{17,25},{25,17},{2,10},{10... | collective-permute-start | bytes 2654216 | tf_op jit(solution)/shard_map/ppermute | solution.py:536

commit v5 on v4

--- a/solution.py
+++ b/solution.py
@@ -198,23 +198,21 @@
     for n in range(shards):
         sums = [None, None]
         for col in range(3):
-            shift = 1 if col == 0 else 0
-            base = n * chunk + shift
 
             def piece(group, offset):
-                return products[pl.ds(base + offset, chunk), pl.ds(group * 128, 128)]
+                return products[pl.ds(n * chunk + offset, chunk), pl.ds(group * 128, 128)]
 
             part = piece(col, 0)
             part = part + jnp.where(slots >= 2, piece(3 + col, plane_step), 0.0)
-            by_row = piece(3 + col, row_step)
+            by_row = piece(3 + col, 0)
             moved = pltpu.roll(by_row, 96, 1)
-            corner = piece(6, plane_step + row_step)
+            corner = piece(6, plane_step)
             if col > 0:
                 corner = pltpu.roll(corner, 32 * col, 1)
             rows = jnp.where(slots == 1, by_row, jnp.where(slots == 3, moved + corner, 0.0))
-            part = part + jnp.where(last_row, 0.0, rows)
-            if shift:
-                part = jnp.where(last_col, 0.0, part)
+            part = part + jnp.where(last_row, 0.0, pltpu.roll(rows, chunk - row_step, 0))
+            if col == 0:
+                part = jnp.where(last_col, 0.0, pltpu.roll(part, chunk - 1, 0))
             to = 0 if col == 1 else 1
             sums[to] = part if sums[to] is None else sums[to] + part
         joined[pl.ds(0, chunk, stride=2), :] = sums[0]
@@ -372,12 +370,14 @@
     return jnp.concatenate(both, axis=1)
 
 
-def lower_first_kernel(core_ref, got_ref, window, rim_ref, done_ref, total_ref, cells, flat, first_cells):
+def lower_first_kernel(
+    core_ref, got_ref, window, rim_ref, other_rim_ref, done_ref, total_ref, other_cells, cells, flat, first_cells
+):
     del done_ref
+    rim_cells(other_rim_ref, flat, other_cells)
     rim_cells(rim_ref, flat, first_cells)
     side = cotangent_side(got_ref, cells)
-    count = total_ref.shape[0]
-    for pair in range(count):
+    for pair in range(total_ref.shape[0]):
         taps = tap_pair(window, first_cells, core_ref[0], pair)
         total_ref[pair] = jnp.dot(side, taps, preferred_element_type=wide)
 
@@ -390,21 +390,23 @@
     ]
 
 
-def lower_first(core, got, window, rim, done, grid):
+def lower_first(core, got, window, rim, other_rim, done, grid):
     middle = 32 * got.shape[0]
     return pl.pallas_call(
         lower_first_kernel,
-        out_shape=jax.ShapeDtypeStruct((7, middle, 2 * window.shape[4]), wide),
-        in_specs=[scalar, whole, whole, whole, whole],
-        out_specs=whole,
+        out_shape=(
+            jax.ShapeDtypeStruct((7, middle, 2 * window.shape[4]), wide),
+            jax.ShapeDtypeStruct((9, *window.shape[3:]), low),
+        ),
+        in_specs=[scalar, whole, whole, whole, whole, whole],
+        out_specs=(whole, whole),
         scratch_shapes=lower_scratch(grid, middle, window, rim),
         compiler_params=params,
         cost_estimate=pl.CostEstimate(flops=5 * 10**8, bytes_accessed=5 * 10**6, transcendentals=0),
-    )(core, got, window, rim, done)
-
-
-def lower_kernel(core_ref, total_ref, other_ref, window, rim_ref, sent_ref, cells, flat, first_cells, staged, left):
-    rim_cells(rim_ref, flat, first_cells)
+    )(core, got, window, rim, other_rim, done)
+
+
+def lower_kernel(core_ref, total_ref, other_ref, window, first_cells, sent_ref, cells, staged, left):
     side = cotangent_side(other_ref, cells)
     shards = staged.shape[0]
     below = window.shape[4]
@@ -432,7 +434,7 @@
         copy.wait()
 
 
-def lower_terms(core, total, other, window, rim, grid):
+def lower_terms(core, total, other, window, first_cells, grid):
     shards = other.shape[0]
     pairs, middle, _ = total.shape
     shape = (shards, 27 * window.shape[4] // shards, 128)
@@ -441,11 +443,14 @@
         out_shape=pltpu.HBM(shape, low),
         in_specs=[scalar, whole, whole, whole, whole],
         out_specs=anywhere,
-        scratch_shapes=lower_scratch(grid, middle, window, rim)
-        + [pltpu.VMEM(shape, low), pltpu.SemaphoreType.DMA((pairs,))],
+        scratch_shapes=[
+            pltpu.VMEM((*grid, middle), wide),
+            pltpu.VMEM(shape, low),
+            pltpu.SemaphoreType.DMA((pairs,)),
+        ],
         compiler_params=params,
         cost_estimate=pl.CostEstimate(flops=5 * 10**8, bytes_accessed=5 * 10**6, transcendentals=0),
-    )(core, total, other, window, rim)
+    )(core, total, other, window, first_cells)
 
 
 def total_kernel(shares_ref, total_ref, *, scale):
@@ -690,8 +695,8 @@
 
     other_cot = partner(cot_got, "sample", 1)
     slab_grid = (slab, *volume_64.shape[1:3])
-    own_terms = lower_first(cores, cot_got, window, rim[0], done, slab_grid)
-    terms = lower_terms(cores, own_terms, other_cot, other_window, other_rim[0], slab_grid)
+    own_terms, below_other = lower_first(cores, cot_got, window, rim[0], other_rim[0], done, slab_grid)
+    terms = lower_terms(cores, own_terms, other_cot, other_window, below_other, slab_grid)
     share = jnp.sum(exchange(terms, "chan").astype(wide), axis=0)
     cot_full = unpack(cot_got, slab_grid)
     shares = lax.all_gather(share.astype(low), "sample", axis=0)

time: 90.3 us -> 89.7 us (level)
  no operation moved by 1% of the time
where the time goes in v5:
time: 89.7 us; the launch traced here: 89 us
  waiting for transfers between devices  31.4 us (35%)
  starting transfers between devices  21.1 us (24%)
  Pallas kernels  18 us (20%)
  blocking collectives  6.73 us (8%)
  local copies, waits for them, and re-layouts  5.99 us (7%)
  other arithmetic  4.95 us (6%)
    all_to_all x3, waiting for transfers between devices, exchange(): return lax.all_to_all(blocks, axis, split_axis=0, concat_axis=0, tiled=True)  26.9 us
    all_to_all x3, starting transfers between devices, exchange(): return lax.all_to_all(blocks, axis, split_axis=0, concat_axis=0, tiled=True)  15.1 us
    all_gather x1, blocking collectives, body(): shares = lax.all_gather(share.astype(low), 'sample', axis=0)  6.73 us
    pallas_call x1, Pallas kernels, upper_terms(): pl.pallas_call(upper_kernel, out_shape=(jax.ShapeDtypeStruct(shape, wide)...  5.58 us
    unnamed x20, local copies, waits for them, and re-layouts  5.15 us
    ppermute x6, waiting for transfers between devices, partner(): return lax.ppermute(array, axis, [(i, i ^ by) for i in range(size)])  4.51 us
    ppermute x1, starting transfers between devices, body(): lax.ppermute(act_128[:, -1:], 'chan', [(i, i + 1) for i in range(shards -...  3.91 us
    pallas_call x2, Pallas kernels, windows(): pl.pallas_call(window_kernel, out_shape=(jax.ShapeDtypeStruct(shape, low)...  2.77 us
  transfers between devices with their start and end apart: 11, of which 7 were waited for; matrix products, arithmetic and copies ran while one was open for 6% of the time, Pallas kernels for 15%

profile of v5, /device:TPU:0, one launch (start us, length us, event | category | flops | bytes accessed | tf_op | source)
XLA Modules:
  0.0 89.0 jit_solution(10461744107923482782)
XLA Ops:
  0.6 0.0 copy-start
  0.7 0.0 copy-start.8
  0.7 2.4 %shard_map.67 = bf16[8,480,128]{2,1,0:T(8,128)(2,1)} custom-call(s32[1]{0:T(128)} %bitcast.core_ref, bf16[27,64,256]{2,1,0:T(8,128)(2,1)} %bitcast.28, bf16[512,64]{1,0:T(8,128)(2,1)} %bitcast.23), custom_call_target="tpu_custom_call" | custom-call | flops 1000000 | bytes 3000000 | tf_op jit(solution)/shard_map/pallas_call | solution.py:88
  3.0 7.3 %all-to-all-start = ((bf16[8,480,128]{2,1,0:T(8,128)(2,1)}), bf16[8,480,128]{2,1,0:T(8,128)(2,1)S(1)}, u32[]{:S(2)}, u32[]{:S(2)}) async-start(bf16[8,480,128]{2,1,0:T(8,128)(2,1)} %shard_map.67), calls=%async_computation | async-start | bytes 1966080 | tf_op jit(solution)/shard_map/all_to_all | solution.py:545
  10.3 0.0 collective-permute-start.1
  10.3 0.0 copy-done
  10.3 0.0 copy-done.8
  10.4 5.6 %shard_map.71 = (f32[27,32,256]{2,1,0:T(8,128)S(1)}, bf16[27,32,256]{2,1,0:T(8,128)(2,1)}) custom-call(s32[1]{0:T(128)} %bitcast.core_ref, bf16[64,8,8,256]{3,2,1,0:T(8,128)(2,1)S(1)} %bitcast.19, bf16[32,4,4,64]{3,2,1,0:T(4,128)(2,1)S(1)} %bitcast.24), custom_call_target="tpu_custom_call" | custom-call | flops 500000000 | bytes 6000000 | tf_op jit(solution)/shard_map/pallas_call | solution.py:523
  15.9 0.0 copy-start.6
  15.9 0.9 %copy-done.6 = f32[27,32,256]{2,1,0:T(8,128)} copy-done((f32[27,32,256]{2,1,0:T(8,128)}, f32[27,32,256]{2,1,0:T(8,128)S(1)}, u32[]{:S(2)}) %copy-start.6) | copy-done | bytes 884760
  16.9 0.5 collective-permute-start.2
  17.3 0.8 slice.3
  18.2 3.9 %collective-permute-start = (bf16[1,1,16,16,128]{4,3,2,1,0:T(8,128)(2,1)S(1)}, bf16[1,1,16,16,128]{4,3,2,1,0:T(8,128)(2,1)S(1)}, u32[]{:S(2)}, u32[]{:S(2)}) collective-permute-start(bf16[1,1,16,16,128]{4,3,2,1,0:T(8,128)(2,1)S(1)} %slice.3), channel_id=1, source_target_pairs={{0,1},{1,2},{2,3},{3,4},{4,5},{5,6},{6,7},{8,9},{9,10},{10,11},{11... | collective-permute-start | bytes 196616 | tf_op jit(solution)/shard_map/ppermute | solution.py:670
  22.1 0.0 copy-start.5
  22.1 1.2 %copy-done.5 = bf16[1,16,16,16,128]{4,3,2,1,0:T(8,128)(2,1)S(1)} copy-done((bf16[1,16,16,16,128]{4,3,2,1,0:T(8,128)(2,1)S(1)}, bf16[1,16,16,16,128]{4,3,2,1,0:T(8,128)(2,1)}, u32[]{:S(2)}) %copy-start.5) | copy-done | bytes 1048600
  23.3 0.0 copy-start.7
  23.3 0.8 shard_map.69
  24.1 0.0 copy-start.1
  24.1 1.4 %copy-done.1 = bf16[9,2,8,64,128]{4,3,2,1,0:T(8,128)(2,1)} copy-done((bf16[9,2,8,64,128]{4,3,2,1,0:T(8,128)(2,1)}, bf16[9,2,8,64,128]{4,3,2,1,0:T(8,128)(2,1)S(1)}, u32[]{:S(2)}) %copy-start.1) | copy-done | bytes 2359320
  25.6 0.4 shard_map.68.own_ref
  26.0 0.0 collective-permute-done.2
  26.0 0.0 copy-done.7
  26.0 1.9 %add_convert_fusion = bf16[27,32,256]{2,1,0:T(8,128)(2,1)} fusion(f32[27,32,256]{2,1,0:T(8,128)S(1)} %copy-done.7, bf16[27,32,256]{2,1,0:T(8,128)(2,1)} %collective-permute-done.2), kind=kLoop, calls=%fused_computation.2 | loop fusion | flops 663552 | bytes 1769472 | tf_op jit(solution)/shard_map/convert_element_type | solution.py:638
  27.9 0.0 collective-permute-done.1
  27.9 2.0 %shard_map.70 = (bf16[9,2,8,64,128]{4,3,2,1,0:T(8,128)(2,1)S(1)}, f32[8,128]{1,0:T(8,128)S(1)}) custom-call(bf16[16,16,16,128]{3,2,1,0:T(8,128)(2,1)} %bitcast.7.volume_ref), custom_call_target="tpu_custom_call" | custom-call | flops 1000000 | bytes 4000000 | tf_op jit(solution)/shard_map/pallas_call | solution.py:317
  29.9 0.0 copy-start.3
  29.9 1.4 %copy-done.3 = bf16[9,2,8,64,128]{4,3,2,1,0:T(8,128)(2,1)} copy-done((bf16[9,2,8,64,128]{4,3,2,1,0:T(8,128)(2,1)}, bf16[9,2,8,64,128]{4,3,2,1,0:T(8,128)(2,1)S(1)}, u32[]{:S(2)}) %copy-start.3) | copy-done | bytes 2359320
  31.3 0.0 collective-permute-done
  31.3 3.4 %all-to-all-done.got_ref = bf16[8,480,128]{2,1,0:T(8,128)(2,1)S(1)} async-done(((bf16[8,480,128]{2,1,0:T(8,128)(2,1)}), bf16[8,480,128]{2,1,0:T(8,128)(2,1)S(1)}, u32[]{:S(2)}, u32[]{:S(2)}) %all-to-all-start) | async-done | bytes 983072 | tf_op jit(solution)/shard_map/all_to_all | solution.py:545
  34.7 0.1 shard_map.72.weight_ref
  34.8 0.1 collective-permute-start.3
  34.9 0.5 shard_map.73
  35.4 0.0 copy-start.2
  35.4 1.3 %collective-permute-done.3.other_ref = bf16[256,896]{1,0:T(8,128)(2,1)S(1)} collective-permute-done((bf16[256,896]{1,0:T(8,128)(2,1)S(1)}, bf16[256,896]{1,0:T(8,128)(2,1)S(1)}, u32[]{:S(2)}, u32[]{:S(2)}) %collective-permute-start.3) | collective-permute-done | bytes 458784 | tf_op jit(solution)/shard_map/ppermute | solution.py:541
  36.7 1.5 %shard_map.74 = bf16[8,128,128]{2,1,0:T(8,128)(2,1)} custom-call(f32[512,896]{1,0:T(8,128)S(1)} %get-tuple-element.28.first_ref, bf16[256,512]{1,0:T(8,128)(2,1)S(1)} %get-tuple-element.29.later_ref, bf16[256,896]{1,0:T(8,128)(2,1)S(1)} %collective-permute-done.3.other_ref, bf16[1024,128]{1,0:T(8,128)(2,1)S(1)} %shard_map.68.own_ref), custom_call_target="tpu_custom_call" | custom-call | flops 500000000 | bytes 3000000 | tf_op jit(solution)/shard_map/pallas_call | solution.py:240
  38.2 4.1 %all-to-all-start.1 = ((bf16[8,128,128]{2,1,0:T(8,128)(2,1)}), bf16[8,128,128]{2,1,0:T(8,128)(2,1)S(1)}, u32[]{:S(2)}, u32[]{:S(2)}) async-start(bf16[8,128,128]{2,1,0:T(8,128)(2,1)} %shard_map.74), calls=%async_computation.1 | async-start | bytes 524288 | tf_op jit(solution)/shard_map/all_to_all | solution.py:545
  42.3 1.5 %collective-permute-start.4 = (bf16[27,32,256]{2,1,0:T(8,128)(2,1)}, bf16[27,32,256]{2,1,0:T(8,128)(2,1)S(1)}, u32[]{:S(2)}, u32[]{:S(2)}) collective-permute-start(bf16[27,32,256]{2,1,0:T(8,128)(2,1)} %add_convert_fusion), channel_id=1, source_target_pairs={{0,16},{8,24},{16,0},{24,8},{1,17},{9,25},{17,1},{25,9},{2,18},{10... | collective-permute-start | bytes 1327112 | tf_op jit(solution)/shard_map/ppermute | solution.py:646
  43.8 0.0 collective-permute-start.6
  43.8 1.3 %collective-permute-done.6 = bf16[1,1,16,16,128]{4,3,2,1,0:T(8,128)(2,1)S(1)} collective-permute-done((bf16[1,1,16,16,128]{4,3,2,1,0:T(8,128)(2,1)S(1)}, bf16[1,1,16,16,128]{4,3,2,1,0:T(8,128)(2,1)S(1)}, u32[]{:S(2)}, u32[]{:S(2)}) %collective-permute-start.6) | collective-permute-done | bytes 65568 | tf_op jit(solution)/shard_map/ppermute | solution.py:541
  45.1 6.5 %all-to-all-done.1.got_ref = bf16[8,128,128]{2,1,0:T(8,128)(2,1)S(1)} async-done(((bf16[8,128,128]{2,1,0:T(8,128)(2,1)}), bf16[8,128,128]{2,1,0:T(8,128)(2,1)S(1)}, u32[]{:S(2)}, u32[]{:S(2)}) %all-to-all-start.1) | async-done | bytes 262176 | tf_op jit(solution)/shard_map/all_to_all | solution.py:545
  51.5 0.0 copy-start.4
  51.5 0.0 collective-permute-start.7
  51.5 0.0 copy-done.2
  51.5 1.0 %shard_map.75 = (f32[7,256,256]{2,1,0:T(8,128)S(1)}, bf16[9,64,128]{2,1,0:T(8,128)(2,1)S(1)}) custom-call(s32[1]{0:T(128)} %bitcast.core_ref, bf16[8,128,128]{2,1,0:T(8,128)(2,1)S(1)} %all-to-all-done.1.got_ref, bf16[9,2,8,64,128]{4,3,2,1,0:T(8,128)(2,1)S(1)} %copy-done.2, bf16[1,16,16,128]{3,2,1,0:T(8,128)(2,1)S(1)} %bitcast.25, ...), custom_call_target="tpu_custom_call" | custom-call | flops 500000000 | bytes 5000000 | tf_op jit(solution)/shard_map/pallas_call | solution.py:395
  52.5 0.6 collective-permute-done.7.other_ref
  53.1 0.1 copy-done.4
  53.2 1.8 %shard_map.76 = bf16[8,432,128]{2,1,0:T(8,128)(2,1)} custom-call(s32[1]{0:T(128)} %bitcast.core_ref, f32[7,256,256]{2,1,0:T(8,128)S(1)} %get-tuple-element.40.total_ref, bf16[8,128,128]{2,1,0:T(8,128)(2,1)S(1)} %collective-permute-done.7.other_ref, bf16[9,2,8,64,128]{4,3,2,1,0:T(8,128)(2,1)S(1)} %copy-done.4, ...), custom_call_target="tpu_custom_call" | custom-call | flops 500000000 | bytes 5000000 | tf_op jit(solution)/shard_map/pallas_call | solution.py:441
  55.0 0.0 copy-start.9
  55.0 3.7 %all-to-all-start.2 = ((bf16[8,432,128]{2,1,0:T(8,128)(2,1)}), bf16[8,432,128]{2,1,0:T(8,128)(2,1)S(1)}, u32[]{:S(2)}, u32[]{:S(2)}) async-start(bf16[8,432,128]{2,1,0:T(8,128)(2,1)} %shard_map.76), calls=%async_computation.2 | async-start | bytes 1769472 | tf_op jit(solution)/shard_map/all_to_all | solution.py:545
  58.8 0.0 collective-permute-done.4
  58.8 0.0 copy-done.9
  58.8 0.1 add_multiply_fusion
  58.9 0.1 collective-permute-start.5
  59.0 1.1 %shard_map.78 = f32[8,8,8,256]{3,2,1,0:T(8,128)} custom-call(bf16[8,128,128]{2,1,0:T(8,128)(2,1)S(1)} %all-to-all-done.1.got_ref), custom_call_target="tpu_custom_call" | custom-call | flops 1000000 | bytes 2000000 | tf_op jit(solution)/shard_map/pallas_call | solution.py:277
  60.1 1.4 %collective-permute-done.5 = f32[27,32,256]{2,1,0:T(8,128)} collective-permute-done((f32[27,32,256]{2,1,0:T(8,128)S(1)}, f32[27,32,256]{2,1,0:T(8,128)}, u32[]{:S(2)}, u32[]{:S(2)}) %collective-permute-start.5) | collective-permute-done | bytes 884768 | tf_op jit(solution)/shard_map/ppermute | solution.py:541
  61.6 1.4 %broadcast_select_fusion.1 = (f32[27,32,256]{2,1,0:T(8,128)S(1)}, f32[27,32,256]{2,1,0:T(8,128)S(1)}) fusion(f32[27,32,256]{2,1,0:T(8,128)} %collective-permute-done.5, pred[]{:T(512)S(6)} %eq.7, bf16[27,32,256]{2,1,0:T(8,128)(2,1)S(1)} %collective-permute-done.4, bf16[27,32,256]{2,1,0:T(8,128)(2,1)S(1)} %copy-done.9), kind=kLoop, calls=%fused_computation.4 | loop fusion | flops 1327104 | bytes 3538945 | tf_op jit(solution)/shard_map/jit(_where)/select_n | solution.py:649
  63.0 1.3 %pad_maximum_fusion = f32[27,64,256]{2,1,0:T(8,128)} fusion(f32[27,32,256]{2,1,0:T(8,128)S(1)} %get-tuple-element.44, f32[27,32,256]{2,1,0:T(8,128)S(1)} %get-tuple-element.43), kind=kLoop, calls=%fused_computation | loop fusion | flops 442368 | bytes 3538944 | tf_op jit(solution)/shard_map/concatenate | solution.py:651
  64.3 17.0 %all-to-all-done.2 = bf16[8,432,128]{2,1,0:T(8,128)(2,1)S(1)} async-done(((bf16[8,432,128]{2,1,0:T(8,128)(2,1)}), bf16[8,432,128]{2,1,0:T(8,128)(2,1)S(1)}, u32[]{:S(2)}, u32[]{:S(2)}) %all-to-all-start.2) | async-done | bytes 884768 | tf_op jit(solution)/shard_map/all_to_all | solution.py:545
  81.4 0.1 reduce_sum.12
  81.5 6.7 %all-gather = bf16[1728,128]{1,0:T(8,128)(2,1)S(1)} all-gather(bf16[432,128]{1,0:T(8,128)(2,1)S(1)} %reduce_sum.12), channel_id=2, replica_groups=mesh['sample'=4,'chan'=8] {'sample'}, dimensions={0}, use_global_device_ids=true | all-gather | bytes 552960 | tf_op jit(solution)/shard_map/all_gather | solution.py:702
  88.2 0.8 shard_map.77
  (1 shorter events, 0.0 us)
Async XLA Ops:
  0.6 9.7 %copy-start = (bf16[1,64,8,8,256]{4,3,2,1,0:T(8,128)(2,1)S(1)}, bf16[1,64,8,8,256]{4,3,2,1,0:T(8,128)(2,1)}, u32[]{:S(2)}) copy-start(bf16[1,64,8,8,256]{4,3,2,1,0:T(8,128)(2,1)} %param.4) | copy-start | bytes 6291460
  0.7 9.7 %copy-start.8 = (bf16[1,32,4,4,64]{4,3,2,1,0:T(4,128)(2,1)S(1)}, bf16[1,32,4,4,64]{4,3,2,1,0:T(4,128)(2,1)}, u32[]{:S(2)}) copy-start(bf16[1,32,4,4,64]{4,3,2,1,0:T(4,128)(2,1)} %param.5) | copy-start | bytes 196612
  3.0 31.7 %all-to-all-start = ((bf16[8,480,128]{2,1,0:T(8,128)(2,1)}), bf16[8,480,128]{2,1,0:T(8,128)(2,1)S(1)}, u32[]{:S(2)}, u32[]{:S(2)}) async-start(bf16[8,480,128]{2,1,0:T(8,128)(2,1)} %shard_map.67), calls=%async_computation | async-start | bytes 1966080 | tf_op jit(solution)/shard_map/all_to_all | solution.py:545
  10.3 17.6 %collective-permute-start.1 = (bf16[1,16,16,16,128]{4,3,2,1,0:T(8,128)(2,1)}, bf16[1,16,16,16,128]{4,3,2,1,0:T(8,128)(2,1)}, u32[]{:S(2)}, u32[]{:S(2)}) collective-permute-start(bf16[1,16,16,16,128]{4,3,2,1,0:T(8,128)(2,1)} %param.7), channel_id=1, source_target_pairs={{0,8},{8,0},{16,24},{24,16},{1,9},{9,1},{17,25},{25,17},{2,10},{10... | collective-permute-start | bytes 3145736 | tf_op jit(solution)/shard_map/ppermute | solution.py:541
  15.9 0.9 %copy-start.6 = (f32[27,32,256]{2,1,0:T(8,128)}, f32[27,32,256]{2,1,0:T(8,128)S(1)}, u32[]{:S(2)}) copy-start(f32[27,32,256]{2,1,0:T(8,128)S(1)} %get-tuple-element.25) | copy-start | bytes 2654212
  16.9 9.1 %collective-permute-start.2 = (bf16[27,32,256]{2,1,0:T(8,128)(2,1)}, bf16[27,32,256]{2,1,0:T(8,128)(2,1)}, u32[]{:S(2)}, u32[]{:S(2)}) collective-permute-start(bf16[27,32,256]{2,1,0:T(8,128)(2,1)} %get-tuple-element.26), channel_id=1, source_target_pairs={{0,8},{8,0},{16,24},{24,16},{1,9},{9,1},{17,25},{25,17},{2,10},{10... | collective-permute-start | bytes 1327112 | tf_op jit(solution)/shard_map/ppermute | solution.py:541
  18.2 13.2 %collective-permute-start = (bf16[1,1,16,16,128]{4,3,2,1,0:T(8,128)(2,1)S(1)}, bf16[1,1,16,16,128]{4,3,2,1,0:T(8,128)(2,1)S(1)}, u32[]{:S(2)}, u32[]{:S(2)}) collective-permute-start(bf16[1,1,16,16,128]{4,3,2,1,0:T(8,128)(2,1)S(1)} %slice.3), channel_id=1, source_target_pairs={{0,1},{1,2},{2,3},{3,4},{4,5},{5,6},{6,7},{8,9},{9,10},{10,11},{11... | collective-permute-start | bytes 196616 | tf_op jit(solution)/shard_map/ppermute | solution.py:670
  22.1 1.2 %copy-start.5 = (bf16[1,16,16,16,128]{4,3,2,1,0:T(8,128)(2,1)S(1)}, bf16[1,16,16,16,128]{4,3,2,1,0:T(8,128)(2,1)}, u32[]{:S(2)}) copy-start(bf16[1,16,16,16,128]{4,3,2,1,0:T(8,128)(2,1)} %param.7) | copy-start | bytes 3145732
  23.3 2.6 %copy-start.7 = (f32[27,32,256]{2,1,0:T(8,128)S(1)}, f32[27,32,256]{2,1,0:T(8,128)}, u32[]{:S(2)}) copy-start(f32[27,32,256]{2,1,0:T(8,128)} %copy-done.6) | copy-start | bytes 2654212
  24.1 1.4 %copy-start.1 = (bf16[9,2,8,64,128]{4,3,2,1,0:T(8,128)(2,1)}, bf16[9,2,8,64,128]{4,3,2,1,0:T(8,128)(2,1)S(1)}, u32[]{:S(2)}) copy-start(bf16[9,2,8,64,128]{4,3,2,1,0:T(8,128)(2,1)S(1)} %get-tuple-element.37.window) | copy-start | bytes 7077892
  29.9 1.4 %copy-start.3 = (bf16[9,2,8,64,128]{4,3,2,1,0:T(8,128)(2,1)}, bf16[9,2,8,64,128]{4,3,2,1,0:T(8,128)(2,1)S(1)}, u32[]{:S(2)}) copy-start(bf16[9,2,8,64,128]{4,3,2,1,0:T(8,128)(2,1)S(1)} %get-tuple-element.41.window) | copy-start | bytes 7077892
  34.8 1.9 %collective-permute-start.3 = (bf16[256,896]{1,0:T(8,128)(2,1)S(1)}, bf16[256,896]{1,0:T(8,128)(2,1)S(1)}, u32[]{:S(2)}, u32[]{:S(2)}) collective-permute-start(bf16[256,896]{1,0:T(8,128)(2,1)S(1)} %shard_map.72.weight_ref), channel_id=1, source_target_pairs={{0,8},{8,0},{16,24},{24,16},{1,9},{9,1},{17,25},{25,17},{2,10},{10... | collective-permute-start | bytes 1376264 | tf_op jit(solution)/shard_map/ppermute | solution.py:541
  35.4 16.1 %copy-start.2 = (bf16[9,2,8,64,128]{4,3,2,1,0:T(8,128)(2,1)S(1)}, bf16[9,2,8,64,128]{4,3,2,1,0:T(8,128)(2,1)}, u32[]{:S(2)}) copy-start(bf16[9,2,8,64,128]{4,3,2,1,0:T(8,128)(2,1)} %copy-done.1) | copy-start | bytes 7077892
  38.2 13.3 %all-to-all-start.1 = ((bf16[8,128,128]{2,1,0:T(8,128)(2,1)}), bf16[8,128,128]{2,1,0:T(8,128)(2,1)S(1)}, u32[]{:S(2)}, u32[]{:S(2)}) async-start(bf16[8,128,128]{2,1,0:T(8,128)(2,1)} %shard_map.74), calls=%async_computation.1 | async-start | bytes 524288 | tf_op jit(solution)/shard_map/all_to_all | solution.py:545
  42.3 16.4 %collective-permute-start.4 = (bf16[27,32,256]{2,1,0:T(8,128)(2,1)}, bf16[27,32,256]{2,1,0:T(8,128)(2,1)S(1)}, u32[]{:S(2)}, u32[]{:S(2)}) collective-permute-start(bf16[27,32,256]{2,1,0:T(8,128)(2,1)} %add_convert_fusion), channel_id=1, source_target_pairs={{0,16},{8,24},{16,0},{24,8},{1,17},{9,25},{17,1},{25,9},{2,18},{10... | collective-permute-start | bytes 1327112 | tf_op jit(solution)/shard_map/ppermute | solution.py:646
  43.8 1.3 %collective-permute-start.6 = (bf16[1,1,16,16,128]{4,3,2,1,0:T(8,128)(2,1)S(1)}, bf16[1,1,16,16,128]{4,3,2,1,0:T(8,128)(2,1)S(1)}, u32[]{:S(2)}, u32[]{:S(2)}) collective-permute-start(bf16[1,1,16,16,128]{4,3,2,1,0:T(8,128)(2,1)S(1)} %collective-permute-done), channel_id=1, source_target_pairs={{0,8},{8,0},{16,24},{24,16},{1,9},{9,1},{17,25},{25,17},{2,10},{10... | collective-permute-start | bytes 196616 | tf_op jit(solution)/shard_map/ppermute | solution.py:541
  51.5 1.7 %copy-start.4 = (bf16[9,2,8,64,128]{4,3,2,1,0:T(8,128)(2,1)S(1)}, bf16[9,2,8,64,128]{4,3,2,1,0:T(8,128)(2,1)}, u32[]{:S(2)}) copy-start(bf16[9,2,8,64,128]{4,3,2,1,0:T(8,128)(2,1)} %copy-done.3) | copy-start | bytes 7077892
  51.5 1.5 %collective-permute-start.7 = (bf16[8,128,128]{2,1,0:T(8,128)(2,1)S(1)}, bf16[8,128,128]{2,1,0:T(8,128)(2,1)S(1)}, u32[]{:S(2)}, u32[]{:S(2)}) collective-permute-start(bf16[8,128,128]{2,1,0:T(8,128)(2,1)S(1)} %all-to-all-done.1.got_ref), channel_id=1, source_target_pairs={{0,8},{8,0},{16,24},{24,16},{1,9},{9,1},{17,25},{25,17},{2,10},{10... | collective-permute-start | bytes 786440 | tf_op jit(solution)/shard_map/ppermute | solution.py:541
  55.0 3.8 %copy-start.9 = (bf16[27,32,256]{2,1,0:T(8,128)(2,1)S(1)}, bf16[27,32,256]{2,1,0:T(8,128)(2,1)}, u32[]{:S(2)}) copy-start(bf16[27,32,256]{2,1,0:T(8,128)(2,1)} %add_convert_fusion) | copy-start | bytes 1327108
  55.0 26.3 %all-to-all-start.2 = ((bf16[8,432,128]{2,1,0:T(8,128)(2,1)}), bf16[8,432,128]{2,1,0:T(8,128)(2,1)S(1)}, u32[]{:S(2)}, u32[]{:S(2)}) async-start(bf16[8,432,128]{2,1,0:T(8,128)(2,1)} %shard_map.76), calls=%async_computation.2 | async-start | bytes 1769472 | tf_op jit(solution)/shard_map/all_to_all | solution.py:545
  58.9 2.6 %collective-permute-start.5 = (f32[27,32,256]{2,1,0:T(8,128)S(1)}, f32[27,32,256]{2,1,0:T(8,128)}, u32[]{:S(2)}, u32[]{:S(2)}) collective-permute-start(f32[27,32,256]{2,1,0:T(8,128)S(1)} %add_multiply_fusion), channel_id=1, source_target_pairs={{0,8},{8,0},{16,24},{24,16},{1,9},{9,1},{17,25},{25,17},{2,10},{10... | collective-permute-start | bytes 2654216 | tf_op jit(solution)/shard_map/ppermute | solution.py:541

commit v6 on v5

--- a/solution.py
+++ b/solution.py
@@ -113,7 +113,7 @@
             block = volume_ref[:, depth_par, :, row_par].astype(wide).reshape(rows, 128)
             block = pltpu.roll(block, (slot - part + 4) % 4 * 32, 1)
             joined = block if joined is None else jnp.where(slots == slot, block, joined)
-    own_ref[...] = joined.astype(low)
+    own_ref[...] = jnp.where(joined > 0, 1.0, leak_slope)
 
 
 def own_signs(position, volume):
@@ -122,7 +122,7 @@
     count = planes * rows * columns // 4
     return pl.pallas_call(
         sign_kernel,
-        out_shape=jax.ShapeDtypeStruct((count, 128), low),
+        out_shape=jax.ShapeDtypeStruct((count, 128), wide),
         grid_spec=pltpu.PrefetchScalarGridSpec(
             num_scalar_prefetch=1,
             grid=(1,),
@@ -218,7 +218,7 @@
         joined[pl.ds(0, chunk, stride=2), :] = sums[0]
         joined[pl.ds(1, chunk, stride=2), :] = sums[1]
         span = pl.ds(n * 2 * chunk, 2 * chunk)
-        slope = jnp.where(own_ref[span, :].astype(wide) > 0, 1.0, leak_slope)
+        slope = own_ref[span, :]
         sent_ref[n] = (joined[...] * slope).astype(low)
 
 
@@ -346,7 +346,7 @@
             for z in range(planes // 2):
                 for y in range(height // 2):
                     cells[2 * z + slot // 2, 2 * y + slot % 2, :, pl.ds(tile * 128, 128)] = joined[z, y]
-    return cells[...].reshape(planes * height * columns, middle).T.astype(low)
+    return cells[...].reshape(planes * height * columns, middle).astype(low).T
 
 
 def rim_cells(rim_ref, flat, first_cells):
@@ -415,7 +415,7 @@
     for pair in range(total_ref.shape[0]):
         taps = tap_pair(window, first_cells, core_ref[0], pair)
         total = total_ref[pair] + jnp.dot(side, taps, preferred_element_type=wide)
-        total = total.T.astype(low)
+        total = total.astype(low).T
         count = 0
         for n in (2 * pair, 2 * pair + 1):
             rows = total[n % 2 * below : (n % 2 + 1) * below]

time: 89.7 us -> 89.5 us (level)
    unnamed x20 -> x24, local copies, waits for them, and re-layouts: 5.15 us -> 5.16 us
  transfers between devices with their start and end apart: 11 -> 11, of which waited for: 7 -> 7; matrix products, arithmetic and copies ran while one was open for 6% -> 7% of each run, Pallas kernels for 15% -> 15%
where the time goes in v6:
time: 89.5 us; the launch traced here: 88.9 us
  waiting for transfers between devices  31.2 us (35%)
  starting transfers between devices  21.1 us (24%)
  Pallas kernels  17.9 us (20%)
  blocking collectives  6.73 us (8%)
  local copies, waits for them, and re-layouts  6 us (7%)
  other arithmetic  5.13 us (6%)
    all_to_all x3, waiting for transfers between devices, exchange(): return lax.all_to_all(blocks, axis, split_axis=0, concat_axis=0, tiled=True)  26.6 us
    all_to_all x3, starting transfers between devices, exchange(): return lax.all_to_all(blocks, axis, split_axis=0, concat_axis=0, tiled=True)  15.1 us
    all_gather x1, blocking collectives, body(): shares = lax.all_gather(share.astype(low), 'sample', axis=0)  6.73 us
    pallas_call x1, Pallas kernels, upper_terms(): pl.pallas_call(upper_kernel, out_shape=(jax.ShapeDtypeStruct(shape, wide)...  5.58 us
    unnamed x24, local copies, waits for them, and re-layouts  5.16 us
    ppermute x6, waiting for transfers between devices, partner(): return lax.ppermute(array, axis, [(i, i ^ by) for i in range(size)])  4.55 us
    ppermute x1, starting transfers between devices, body(): lax.ppermute(act_128[:, -1:], 'chan', [(i, i + 1) for i in range(shards -...  3.91 us
    pallas_call x2, Pallas kernels, windows(): pl.pallas_call(window_kernel, out_shape=(jax.ShapeDtypeStruct(shape, low)...  2.83 us
  transfers between devices with their start and end apart: 11, of which 7 were waited for; matrix products, arithmetic and copies ran while one was open for 7% of the time, Pallas kernels for 15%

profile of v6, /device:TPU:0, one launch (start us, length us, event | category | flops | bytes accessed | tf_op | source)
XLA Modules:
  0.0 88.9 jit_solution(16611389316237356877)
XLA Ops:
  0.6 0.0 copy-start
  0.7 0.0 copy-start.10
  0.7 2.4 %shard_map.67 = bf16[8,480,128]{2,1,0:T(8,128)(2,1)} custom-call(s32[1]{0:T(128)} %bitcast.core_ref, bf16[27,64,256]{2,1,0:T(8,128)(2,1)} %bitcast.28, bf16[512,64]{1,0:T(8,128)(2,1)} %bitcast.23), custom_call_target="tpu_custom_call" | custom-call | flops 1000000 | bytes 3000000 | tf_op jit(solution)/shard_map/pallas_call | solution.py:88
  3.0 7.3 %all-to-all-start = ((bf16[8,480,128]{2,1,0:T(8,128)(2,1)}), bf16[8,480,128]{2,1,0:T(8,128)(2,1)S(1)}, u32[]{:S(2)}, u32[]{:S(2)}) async-start(bf16[8,480,128]{2,1,0:T(8,128)(2,1)} %shard_map.67), calls=%async_computation | async-start | bytes 1966080 | tf_op jit(solution)/shard_map/all_to_all | solution.py:545
  10.3 0.0 collective-permute-start.1
  10.3 0.0 copy-done
  10.3 0.0 copy-done.10
  10.4 5.6 %shard_map.71 = (f32[27,32,256]{2,1,0:T(8,128)S(1)}, bf16[27,32,256]{2,1,0:T(8,128)(2,1)}) custom-call(s32[1]{0:T(128)} %bitcast.core_ref, bf16[64,8,8,256]{3,2,1,0:T(8,128)(2,1)S(1)} %bitcast.19, bf16[32,4,4,64]{3,2,1,0:T(4,128)(2,1)S(1)} %bitcast.24), custom_call_target="tpu_custom_call" | custom-call | flops 500000000 | bytes 6000000 | tf_op jit(solution)/shard_map/pallas_call | solution.py:523
  15.9 0.0 copy-start.8
  15.9 0.9 %copy-done.8 = f32[27,32,256]{2,1,0:T(8,128)} copy-done((f32[27,32,256]{2,1,0:T(8,128)}, f32[27,32,256]{2,1,0:T(8,128)S(1)}, u32[]{:S(2)}) %copy-start.8) | copy-done | bytes 884760
  16.9 0.5 collective-permute-start.2
  17.3 0.8 slice.3
  18.2 3.9 %collective-permute-start = (bf16[1,1,16,16,128]{4,3,2,1,0:T(8,128)(2,1)S(1)}, bf16[1,1,16,16,128]{4,3,2,1,0:T(8,128)(2,1)S(1)}, u32[]{:S(2)}, u32[]{:S(2)}) collective-permute-start(bf16[1,1,16,16,128]{4,3,2,1,0:T(8,128)(2,1)S(1)} %slice.3), channel_id=1, source_target_pairs={{0,1},{1,2},{2,3},{3,4},{4,5},{5,6},{6,7},{8,9},{9,10},{10,11},{11... | collective-permute-start | bytes 196616 | tf_op jit(solution)/shard_map/ppermute | solution.py:670
  22.1 0.0 copy-start.7
  22.1 1.2 %copy-done.7 = bf16[1,16,16,16,128]{4,3,2,1,0:T(8,128)(2,1)S(1)} copy-done((bf16[1,16,16,16,128]{4,3,2,1,0:T(8,128)(2,1)S(1)}, bf16[1,16,16,16,128]{4,3,2,1,0:T(8,128)(2,1)}, u32[]{:S(2)}) %copy-start.7) | copy-done | bytes 1048600
  23.3 0.0 copy-start.9
  23.3 0.8 shard_map.69
  24.1 0.0 copy-start.1
  24.1 1.4 %copy-done.1 = bf16[9,2,8,64,128]{4,3,2,1,0:T(8,128)(2,1)} copy-done((bf16[9,2,8,64,128]{4,3,2,1,0:T(8,128)(2,1)}, bf16[9,2,8,64,128]{4,3,2,1,0:T(8,128)(2,1)S(1)}, u32[]{:S(2)}) %copy-start.1) | copy-done | bytes 2359320
  25.5 0.4 shard_map.68.own_ref
  26.0 0.0 copy-start.5
  26.0 0.0 collective-permute-done.2
  26.0 0.0 copy-done.9
  26.0 2.1 %add_convert_fusion = bf16[27,32,256]{2,1,0:T(8,128)(2,1)} fusion(f32[27,32,256]{2,1,0:T(8,128)S(1)} %copy-done.9, bf16[27,32,256]{2,1,0:T(8,128)(2,1)} %collective-permute-done.2), kind=kLoop, calls=%fused_computation.2 | loop fusion | flops 663552 | bytes 1769472 | tf_op jit(solution)/shard_map/convert_element_type | solution.py:638
  28.1 0.0 collective-permute-done.1
  28.1 0.0 copy-done.5
  28.1 2.1 %shard_map.70 = (bf16[9,2,8,64,128]{4,3,2,1,0:T(8,128)(2,1)S(1)}, f32[8,128]{1,0:T(8,128)S(1)}) custom-call(bf16[16,16,16,128]{3,2,1,0:T(8,128)(2,1)} %bitcast.7.volume_ref), custom_call_target="tpu_custom_call" | custom-call | flops 1000000 | bytes 4000000 | tf_op jit(solution)/shard_map/pallas_call | solution.py:317
  30.2 0.0 copy-start.3
  30.2 1.4 %copy-done.3 = bf16[9,2,8,64,128]{4,3,2,1,0:T(8,128)(2,1)} copy-done((bf16[9,2,8,64,128]{4,3,2,1,0:T(8,128)(2,1)}, bf16[9,2,8,64,128]{4,3,2,1,0:T(8,128)(2,1)S(1)}, u32[]{:S(2)}) %copy-start.3) | copy-done | bytes 2359320
  31.6 0.0 collective-permute-done
  31.6 3.1 %all-to-all-done.got_ref = bf16[8,480,128]{2,1,0:T(8,128)(2,1)S(1)} async-done(((bf16[8,480,128]{2,1,0:T(8,128)(2,1)}), bf16[8,480,128]{2,1,0:T(8,128)(2,1)S(1)}, u32[]{:S(2)}, u32[]{:S(2)}) %all-to-all-start) | async-done | bytes 983072 | tf_op jit(solution)/shard_map/all_to_all | solution.py:545
  34.7 0.1 shard_map.72.weight_ref
  34.8 0.1 collective-permute-start.3
  34.9 0.5 shard_map.73
  35.4 1.3 %collective-permute-done.3.other_ref = bf16[256,896]{1,0:T(8,128)(2,1)S(1)} collective-permute-done((bf16[256,896]{1,0:T(8,128)(2,1)S(1)}, bf16[256,896]{1,0:T(8,128)(2,1)S(1)}, u32[]{:S(2)}, u32[]{:S(2)}) %collective-permute-start.3) | collective-permute-done | bytes 458784 | tf_op jit(solution)/shard_map/ppermute | solution.py:541
  36.7 0.0 copy-done.6
  36.7 0.0 copy-start.2
  36.7 1.5 %shard_map.74 = bf16[8,128,128]{2,1,0:T(8,128)(2,1)} custom-call(f32[512,896]{1,0:T(8,128)S(1)} %get-tuple-element.28.first_ref, bf16[256,512]{1,0:T(8,128)(2,1)S(1)} %get-tuple-element.29.later_ref, bf16[256,896]{1,0:T(8,128)(2,1)S(1)} %collective-permute-done.3.other_ref, f32[1024,128]{1,0:T(8,128)S(1)} %copy-done.6), custom_call_target="tpu_custom_call" | custom-call | flops 500000000 | bytes 3000000 | tf_op jit(solution)/shard_map/pallas_call | solution.py:240
  38.2 4.1 %all-to-all-start.1 = ((bf16[8,128,128]{2,1,0:T(8,128)(2,1)}), bf16[8,128,128]{2,1,0:T(8,128)(2,1)S(1)}, u32[]{:S(2)}, u32[]{:S(2)}) async-start(bf16[8,128,128]{2,1,0:T(8,128)(2,1)} %shard_map.74), calls=%async_computation.1 | async-start | bytes 524288 | tf_op jit(solution)/shard_map/all_to_all | solution.py:545
  42.3 1.5 %collective-permute-start.4 = (bf16[27,32,256]{2,1,0:T(8,128)(2,1)}, bf16[27,32,256]{2,1,0:T(8,128)(2,1)S(1)}, u32[]{:S(2)}, u32[]{:S(2)}) collective-permute-start(bf16[27,32,256]{2,1,0:T(8,128)(2,1)} %add_convert_fusion), channel_id=1, source_target_pairs={{0,16},{8,24},{16,0},{24,8},{1,17},{9,25},{17,1},{25,9},{2,18},{10... | collective-permute-start | bytes 1327112 | tf_op jit(solution)/shard_map/ppermute | solution.py:646
  43.8 0.0 collective-permute-start.6
  43.8 1.3 %collective-permute-done.6 = bf16[1,1,16,16,128]{4,3,2,1,0:T(8,128)(2,1)S(1)} collective-permute-done((bf16[1,1,16,16,128]{4,3,2,1,0:T(8,128)(2,1)S(1)}, bf16[1,1,16,16,128]{4,3,2,1,0:T(8,128)(2,1)S(1)}, u32[]{:S(2)}, u32[]{:S(2)}) %collective-permute-start.6) | collective-permute-done | bytes 65568 | tf_op jit(solution)/shard_map/ppermute | solution.py:541
  45.0 6.5 %all-to-all-done.1.got_ref = bf16[8,128,128]{2,1,0:T(8,128)(2,1)S(1)} async-done(((bf16[8,128,128]{2,1,0:T(8,128)(2,1)}), bf16[8,128,128]{2,1,0:T(8,128)(2,1)S(1)}, u32[]{:S(2)}, u32[]{:S(2)}) %all-to-all-start.1) | async-done | bytes 262176 | tf_op jit(solution)/shard_map/all_to_all | solution.py:545
  51.5 0.0 copy-start.4
  51.5 0.0 collective-permute-start.7
  51.5 0.0 copy-done.2
  51.5 0.9 %shard_map.75 = (f32[7,256,256]{2,1,0:T(8,128)S(1)}, bf16[9,64,128]{2,1,0:T(8,128)(2,1)S(1)}) custom-call(s32[1]{0:T(128)} %bitcast.core_ref, bf16[8,128,128]{2,1,0:T(8,128)(2,1)S(1)} %all-to-all-done.1.got_ref, bf16[9,2,8,64,128]{4,3,2,1,0:T(8,128)(2,1)S(1)} %copy-done.2, bf16[1,16,16,128]{3,2,1,0:T(8,128)(2,1)S(1)} %bitcast.25, ...), custom_call_target="tpu_custom_call" | custom-call | flops 500000000 | bytes 5000000 | tf_op jit(solution)/shard_map/pallas_call | solution.py:395
  52.5 0.6 collective-permute-done.7.other_ref
  53.1 0.1 copy-done.4
  53.2 1.7 %shard_map.76 = bf16[8,432,128]{2,1,0:T(8,128)(2,1)} custom-call(s32[1]{0:T(128)} %bitcast.core_ref, f32[7,256,256]{2,1,0:T(8,128)S(1)} %get-tuple-element.40.total_ref, bf16[8,128,128]{2,1,0:T(8,128)(2,1)S(1)} %collective-permute-done.7.other_ref, bf16[9,2,8,64,128]{4,3,2,1,0:T(8,128)(2,1)S(1)} %copy-done.4, ...), custom_call_target="tpu_custom_call" | custom-call | flops 500000000 | bytes 5000000 | tf_op jit(solution)/shard_map/pallas_call | solution.py:441
  54.9 0.0 copy-start.11
  54.9 3.7 %all-to-all-start.2 = ((bf16[8,432,128]{2,1,0:T(8,128)(2,1)}), bf16[8,432,128]{2,1,0:T(8,128)(2,1)S(1)}, u32[]{:S(2)}, u32[]{:S(2)}) async-start(bf16[8,432,128]{2,1,0:T(8,128)(2,1)} %shard_map.76), calls=%async_computation.2 | async-start | bytes 1769472 | tf_op jit(solution)/shard_map/all_to_all | solution.py:545
  58.6 0.0 collective-permute-done.4
  58.7 0.0 copy-done.11
  58.7 0.1 add_multiply_fusion
  58.8 0.1 collective-permute-start.5
  58.9 1.1 %shard_map.78 = f32[8,8,8,256]{3,2,1,0:T(8,128)} custom-call(bf16[8,128,128]{2,1,0:T(8,128)(2,1)S(1)} %all-to-all-done.1.got_ref), custom_call_target="tpu_custom_call" | custom-call | flops 1000000 | bytes 2000000 | tf_op jit(solution)/shard_map/pallas_call | solution.py:277
  60.0 1.4 %collective-permute-done.5 = f32[27,32,256]{2,1,0:T(8,128)} collective-permute-done((f32[27,32,256]{2,1,0:T(8,128)S(1)}, f32[27,32,256]{2,1,0:T(8,128)}, u32[]{:S(2)}, u32[]{:S(2)}) %collective-permute-start.5) | collective-permute-done | bytes 884768 | tf_op jit(solution)/shard_map/ppermute | solution.py:541
  61.4 1.4 %broadcast_select_fusion.1 = (f32[27,32,256]{2,1,0:T(8,128)S(1)}, f32[27,32,256]{2,1,0:T(8,128)S(1)}) fusion(f32[27,32,256]{2,1,0:T(8,128)} %collective-permute-done.5, pred[]{:T(512)S(6)} %eq.7, bf16[27,32,256]{2,1,0:T(8,128)(2,1)S(1)} %collective-permute-done.4, bf16[27,32,256]{2,1,0:T(8,128)(2,1)S(1)} %copy-done.11), kind=kLoop, calls=%fused_computation.4 | loop fusion | flops 1327104 | bytes 3538945 | tf_op jit(solution)/shard_map/jit(_where)/select_n | solution.py:649
  62.9 1.3 %pad_maximum_fusion = f32[27,64,256]{2,1,0:T(8,128)} fusion(f32[27,32,256]{2,1,0:T(8,128)S(1)} %get-tuple-element.44, f32[27,32,256]{2,1,0:T(8,128)S(1)} %get-tuple-element.43), kind=kLoop, calls=%fused_computation | loop fusion | flops 442368 | bytes 3538944 | tf_op jit(solution)/shard_map/concatenate | solution.py:651
  64.2 17.0 %all-to-all-done.2 = bf16[8,432,128]{2,1,0:T(8,128)(2,1)S(1)} async-done(((bf16[8,432,128]{2,1,0:T(8,128)(2,1)}), bf16[8,432,128]{2,1,0:T(8,128)(2,1)S(1)}, u32[]{:S(2)}, u32[]{:S(2)}) %all-to-all-start.2) | async-done | bytes 884768 | tf_op jit(solution)/shard_map/all_to_all | solution.py:545
  81.2 0.1 reduce_sum.12
  81.4 6.7 %all-gather = bf16[1728,128]{1,0:T(8,128)(2,1)S(1)} all-gather(bf16[432,128]{1,0:T(8,128)(2,1)S(1)} %reduce_sum.12), channel_id=2, replica_groups=mesh['sample'=4,'chan'=8] {'sample'}, dimensions={0}, use_global_device_ids=true | all-gather | bytes 552960 | tf_op jit(solution)/shard_map/all_gather | solution.py:702
  88.1 0.8 shard_map.77
  (2 shorter events, 0.0 us)
Async XLA Ops:
  0.6 9.7 %copy-start = (bf16[1,64,8,8,256]{4,3,2,1,0:T(8,128)(2,1)S(1)}, bf16[1,64,8,8,256]{4,3,2,1,0:T(8,128)(2,1)}, u32[]{:S(2)}) copy-start(bf16[1,64,8,8,256]{4,3,2,1,0:T(8,128)(2,1)} %param.4) | copy-start | bytes 6291460
  0.7 9.7 %copy-start.10 = (bf16[1,32,4,4,64]{4,3,2,1,0:T(4,128)(2,1)S(1)}, bf16[1,32,4,4,64]{4,3,2,1,0:T(4,128)(2,1)}, u32[]{:S(2)}) copy-start(bf16[1,32,4,4,64]{4,3,2,1,0:T(4,128)(2,1)} %param.5) | copy-start | bytes 196612
  3.0 31.7 %all-to-all-start = ((bf16[8,480,128]{2,1,0:T(8,128)(2,1)}), bf16[8,480,128]{2,1,0:T(8,128)(2,1)S(1)}, u32[]{:S(2)}, u32[]{:S(2)}) async-start(bf16[8,480,128]{2,1,0:T(8,128)(2,1)} %shard_map.67), calls=%async_computation | async-start | bytes 1966080 | tf_op jit(solution)/shard_map/all_to_all | solution.py:545
  10.3 17.8 %collective-permute-start.1 = (bf16[1,16,16,16,128]{4,3,2,1,0:T(8,128)(2,1)}, bf16[1,16,16,16,128]{4,3,2,1,0:T(8,128)(2,1)}, u32[]{:S(2)}, u32[]{:S(2)}) collective-permute-start(bf16[1,16,16,16,128]{4,3,2,1,0:T(8,128)(2,1)} %param.7), channel_id=1, source_target_pairs={{0,8},{8,0},{16,24},{24,16},{1,9},{9,1},{17,25},{25,17},{2,10},{10... | collective-permute-start | bytes 3145736 | tf_op jit(solution)/shard_map/ppermute | solution.py:541
  15.9 0.9 %copy-start.8 = (f32[27,32,256]{2,1,0:T(8,128)}, f32[27,32,256]{2,1,0:T(8,128)S(1)}, u32[]{:S(2)}) copy-start(f32[27,32,256]{2,1,0:T(8,128)S(1)} %get-tuple-element.25) | copy-start | bytes 2654212
  16.9 9.1 %collective-permute-start.2 = (bf16[27,32,256]{2,1,0:T(8,128)(2,1)}, bf16[27,32,256]{2,1,0:T(8,128)(2,1)}, u32[]{:S(2)}, u32[]{:S(2)}) collective-permute-start(bf16[27,32,256]{2,1,0:T(8,128)(2,1)} %get-tuple-element.26), channel_id=1, source_target_pairs={{0,8},{8,0},{16,24},{24,16},{1,9},{9,1},{17,25},{25,17},{2,10},{10... | collective-permute-start | bytes 1327112 | tf_op jit(solution)/shard_map/ppermute | solution.py:541
  18.2 13.4 %collective-permute-start = (bf16[1,1,16,16,128]{4,3,2,1,0:T(8,128)(2,1)S(1)}, bf16[1,1,16,16,128]{4,3,2,1,0:T(8,128)(2,1)S(1)}, u32[]{:S(2)}, u32[]{:S(2)}) collective-permute-start(bf16[1,1,16,16,128]{4,3,2,1,0:T(8,128)(2,1)S(1)} %slice.3), channel_id=1, source_target_pairs={{0,1},{1,2},{2,3},{3,4},{4,5},{5,6},{6,7},{8,9},{9,10},{10,11},{11... | collective-permute-start | bytes 196616 | tf_op jit(solution)/shard_map/ppermute | solution.py:670
  22.1 1.2 %copy-start.7 = (bf16[1,16,16,16,128]{4,3,2,1,0:T(8,128)(2,1)S(1)}, bf16[1,16,16,16,128]{4,3,2,1,0:T(8,128)(2,1)}, u32[]{:S(2)}) copy-start(bf16[1,16,16,16,128]{4,3,2,1,0:T(8,128)(2,1)} %param.7) | copy-start | bytes 3145732
  23.3 2.6 %copy-start.9 = (f32[27,32,256]{2,1,0:T(8,128)S(1)}, f32[27,32,256]{2,1,0:T(8,128)}, u32[]{:S(2)}) copy-start(f32[27,32,256]{2,1,0:T(8,128)} %copy-done.8) | copy-start | bytes 2654212
  24.1 1.4 %copy-start.1 = (bf16[9,2,8,64,128]{4,3,2,1,0:T(8,128)(2,1)}, bf16[9,2,8,64,128]{4,3,2,1,0:T(8,128)(2,1)S(1)}, u32[]{:S(2)}) copy-start(bf16[9,2,8,64,128]{4,3,2,1,0:T(8,128)(2,1)S(1)} %get-tuple-element.37.window) | copy-start | bytes 7077892
  26.0 2.1 %copy-start.5 = (f32[1024,128]{1,0:T(8,128)}, f32[1024,128]{1,0:T(8,128)S(1)}, u32[]{:S(2)}) copy-start(f32[1024,128]{1,0:T(8,128)S(1)} %shard_map.68.own_ref) | copy-start | bytes 1572868
  28.1 8.6 %copy-start.6 = (f32[1024,128]{1,0:T(8,128)S(1)}, f32[1024,128]{1,0:T(8,128)}, u32[]{:S(2)}) copy-start(f32[1024,128]{1,0:T(8,128)} %copy-done.5) | copy-start | bytes 1572868
  30.2 1.4 %copy-start.3 = (bf16[9,2,8,64,128]{4,3,2,1,0:T(8,128)(2,1)}, bf16[9,2,8,64,128]{4,3,2,1,0:T(8,128)(2,1)S(1)}, u32[]{:S(2)}) copy-start(bf16[9,2,8,64,128]{4,3,2,1,0:T(8,128)(2,1)S(1)} %get-tuple-element.41.window) | copy-start | bytes 7077892
  34.8 1.9 %collective-permute-start.3 = (bf16[256,896]{1,0:T(8,128)(2,1)S(1)}, bf16[256,896]{1,0:T(8,128)(2,1)S(1)}, u32[]{:S(2)}, u32[]{:S(2)}) collective-permute-start(bf16[256,896]{1,0:T(8,128)(2,1)S(1)} %shard_map.72.weight_ref), channel_id=1, source_target_pairs={{0,8},{8,0},{16,24},{24,16},{1,9},{9,1},{17,25},{25,17},{2,10},{10... | collective-permute-start | bytes 1376264 | tf_op jit(solution)/shard_map/ppermute | solution.py:541
  36.7 14.8 %copy-start.2 = (bf16[9,2,8,64,128]{4,3,2,1,0:T(8,128)(2,1)S(1)}, bf16[9,2,8,64,128]{4,3,2,1,0:T(8,128)(2,1)}, u32[]{:S(2)}) copy-start(bf16[9,2,8,64,128]{4,3,2,1,0:T(8,128)(2,1)} %copy-done.1) | copy-start | bytes 7077892
  38.2 13.3 %all-to-all-start.1 = ((bf16[8,128,128]{2,1,0:T(8,128)(2,1)}), bf16[8,128,128]{2,1,0:T(8,128)(2,1)S(1)}, u32[]{:S(2)}, u32[]{:S(2)}) async-start(bf16[8,128,128]{2,1,0:T(8,128)(2,1)} %shard_map.74), calls=%async_computation.1 | async-start | bytes 524288 | tf_op jit(solution)/shard_map/all_to_all | solution.py:545
  42.3 16.4 %collective-permute-start.4 = (bf16[27,32,256]{2,1,0:T(8,128)(2,1)}, bf16[27,32,256]{2,1,0:T(8,128)(2,1)S(1)}, u32[]{:S(2)}, u32[]{:S(2)}) collective-permute-start(bf16[27,32,256]{2,1,0:T(8,128)(2,1)} %add_convert_fusion), channel_id=1, source_target_pairs={{0,16},{8,24},{16,0},{24,8},{1,17},{9,25},{17,1},{25,9},{2,18},{10... | collective-permute-start | bytes 1327112 | tf_op jit(solution)/shard_map/ppermute | solution.py:646
  43.8 1.3 %collective-permute-start.6 = (bf16[1,1,16,16,128]{4,3,2,1,0:T(8,128)(2,1)S(1)}, bf16[1,1,16,16,128]{4,3,2,1,0:T(8,128)(2,1)S(1)}, u32[]{:S(2)}, u32[]{:S(2)}) collective-permute-start(bf16[1,1,16,16,128]{4,3,2,1,0:T(8,128)(2,1)S(1)} %collective-permute-done), channel_id=1, source_target_pairs={{0,8},{8,0},{16,24},{24,16},{1,9},{9,1},{17,25},{25,17},{2,10},{10... | collective-permute-start | bytes 196616 | tf_op jit(solution)/shard_map/ppermute | solution.py:541
  51.5 1.7 %copy-start.4 = (bf16[9,2,8,64,128]{4,3,2,1,0:T(8,128)(2,1)S(1)}, bf16[9,2,8,64,128]{4,3,2,1,0:T(8,128)(2,1)}, u32[]{:S(2)}) copy-start(bf16[9,2,8,64,128]{4,3,2,1,0:T(8,128)(2,1)} %copy-done.3) | copy-start | bytes 7077892
  51.5 1.5 %collective-permute-start.7 = (bf16[8,128,128]{2,1,0:T(8,128)(2,1)S(1)}, bf16[8,128,128]{2,1,0:T(8,128)(2,1)S(1)}, u32[]{:S(2)}, u32[]{:S(2)}) collective-permute-start(bf16[8,128,128]{2,1,0:T(8,128)(2,1)S(1)} %all-to-all-done.1.got_ref), channel_id=1, source_target_pairs={{0,8},{8,0},{16,24},{24,16},{1,9},{9,1},{17,25},{25,17},{2,10},{10... | collective-permute-start | bytes 786440 | tf_op jit(solution)/shard_map/ppermute | solution.py:541
  54.9 3.7 %copy-start.11 = (bf16[27,32,256]{2,1,0:T(8,128)(2,1)S(1)}, bf16[27,32,256]{2,1,0:T(8,128)(2,1)}, u32[]{:S(2)}) copy-start(bf16[27,32,256]{2,1,0:T(8,128)(2,1)} %add_convert_fusion) | copy-start | bytes 1327108
  54.9 26.3 %all-to-all-start.2 = ((bf16[8,432,128]{2,1,0:T(8,128)(2,1)}), bf16[8,432,128]{2,1,0:T(8,128)(2,1)S(1)}, u32[]{:S(2)}, u32[]{:S(2)}) async-start(bf16[8,432,128]{2,1,0:T(8,128)(2,1)} %shard_map.76), calls=%async_computation.2 | async-start | bytes 1769472 | tf_op jit(solution)/shard_map/all_to_all | solution.py:545
  58.8 2.6 %collective-permute-start.5 = (f32[27,32,256]{2,1,0:T(8,128)S(1)}, f32[27,32,256]{2,1,0:T(8,128)}, u32[]{:S(2)}, u32[]{:S(2)}) collective-permute-start(f32[27,32,256]{2,1,0:T(8,128)S(1)} %add_multiply_fusion), channel_id=1, source_target_pairs={{0,8},{8,0},{16,24},{24,16},{1,9},{9,1},{17,25},{25,17},{2,10},{10... | collective-permute-start | bytes 2654216 | tf_op jit(solution)/shard_map/ppermute | solution.py:541

commit v7 on v6

--- a/solution.py
+++ b/solution.py
@@ -243,7 +243,7 @@
         in_specs=[whole, whole, whole, whole],
         out_specs=whole,
         scratch_shapes=[
-            pltpu.VMEM((cells + 32, lanes), wide),
+            pltpu.VMEM((cells + grid[1] * grid[2], lanes), wide),
             pltpu.VMEM((2 * cells // shards, 128), wide),
         ],
         compiler_params=params,

time: 89.5 us -> 89.5 us (level)
  no operation moved by 1% of the time
where the time goes in v7:
time: 89.5 us; the launch traced here: 88.9 us
  waiting for transfers between devices  31.2 us (35%)
  starting transfers between devices  21.1 us (24%)
  Pallas kernels  17.9 us (20%)
  blocking collectives  6.73 us (8%)
  local copies, waits for them, and re-layouts  6 us (7%)
  other arithmetic  5.13 us (6%)
    all_to_all x3, waiting for transfers between devices, exchange(): return lax.all_to_all(blocks, axis, split_axis=0, concat_axis=0, tiled=True)  26.6 us
    all_to_all x3, starting transfers between devices, exchange(): return lax.all_to_all(blocks, axis, split_axis=0, concat_axis=0, tiled=True)  15.1 us
    all_gather x1, blocking collectives, body(): shares = lax.all_gather(share.astype(low), 'sample', axis=0)  6.73 us
    pallas_call x1, Pallas kernels, upper_terms(): pl.pallas_call(upper_kernel, out_shape=(jax.ShapeDtypeStruct(shape, wide)...  5.58 us
    unnamed x24, local copies, waits for them, and re-layouts  5.16 us
    ppermute x6, waiting for transfers between devices, partner(): return lax.ppermute(array, axis, [(i, i ^ by) for i in range(size)])  4.55 us
    ppermute x1, starting transfers between devices, body(): lax.ppermute(act_128[:, -1:], 'chan', [(i, i + 1) for i in range(shards -...  3.91 us
    pallas_call x2, Pallas kernels, windows(): pl.pallas_call(window_kernel, out_shape=(jax.ShapeDtypeStruct(shape, low)...  2.83 us
  transfers between devices with their start and end apart: 11, of which 7 were waited for; matrix products, arithmetic and copies ran while one was open for 7% of the time, Pallas kernels for 15%

profile of v7, /device:TPU:0, one launch (start us, length us, event | category | flops | bytes accessed | tf_op | source)
XLA Modules:
  0.0 88.9 jit_solution(16611389316237356877)
XLA Ops:
  0.6 0.0 copy-start
  0.7 0.0 copy-start.10
  0.7 2.4 %shard_map.67 = bf16[8,480,128]{2,1,0:T(8,128)(2,1)} custom-call(s32[1]{0:T(128)} %bitcast.core_ref, bf16[27,64,256]{2,1,0:T(8,128)(2,1)} %bitcast.28, bf16[512,64]{1,0:T(8,128)(2,1)} %bitcast.23), custom_call_target="tpu_custom_call" | custom-call | flops 1000000 | bytes 3000000 | tf_op jit(solution)/shard_map/pallas_call | solution.py:88
  3.0 7.3 %all-to-all-start = ((bf16[8,480,128]{2,1,0:T(8,128)(2,1)}), bf16[8,480,128]{2,1,0:T(8,128)(2,1)S(1)}, u32[]{:S(2)}, u32[]{:S(2)}) async-start(bf16[8,480,128]{2,1,0:T(8,128)(2,1)} %shard_map.67), calls=%async_computation | async-start | bytes 1966080 | tf_op jit(solution)/shard_map/all_to_all | solution.py:545
  10.3 0.0 collective-permute-start.1
  10.3 0.0 copy-done
  10.3 0.0 copy-done.10
  10.4 5.6 %shard_map.71 = (f32[27,32,256]{2,1,0:T(8,128)S(1)}, bf16[27,32,256]{2,1,0:T(8,128)(2,1)}) custom-call(s32[1]{0:T(128)} %bitcast.core_ref, bf16[64,8,8,256]{3,2,1,0:T(8,128)(2,1)S(1)} %bitcast.19, bf16[32,4,4,64]{3,2,1,0:T(4,128)(2,1)S(1)} %bitcast.24), custom_call_target="tpu_custom_call" | custom-call | flops 500000000 | bytes 6000000 | tf_op jit(solution)/shard_map/pallas_call | solution.py:523
  15.9 0.0 copy-start.8
  15.9 0.9 %copy-done.8 = f32[27,32,256]{2,1,0:T(8,128)} copy-done((f32[27,32,256]{2,1,0:T(8,128)}, f32[27,32,256]{2,1,0:T(8,128)S(1)}, u32[]{:S(2)}) %copy-start.8) | copy-done | bytes 884760
  16.9 0.5 collective-permute-start.2
  17.3 0.8 slice.3
  18.2 3.9 %collective-permute-start = (bf16[1,1,16,16,128]{4,3,2,1,0:T(8,128)(2,1)S(1)}, bf16[1,1,16,16,128]{4,3,2,1,0:T(8,128)(2,1)S(1)}, u32[]{:S(2)}, u32[]{:S(2)}) collective-permute-start(bf16[1,1,16,16,128]{4,3,2,1,0:T(8,128)(2,1)S(1)} %slice.3), channel_id=1, source_target_pairs={{0,1},{1,2},{2,3},{3,4},{4,5},{5,6},{6,7},{8,9},{9,10},{10,11},{11... | collective-permute-start | bytes 196616 | tf_op jit(solution)/shard_map/ppermute | solution.py:670
  22.1 0.0 copy-start.7
  22.1 1.2 %copy-done.7 = bf16[1,16,16,16,128]{4,3,2,1,0:T(8,128)(2,1)S(1)} copy-done((bf16[1,16,16,16,128]{4,3,2,1,0:T(8,128)(2,1)S(1)}, bf16[1,16,16,16,128]{4,3,2,1,0:T(8,128)(2,1)}, u32[]{:S(2)}) %copy-start.7) | copy-done | bytes 1048600
  23.3 0.0 copy-start.9
  23.3 0.8 shard_map.69
  24.1 0.0 copy-start.1
  24.1 1.4 %copy-done.1 = bf16[9,2,8,64,128]{4,3,2,1,0:T(8,128)(2,1)} copy-done((bf16[9,2,8,64,128]{4,3,2,1,0:T(8,128)(2,1)}, bf16[9,2,8,64,128]{4,3,2,1,0:T(8,128)(2,1)S(1)}, u32[]{:S(2)}) %copy-start.1) | copy-done | bytes 2359320
  25.5 0.4 shard_map.68.own_ref
  26.0 0.0 copy-start.5
  26.0 0.0 collective-permute-done.2
  26.0 0.0 copy-done.9
  26.0 2.1 %add_convert_fusion = bf16[27,32,256]{2,1,0:T(8,128)(2,1)} fusion(f32[27,32,256]{2,1,0:T(8,128)S(1)} %copy-done.9, bf16[27,32,256]{2,1,0:T(8,128)(2,1)} %collective-permute-done.2), kind=kLoop, calls=%fused_computation.2 | loop fusion | flops 663552 | bytes 1769472 | tf_op jit(solution)/shard_map/convert_element_type | solution.py:638
  28.1 0.0 collective-permute-done.1
  28.1 0.0 copy-done.5
  28.1 2.1 %shard_map.70 = (bf16[9,2,8,64,128]{4,3,2,1,0:T(8,128)(2,1)S(1)}, f32[8,128]{1,0:T(8,128)S(1)}) custom-call(bf16[16,16,16,128]{3,2,1,0:T(8,128)(2,1)} %bitcast.7.volume_ref), custom_call_target="tpu_custom_call" | custom-call | flops 1000000 | bytes 4000000 | tf_op jit(solution)/shard_map/pallas_call | solution.py:317
  30.2 0.0 copy-start.3
  30.2 1.4 %copy-done.3 = bf16[9,2,8,64,128]{4,3,2,1,0:T(8,128)(2,1)} copy-done((bf16[9,2,8,64,128]{4,3,2,1,0:T(8,128)(2,1)}, bf16[9,2,8,64,128]{4,3,2,1,0:T(8,128)(2,1)S(1)}, u32[]{:S(2)}) %copy-start.3) | copy-done | bytes 2359320
  31.6 0.0 collective-permute-done
  31.6 3.1 %all-to-all-done.got_ref = bf16[8,480,128]{2,1,0:T(8,128)(2,1)S(1)} async-done(((bf16[8,480,128]{2,1,0:T(8,128)(2,1)}), bf16[8,480,128]{2,1,0:T(8,128)(2,1)S(1)}, u32[]{:S(2)}, u32[]{:S(2)}) %all-to-all-start) | async-done | bytes 983072 | tf_op jit(solution)/shard_map/all_to_all | solution.py:545
  34.7 0.1 shard_map.72.weight_ref
  34.8 0.1 collective-permute-start.3
  34.9 0.5 shard_map.73
  35.4 1.3 %collective-permute-done.3.other_ref = bf16[256,896]{1,0:T(8,128)(2,1)S(1)} collective-permute-done((bf16[256,896]{1,0:T(8,128)(2,1)S(1)}, bf16[256,896]{1,0:T(8,128)(2,1)S(1)}, u32[]{:S(2)}, u32[]{:S(2)}) %collective-permute-start.3) | collective-permute-done | bytes 458784 | tf_op jit(solution)/shard_map/ppermute | solution.py:541
  36.7 0.0 copy-done.6
  36.7 0.0 copy-start.2
  36.7 1.5 %shard_map.74 = bf16[8,128,128]{2,1,0:T(8,128)(2,1)} custom-call(f32[512,896]{1,0:T(8,128)S(1)} %get-tuple-element.28.first_ref, bf16[256,512]{1,0:T(8,128)(2,1)S(1)} %get-tuple-element.29.later_ref, bf16[256,896]{1,0:T(8,128)(2,1)S(1)} %collective-permute-done.3.other_ref, f32[1024,128]{1,0:T(8,128)S(1)} %copy-done.6), custom_call_target="tpu_custom_call" | custom-call | flops 500000000 | bytes 3000000 | tf_op jit(solution)/shard_map/pallas_call | solution.py:240
  38.2 4.1 %all-to-all-start.1 = ((bf16[8,128,128]{2,1,0:T(8,128)(2,1)}), bf16[8,128,128]{2,1,0:T(8,128)(2,1)S(1)}, u32[]{:S(2)}, u32[]{:S(2)}) async-start(bf16[8,128,128]{2,1,0:T(8,128)(2,1)} %shard_map.74), calls=%async_computation.1 | async-start | bytes 524288 | tf_op jit(solution)/shard_map/all_to_all | solution.py:545
  42.3 1.5 %collective-permute-start.4 = (bf16[27,32,256]{2,1,0:T(8,128)(2,1)}, bf16[27,32,256]{2,1,0:T(8,128)(2,1)S(1)}, u32[]{:S(2)}, u32[]{:S(2)}) collective-permute-start(bf16[27,32,256]{2,1,0:T(8,128)(2,1)} %add_convert_fusion), channel_id=1, source_target_pairs={{0,16},{8,24},{16,0},{24,8},{1,17},{9,25},{17,1},{25,9},{2,18},{10... | collective-permute-start | bytes 1327112 | tf_op jit(solution)/shard_map/ppermute | solution.py:646
  43.8 0.0 collective-permute-start.6
  43.8 1.3 %collective-permute-done.6 = bf16[1,1,16,16,128]{4,3,2,1,0:T(8,128)(2,1)S(1)} collective-permute-done((bf16[1,1,16,16,128]{4,3,2,1,0:T(8,128)(2,1)S(1)}, bf16[1,1,16,16,128]{4,3,2,1,0:T(8,128)(2,1)S(1)}, u32[]{:S(2)}, u32[]{:S(2)}) %collective-permute-start.6) | collective-permute-done | bytes 65568 | tf_op jit(solution)/shard_map/ppermute | solution.py:541
  45.0 6.5 %all-to-all-done.1.got_ref = bf16[8,128,128]{2,1,0:T(8,128)(2,1)S(1)} async-done(((bf16[8,128,128]{2,1,0:T(8,128)(2,1)}), bf16[8,128,128]{2,1,0:T(8,128)(2,1)S(1)}, u32[]{:S(2)}, u32[]{:S(2)}) %all-to-all-start.1) | async-done | bytes 262176 | tf_op jit(solution)/shard_map/all_to_all | solution.py:545
  51.5 0.0 copy-start.4
  51.5 0.0 collective-permute-start.7
  51.5 0.0 copy-done.2
  51.5 0.9 %shard_map.75 = (f32[7,256,256]{2,1,0:T(8,128)S(1)}, bf16[9,64,128]{2,1,0:T(8,128)(2,1)S(1)}) custom-call(s32[1]{0:T(128)} %bitcast.core_ref, bf16[8,128,128]{2,1,0:T(8,128)(2,1)S(1)} %all-to-all-done.1.got_ref, bf16[9,2,8,64,128]{4,3,2,1,0:T(8,128)(2,1)S(1)} %copy-done.2, bf16[1,16,16,128]{3,2,1,0:T(8,128)(2,1)S(1)} %bitcast.25, ...), custom_call_target="tpu_custom_call" | custom-call | flops 500000000 | bytes 5000000 | tf_op jit(solution)/shard_map/pallas_call | solution.py:395
  52.5 0.6 collective-permute-done.7.other_ref
  53.1 0.1 copy-done.4
  53.2 1.7 %shard_map.76 = bf16[8,432,128]{2,1,0:T(8,128)(2,1)} custom-call(s32[1]{0:T(128)} %bitcast.core_ref, f32[7,256,256]{2,1,0:T(8,128)S(1)} %get-tuple-element.40.total_ref, bf16[8,128,128]{2,1,0:T(8,128)(2,1)S(1)} %collective-permute-done.7.other_ref, bf16[9,2,8,64,128]{4,3,2,1,0:T(8,128)(2,1)S(1)} %copy-done.4, ...), custom_call_target="tpu_custom_call" | custom-call | flops 500000000 | bytes 5000000 | tf_op jit(solution)/shard_map/pallas_call | solution.py:441
  54.9 0.0 copy-start.11
  54.9 3.7 %all-to-all-start.2 = ((bf16[8,432,128]{2,1,0:T(8,128)(2,1)}), bf16[8,432,128]{2,1,0:T(8,128)(2,1)S(1)}, u32[]{:S(2)}, u32[]{:S(2)}) async-start(bf16[8,432,128]{2,1,0:T(8,128)(2,1)} %shard_map.76), calls=%async_computation.2 | async-start | bytes 1769472 | tf_op jit(solution)/shard_map/all_to_all | solution.py:545
  58.6 0.0 collective-permute-done.4
  58.7 0.0 copy-done.11
  58.7 0.1 add_multiply_fusion
  58.8 0.1 collective-permute-start.5
  58.9 1.1 %shard_map.78 = f32[8,8,8,256]{3,2,1,0:T(8,128)} custom-call(bf16[8,128,128]{2,1,0:T(8,128)(2,1)S(1)} %all-to-all-done.1.got_ref), custom_call_target="tpu_custom_call" | custom-call | flops 1000000 | bytes 2000000 | tf_op jit(solution)/shard_map/pallas_call | solution.py:277
  60.0 1.4 %collective-permute-done.5 = f32[27,32,256]{2,1,0:T(8,128)} collective-permute-done((f32[27,32,256]{2,1,0:T(8,128)S(1)}, f32[27,32,256]{2,1,0:T(8,128)}, u32[]{:S(2)}, u32[]{:S(2)}) %collective-permute-start.5) | collective-permute-done | bytes 884768 | tf_op jit(solution)/shard_map/ppermute | solution.py:541
  61.4 1.4 %broadcast_select_fusion.1 = (f32[27,32,256]{2,1,0:T(8,128)S(1)}, f32[27,32,256]{2,1,0:T(8,128)S(1)}) fusion(f32[27,32,256]{2,1,0:T(8,128)} %collective-permute-done.5, pred[]{:T(512)S(6)} %eq.7, bf16[27,32,256]{2,1,0:T(8,128)(2,1)S(1)} %collective-permute-done.4, bf16[27,32,256]{2,1,0:T(8,128)(2,1)S(1)} %copy-done.11), kind=kLoop, calls=%fused_computation.4 | loop fusion | flops 1327104 | bytes 3538945 | tf_op jit(solution)/shard_map/jit(_where)/select_n | solution.py:649
  62.9 1.3 %pad_maximum_fusion = f32[27,64,256]{2,1,0:T(8,128)} fusion(f32[27,32,256]{2,1,0:T(8,128)S(1)} %get-tuple-element.44, f32[27,32,256]{2,1,0:T(8,128)S(1)} %get-tuple-element.43), kind=kLoop, calls=%fused_computation | loop fusion | flops 442368 | bytes 3538944 | tf_op jit(solution)/shard_map/concatenate | solution.py:651
  64.2 17.0 %all-to-all-done.2 = bf16[8,432,128]{2,1,0:T(8,128)(2,1)S(1)} async-done(((bf16[8,432,128]{2,1,0:T(8,128)(2,1)}), bf16[8,432,128]{2,1,0:T(8,128)(2,1)S(1)}, u32[]{:S(2)}, u32[]{:S(2)}) %all-to-all-start.2) | async-done | bytes 884768 | tf_op jit(solution)/shard_map/all_to_all | solution.py:545
  81.2 0.1 reduce_sum.12
  81.4 6.7 %all-gather = bf16[1728,128]{1,0:T(8,128)(2,1)S(1)} all-gather(bf16[432,128]{1,0:T(8,128)(2,1)S(1)} %reduce_sum.12), channel_id=2, replica_groups=mesh['sample'=4,'chan'=8] {'sample'}, dimensions={0}, use_global_device_ids=true | all-gather | bytes 552960 | tf_op jit(solution)/shard_map/all_gather | solution.py:702
  88.1 0.8 shard_map.77
  (2 shorter events, 0.0 us)
Async XLA Ops:
  0.6 9.7 %copy-start = (bf16[1,64,8,8,256]{4,3,2,1,0:T(8,128)(2,1)S(1)}, bf16[1,64,8,8,256]{4,3,2,1,0:T(8,128)(2,1)}, u32[]{:S(2)}) copy-start(bf16[1,64,8,8,256]{4,3,2,1,0:T(8,128)(2,1)} %param.4) | copy-start | bytes 6291460
  0.7 9.7 %copy-start.10 = (bf16[1,32,4,4,64]{4,3,2,1,0:T(4,128)(2,1)S(1)}, bf16[1,32,4,4,64]{4,3,2,1,0:T(4,128)(2,1)}, u32[]{:S(2)}) copy-start(bf16[1,32,4,4,64]{4,3,2,1,0:T(4,128)(2,1)} %param.5) | copy-start | bytes 196612
  3.0 31.7 %all-to-all-start = ((bf16[8,480,128]{2,1,0:T(8,128)(2,1)}), bf16[8,480,128]{2,1,0:T(8,128)(2,1)S(1)}, u32[]{:S(2)}, u32[]{:S(2)}) async-start(bf16[8,480,128]{2,1,0:T(8,128)(2,1)} %shard_map.67), calls=%async_computation | async-start | bytes 1966080 | tf_op jit(solution)/shard_map/all_to_all | solution.py:545
  10.3 17.8 %collective-permute-start.1 = (bf16[1,16,16,16,128]{4,3,2,1,0:T(8,128)(2,1)}, bf16[1,16,16,16,128]{4,3,2,1,0:T(8,128)(2,1)}, u32[]{:S(2)}, u32[]{:S(2)}) collective-permute-start(bf16[1,16,16,16,128]{4,3,2,1,0:T(8,128)(2,1)} %param.7), channel_id=1, source_target_pairs={{0,8},{8,0},{16,24},{24,16},{1,9},{9,1},{17,25},{25,17},{2,10},{10... | collective-permute-start | bytes 3145736 | tf_op jit(solution)/shard_map/ppermute | solution.py:541
  15.9 0.9 %copy-start.8 = (f32[27,32,256]{2,1,0:T(8,128)}, f32[27,32,256]{2,1,0:T(8,128)S(1)}, u32[]{:S(2)}) copy-start(f32[27,32,256]{2,1,0:T(8,128)S(1)} %get-tuple-element.25) | copy-start | bytes 2654212
  16.9 9.1 %collective-permute-start.2 = (bf16[27,32,256]{2,1,0:T(8,128)(2,1)}, bf16[27,32,256]{2,1,0:T(8,128)(2,1)}, u32[]{:S(2)}, u32[]{:S(2)}) collective-permute-start(bf16[27,32,256]{2,1,0:T(8,128)(2,1)} %get-tuple-element.26), channel_id=1, source_target_pairs={{0,8},{8,0},{16,24},{24,16},{1,9},{9,1},{17,25},{25,17},{2,10},{10... | collective-permute-start | bytes 1327112 | tf_op jit(solution)/shard_map/ppermute | solution.py:541
  18.2 13.4 %collective-permute-start = (bf16[1,1,16,16,128]{4,3,2,1,0:T(8,128)(2,1)S(1)}, bf16[1,1,16,16,128]{4,3,2,1,0:T(8,128)(2,1)S(1)}, u32[]{:S(2)}, u32[]{:S(2)}) collective-permute-start(bf16[1,1,16,16,128]{4,3,2,1,0:T(8,128)(2,1)S(1)} %slice.3), channel_id=1, source_target_pairs={{0,1},{1,2},{2,3},{3,4},{4,5},{5,6},{6,7},{8,9},{9,10},{10,11},{11... | collective-permute-start | bytes 196616 | tf_op jit(solution)/shard_map/ppermute | solution.py:670
  22.1 1.2 %copy-start.7 = (bf16[1,16,16,16,128]{4,3,2,1,0:T(8,128)(2,1)S(1)}, bf16[1,16,16,16,128]{4,3,2,1,0:T(8,128)(2,1)}, u32[]{:S(2)}) copy-start(bf16[1,16,16,16,128]{4,3,2,1,0:T(8,128)(2,1)} %param.7) | copy-start | bytes 3145732
  23.3 2.6 %copy-start.9 = (f32[27,32,256]{2,1,0:T(8,128)S(1)}, f32[27,32,256]{2,1,0:T(8,128)}, u32[]{:S(2)}) copy-start(f32[27,32,256]{2,1,0:T(8,128)} %copy-done.8) | copy-start | bytes 2654212
  24.1 1.4 %copy-start.1 = (bf16[9,2,8,64,128]{4,3,2,1,0:T(8,128)(2,1)}, bf16[9,2,8,64,128]{4,3,2,1,0:T(8,128)(2,1)S(1)}, u32[]{:S(2)}) copy-start(bf16[9,2,8,64,128]{4,3,2,1,0:T(8,128)(2,1)S(1)} %get-tuple-element.37.window) | copy-start | bytes 7077892
  26.0 2.1 %copy-start.5 = (f32[1024,128]{1,0:T(8,128)}, f32[1024,128]{1,0:T(8,128)S(1)}, u32[]{:S(2)}) copy-start(f32[1024,128]{1,0:T(8,128)S(1)} %shard_map.68.own_ref) | copy-start | bytes 1572868
  28.1 8.6 %copy-start.6 = (f32[1024,128]{1,0:T(8,128)S(1)}, f32[1024,128]{1,0:T(8,128)}, u32[]{:S(2)}) copy-start(f32[1024,128]{1,0:T(8,128)} %copy-done.5) | copy-start | bytes 1572868
  30.2 1.4 %copy-start.3 = (bf16[9,2,8,64,128]{4,3,2,1,0:T(8,128)(2,1)}, bf16[9,2,8,64,128]{4,3,2,1,0:T(8,128)(2,1)S(1)}, u32[]{:S(2)}) copy-start(bf16[9,2,8,64,128]{4,3,2,1,0:T(8,128)(2,1)S(1)} %get-tuple-element.41.window) | copy-start | bytes 7077892
  34.8 1.9 %collective-permute-start.3 = (bf16[256,896]{1,0:T(8,128)(2,1)S(1)}, bf16[256,896]{1,0:T(8,128)(2,1)S(1)}, u32[]{:S(2)}, u32[]{:S(2)}) collective-permute-start(bf16[256,896]{1,0:T(8,128)(2,1)S(1)} %shard_map.72.weight_ref), channel_id=1, source_target_pairs={{0,8},{8,0},{16,24},{24,16},{1,9},{9,1},{17,25},{25,17},{2,10},{10... | collective-permute-start | bytes 1376264 | tf_op jit(solution)/shard_map/ppermute | solution.py:541
  36.7 14.8 %copy-start.2 = (bf16[9,2,8,64,128]{4,3,2,1,0:T(8,128)(2,1)S(1)}, bf16[9,2,8,64,128]{4,3,2,1,0:T(8,128)(2,1)}, u32[]{:S(2)}) copy-start(bf16[9,2,8,64,128]{4,3,2,1,0:T(8,128)(2,1)} %copy-done.1) | copy-start | bytes 7077892
  38.2 13.3 %all-to-all-start.1 = ((bf16[8,128,128]{2,1,0:T(8,128)(2,1)}), bf16[8,128,128]{2,1,0:T(8,128)(2,1)S(1)}, u32[]{:S(2)}, u32[]{:S(2)}) async-start(bf16[8,128,128]{2,1,0:T(8,128)(2,1)} %shard_map.74), calls=%async_computation.1 | async-start | bytes 524288 | tf_op jit(solution)/shard_map/all_to_all | solution.py:545
  42.3 16.4 %collective-permute-start.4 = (bf16[27,32,256]{2,1,0:T(8,128)(2,1)}, bf16[27,32,256]{2,1,0:T(8,128)(2,1)S(1)}, u32[]{:S(2)}, u32[]{:S(2)}) collective-permute-start(bf16[27,32,256]{2,1,0:T(8,128)(2,1)} %add_convert_fusion), channel_id=1, source_target_pairs={{0,16},{8,24},{16,0},{24,8},{1,17},{9,25},{17,1},{25,9},{2,18},{10... | collective-permute-start | bytes 1327112 | tf_op jit(solution)/shard_map/ppermute | solution.py:646
  43.8 1.3 %collective-permute-start.6 = (bf16[1,1,16,16,128]{4,3,2,1,0:T(8,128)(2,1)S(1)}, bf16[1,1,16,16,128]{4,3,2,1,0:T(8,128)(2,1)S(1)}, u32[]{:S(2)}, u32[]{:S(2)}) collective-permute-start(bf16[1,1,16,16,128]{4,3,2,1,0:T(8,128)(2,1)S(1)} %collective-permute-done), channel_id=1, source_target_pairs={{0,8},{8,0},{16,24},{24,16},{1,9},{9,1},{17,25},{25,17},{2,10},{10... | collective-permute-start | bytes 196616 | tf_op jit(solution)/shard_map/ppermute | solution.py:541
  51.5 1.7 %copy-start.4 = (bf16[9,2,8,64,128]{4,3,2,1,0:T(8,128)(2,1)S(1)}, bf16[9,2,8,64,128]{4,3,2,1,0:T(8,128)(2,1)}, u32[]{:S(2)}) copy-start(bf16[9,2,8,64,128]{4,3,2,1,0:T(8,128)(2,1)} %copy-done.3) | copy-start | bytes 7077892
  51.5 1.5 %collective-permute-start.7 = (bf16[8,128,128]{2,1,0:T(8,128)(2,1)S(1)}, bf16[8,128,128]{2,1,0:T(8,128)(2,1)S(1)}, u32[]{:S(2)}, u32[]{:S(2)}) collective-permute-start(bf16[8,128,128]{2,1,0:T(8,128)(2,1)S(1)} %all-to-all-done.1.got_ref), channel_id=1, source_target_pairs={{0,8},{8,0},{16,24},{24,16},{1,9},{9,1},{17,25},{25,17},{2,10},{10... | collective-permute-start | bytes 786440 | tf_op jit(solution)/shard_map/ppermute | solution.py:541
  54.9 3.7 %copy-start.11 = (bf16[27,32,256]{2,1,0:T(8,128)(2,1)S(1)}, bf16[27,32,256]{2,1,0:T(8,128)(2,1)}, u32[]{:S(2)}) copy-start(bf16[27,32,256]{2,1,0:T(8,128)(2,1)} %add_convert_fusion) | copy-start | bytes 1327108
  54.9 26.3 %all-to-all-start.2 = ((bf16[8,432,128]{2,1,0:T(8,128)(2,1)}), bf16[8,432,128]{2,1,0:T(8,128)(2,1)S(1)}, u32[]{:S(2)}, u32[]{:S(2)}) async-start(bf16[8,432,128]{2,1,0:T(8,128)(2,1)} %shard_map.76), calls=%async_computation.2 | async-start | bytes 1769472 | tf_op jit(solution)/shard_map/all_to_all | solution.py:545
  58.8 2.6 %collective-permute-start.5 = (f32[27,32,256]{2,1,0:T(8,128)S(1)}, f32[27,32,256]{2,1,0:T(8,128)}, u32[]{:S(2)}, u32[]{:S(2)}) collective-permute-start(f32[27,32,256]{2,1,0:T(8,128)S(1)} %add_multiply_fusion), channel_id=1, source_target_pairs={{0,8},{8,0},{16,24},{24,16},{1,9},{9,1},{17,25},{25,17},{2,10},{10... | collective-permute-start | bytes 2654216 | tf_op jit(solution)/shard_map/ppermute | solution.py:541
